TPU v7x, 768 devices: a whole 4x8x12 slice. The times are simulated.
768 devices in a mesh: blk: 12 (over x, z_hi), col: 64 (over z_lo, y, core).
Axes of the slice: x: 4, y: 8, z: 12 (z_hi: 3, z_lo: 4; z = z_hi * 4 + z_lo), core: 2. Of those that a mesh axis runs over, the one named last changes fastest.
Arguments:
- vectors: float32 [49152, 64], P(('blk', 'col')), may hold values from -6 to 6
- blocks: bfloat16 [12, 64, 4, 2, 256, 256], P('blk', 'col'), may hold values from -0.046875 to 0.046875
- row_blocks: int32 [12, 64, 4, 2], P('blk', 'col'), may hold values from 0 to 15, as said below
- col_blocks: int32 [12, 64, 4, 2], P('blk', 'col'), may hold values from 0 to 15, as said below
Outputs:
- product: float32 [49152, 64], P(('blk', 'col'))
Inputs may be any that keep to these rules, and one draw needn't show every extreme that they name: Within one shard and distance no pair of row_blocks and col_blocks occurs twice; at distance 0 the row block is at most the column block. `col_blocks`: drawn together with row_blocks, as stated there.
All inputs are finite; a program needn't handle non-finite values.
Results may differ from a plain program's by a relative error of at most 0.0029.
Values may be sent and summed in bfloat16 or wider, within the bound.
No kernel may reach another device: no remote copies, remote signals or barrier semaphores. Data moves between devices by JAX's collectives and lax.ppermute only.
A program may use at most 32 MiB of HBM per device.

v0:
```python
import jax
import jax.numpy as jnp
from jax import lax
from jax.sharding import PartitionSpec as P


def passed_along(block, axis, distance):
    devices = range(lax.axis_size(axis))
    route = [((i - distance) % len(devices), i) for i in devices]
    return lax.ppermute(block, axis, route)


def place_rows(indices, values, count):
    table = (indices[:, None] == jnp.arange(count, dtype=jnp.int32)[None, :]).astype(jnp.float32)
    return jnp.einsum("kn,kiv->niv", table, values, precision=lax.Precision.HIGHEST)


def per_device(vectors, blocks, row_blocks, col_blocks):
    width = vectors.shape[1]
    size = blocks.shape[-1]
    stored = blocks[0, 0]
    rows_at = row_blocks[0, 0]
    cols_at = col_blocks[0, 0]
    steps = stored.shape[0]
    gathered = lax.all_gather(vectors.astype(jnp.bfloat16), "col", axis=0, tiled=True)
    count = gathered.shape[0] // size
    shard = gathered.reshape(count, size, width)

    def products(step, arriving):
        block_set = stored[step]
        right = arriving[cols_at[step]]
        left = shard[rows_at[step]]
        direct = jnp.einsum("kij,kjv->kiv", block_set, right, preferred_element_type=jnp.float32)
        transposed = jnp.einsum("kji,kjv->kiv", block_set, left, preferred_element_type=jnp.float32)
        return (
            place_rows(rows_at[step], direct, count),
            place_rows(cols_at[step], transposed, count),
        )

    own_direct, own_transposed = products(0, shard)
    own_total = own_direct + own_transposed
    homed = None
    arriving = shard
    for step in range(1, steps):
        arriving = passed_along(arriving, "blk", 1)
        direct_part, transposed_part = products(step, arriving)
        own_total = own_total + direct_part
        summed = lax.psum_scatter(
            transposed_part.reshape(count * size, width), "col", scatter_dimension=0, tiled=True
        )
        returned = passed_along(summed, "blk", -step)
        homed = returned if homed is None else homed + returned
    mine = lax.psum_scatter(
        own_total.reshape(count * size, width), "col", scatter_dimension=0, tiled=True
    )
    mine = mine + homed
    return mine


def solution(mesh):
    return jax.shard_map(
        per_device,
        mesh=mesh,
        in_specs=(
            P(("blk", "col"), None),
            P("blk", "col", None, None, None, None),
            P("blk", "col", None, None),
            P("blk", "col", None, None),
        ),
        out_specs=P(("blk", "col"), None),
        check_vma=False,
    )
```

profile of v0, /device:TPU:1, one launch (start us, length us, event | category | flops | bytes accessed | tf_op | source)
XLA Modules:
  0.0 1294.8 jit_solution(11271396014292195077)
XLA Ops:
  6.5 1.0 slice_reduce_fusion.1
  7.6 0.8 convert_element_type.2
  8.4 86.8 %all_gather.3 = bf16[4096,64]{1,0:T(8,128)(2,1)S(1)} all-gather(bf16[64,64]{1,0:T(8,128)(2,1)S(1)} %convert_element_type.2), channel_id=1, replica_groups=mesh['blk'=12,'col'=64] {'col'}, dimensions={0}, use_global_device_ids=true | all-gather | bytes 532480 | tf_op jit(solution)/shard_map/all_gather | solution.py:25
  97.2 2.1 copy.57
  100.8 2.0 copy.59
  102.9 10.2 collective-permute-start
  114.6 2.0 copy.61
  119.0 64.0 %collective-permute-done = bf16[16,256,64]{1,2,0:T(8,128)(2,1)S(1)} collective-permute-done((bf16[16,256,64]{1,2,0:T(8,128)(2,1)S(1)}, bf16[16,256,64]{1,2,0:T(8,128)(2,1)S(1)}, u32[]{:S(2)}, u32[]{:S(2)}) %collective-permute-start) | collective-permute-done | bytes 524320 | tf_op jit(solution)/shard_map/ppermute | solution.py:10
  183.0 1.9 collective-permute-start.1
  186.5 34.1 %collective-permute-done.1 = bf16[16,256,64]{1,2,0:T(8,128)(2,1)} collective-permute-done((bf16[16,256,64]{1,2,0:T(8,128)(2,1)S(1)}, bf16[16,256,64]{1,2,0:T(8,128)(2,1)}, u32[]{:S(2)}, u32[]{:S(2)}) %collective-permute-start.1) | collective-permute-done | bytes 524320 | tf_op jit(solution)/shard_map/ppermute | solution.py:10
  220.6 3.0 collective-permute-start.2
  224.3 1.6 gather_fusion.3
  226.9 19.1 %collective-permute-done.2 = bf16[16,256,64]{1,2,0:T(8,128)(2,1)} collective-permute-done((bf16[16,256,64]{1,2,0:T(8,128)(2,1)}, bf16[16,256,64]{1,2,0:T(8,128)(2,1)}, u32[]{:S(2)}, u32[]{:S(2)}) %collective-permute-start.2) | collective-permute-done | bytes 524320 | tf_op jit(solution)/shard_map/ppermute | solution.py:10
  246.0 1.6 gather_fusion.4
  248.5 2.1 copy.55
  250.6 189.3 %reduce-scatter.7.cloned.1.call-done = f32[64,64]{1,0:T(8,128)} async-done(((f32[4096,64]{1,0:T(8,128)}), f32[64,64]{1,0:T(8,128)}) %reduce-scatter.7.cloned.1.call-update) | async-done | bytes 16400 | tf_op jit(solution)/shard_map/reduce_scatter | solution.py:48
  439.9 8.8 collective-permute-start.3
  448.7 274.5 %reduce-scatter.9.cloned.1.call-done = f32[64,64]{1,0:T(8,128)} async-done(((f32[4096,64]{1,0:T(8,128)}), f32[64,64]{1,0:T(8,128)}) %reduce-scatter.9.cloned.1.call-update) | async-done | bytes 16400 | tf_op jit(solution)/shard_map/reduce_scatter | solution.py:48
  723.3 8.1 collective-permute-start.4
  731.4 273.4 %reduce-scatter.11.cloned.1.call-done = f32[64,64]{1,0:T(8,128)} async-done(((f32[4096,64]{1,0:T(8,128)}), f32[64,64]{1,0:T(8,128)}) %reduce-scatter.11.cloned.1.call-update) | async-done | bytes 16400 | tf_op jit(solution)/shard_map/reduce_scatter | solution.py:48
  1004.8 3.0 collective-permute-start.5
  1007.8 1.8 collective-permute-done.5
  1009.6 277.2 %reduce-scatter.5.cloned.1.call-done = f32[64,64]{1,0:T(8,128)} async-done(((f32[4096,64]{1,0:T(8,128)}), f32[64,64]{1,0:T(8,128)}) %reduce-scatter.5.cloned.1.call-update) | async-done | bytes 16400 | tf_op jit(solution)/shard_map/reduce_scatter | solution.py:53
  1286.9 1.4 add_add_fusion
  (52 shorter events, 11.5 us)
Async XLA Ops:
  6.5 88.9 %copy-start.1 = (s32[1,1,4,2]{2,3,1,0:T(2,128)S(1)}, s32[1,1,4,2]{2,3,1,0:T(2,128)}, u32[]{:S(2)}) copy-start(s32[1,1,4,2]{2,3,1,0:T(2,128)} %param.7) | copy-start | bytes 100
  6.5 89.8 %copy-start = (bf16[1,1,4,2,256,256]{5,4,3,2,1,0:T(8,128)(2,1)S(1)}, bf16[1,1,4,2,256,256]{5,4,3,2,1,0:T(8,128)(2,1)}, u32[]{:S(2)}) copy-start(bf16[1,1,4,2,256,256]{5,4,3,2,1,0:T(8,128)(2,1)} %param.5) | copy-start | bytes 3145732
  6.5 433.4 %reduce-scatter.7.cloned.1.call-start = ((), (), s32[]{:S(2)}) async-start(), calls=%async_computation.5 | async-start | bytes 2129920 | tf_op jit(solution)/shard_map/reduce_scatter | solution.py:48
  99.3 624.0 %reduce-scatter.9.cloned.1.call-start = ((), (), s32[]{:S(2)}) async-start(), calls=%async_computation.6 | async-start | bytes 2129920 | tf_op jit(solution)/shard_map/reduce_scatter | solution.py:48
  102.9 901.9 %reduce-scatter.11.cloned.1.call-start = ((), (), s32[]{:S(2)}) async-start(), calls=%async_computation.7 | async-start | bytes 2129920 | tf_op jit(solution)/shard_map/reduce_scatter | solution.py:48
  102.9 80.1 %collective-permute-start = (bf16[16,256,64]{1,2,0:T(8,128)(2,1)S(1)}, bf16[16,256,64]{1,2,0:T(8,128)(2,1)S(1)}, u32[]{:S(2)}, u32[]{:S(2)}) collective-permute-start(bf16[16,256,64]{1,2,0:T(8,128)(2,1)S(1)} %copy.33), channel_id=1, source_target_pairs={{704,0},{0,64},{64,128},{128,192},{192,256},{256,320},{320,384},{3... | collective-permute-start | bytes 1572872 | tf_op jit(solution)/shard_map/ppermute | solution.py:10
  116.7 1170.2 %reduce-scatter.5.cloned.1.call-start = ((), (), s32[]{:S(2)}) async-start(), calls=%async_computation.4 | async-start | bytes 2129920 | tf_op jit(solution)/shard_map/reduce_scatter | solution.py:53
  183.0 37.6 %collective-permute-start.1 = (bf16[16,256,64]{1,2,0:T(8,128)(2,1)S(1)}, bf16[16,256,64]{1,2,0:T(8,128)(2,1)}, u32[]{:S(2)}, u32[]{:S(2)}) collective-permute-start(bf16[16,256,64]{1,2,0:T(8,128)(2,1)S(1)} %collective-permute-done), channel_id=1, source_target_pairs={{704,0},{0,64},{64,128},{128,192},{192,256},{256,320},{320,384},{3... | collective-permute-start | bytes 1572872 | tf_op jit(solution)/shard_map/ppermute | solution.py:10
  220.6 25.4 %collective-permute-start.2 = (bf16[16,256,64]{1,2,0:T(8,128)(2,1)}, bf16[16,256,64]{1,2,0:T(8,128)(2,1)}, u32[]{:S(2)}, u32[]{:S(2)}) collective-permute-start(bf16[16,256,64]{1,2,0:T(8,128)(2,1)} %collective-permute-done.1), channel_id=1, source_target_pairs={{704,0},{0,64},{64,128},{128,192},{192,256},{256,320},{320,384},{3... | collective-permute-start | bytes 1572872 | tf_op jit(solution)/shard_map/ppermute | solution.py:10
  439.9 567.9 %collective-permute-start.3 = (f32[64,64]{1,0:T(8,128)}, f32[64,64]{1,0:T(8,128)S(1)}, u32[]{:S(2)}, u32[]{:S(2)}) collective-permute-start(f32[64,64]{1,0:T(8,128)} %reduce-scatter.7.cloned.1.call-done), channel_id=1, source_target_pairs={{64,0},{128,64},{192,128},{256,192},{320,256},{384,320},{448,384},... | collective-permute-start | bytes 49160 | tf_op jit(solution)/shard_map/ppermute | solution.py:10
  723.3 284.5 %collective-permute-start.4 = (f32[64,64]{1,0:T(8,128)}, f32[64,64]{1,0:T(8,128)S(1)}, u32[]{:S(2)}, u32[]{:S(2)}) collective-permute-start(f32[64,64]{1,0:T(8,128)} %reduce-scatter.9.cloned.1.call-done), channel_id=1, source_target_pairs={{128,0},{192,64},{256,128},{320,192},{384,256},{448,320},{512,384}... | collective-permute-start | bytes 49160 | tf_op jit(solution)/shard_map/ppermute | solution.py:10
  1004.8 4.9 collective-permute-start.5
Sparse Core Ops, SparseCore 0:
  99.4 340.4 reduce-scatter.6
  443.3 279.9 reduce-scatter.8
  726.4 278.3 reduce-scatter.10
  1008.0 278.8 reduce-scatter.4
where the time goes:
time: 1300 us; the launch traced here: 1290 us
  waiting for transfers between devices  1130 us (87%)
  blocking collectives  86.8 us (7%)
  starting transfers between devices  35.2 us (3%)
  local copies, waits for them, and re-layouts  16.3 us (1%)
  between operations  13.5 us (1%)
    reduce_scatter x3, waiting for transfers between devices, per_device(): lax.psum_scatter(transposed_part.reshape(count * size, width), 'col', sca...  737 us
    reduce_scatter x1, waiting for transfers between devices, per_device(): lax.psum_scatter(own_total.reshape(count * size, width), 'col', scatter_d...  277 us
    ppermute x6, waiting for transfers between devices, passed_along(): return lax.ppermute(block, axis, route)  119 us
    all_gather x1, blocking collectives, per_device(): lax.all_gather(vectors.astype(jnp.bfloat16), 'col', axis=0, tiled=True)  86.8 us
    ppermute x6, starting transfers between devices, passed_along(): return lax.ppermute(block, axis, route)  35 us
  transfers between devices with their start and end apart: 10, of which 8 were waited for; matrix products, arithmetic and copies ran while one was open for 1% of the time, Pallas kernels for 0%

commit v1 on v0

v1 whole, which is shorter than its diff:
```python
import jax
import jax.numpy as jnp
from jax import lax
from jax.experimental import pallas as pl
from jax.experimental.pallas import tpu as pltpu
from jax.sharding import PartitionSpec as P

BF16 = jnp.bfloat16
F32 = jnp.float32
COL = 64
NBB = 16
NV = 64
BS = 256
STEPS = 4
SLOTS = 2
HALF = 128
CHUNK = 32
MIX = 16
REMOTE = (STEPS - 1) * SLOTS


def passed_along(block, axis, distance):
    n = lax.axis_size(axis)
    return lax.ppermute(block, axis, [((i - distance) % n, i) for i in range(n)])


def exchanged(flat, rows):
    pieces = lax.all_to_all(flat.reshape(COL, rows, HALF), "col", 0, 0, tiled=True)
    return pieces.reshape(COL * rows, HALF)


def dense_block(held, index):
    tops, bottoms = [], []
    for quarter in range(4):
        start = pl.multiple_of((index * 4 + quarter) * CHUNK, CHUNK)
        piece = held[pl.ds(start, CHUNK), :]
        tops.append(piece[:, :64])
        bottoms.append(piece[:, 64:])
    top = jnp.concatenate(tops, axis=1)
    bottom = jnp.concatenate(bottoms, axis=1)
    return jnp.concatenate([top, bottom], axis=0)


def times(left, block):
    return lax.dot_general(left, block, (((1,), (0,)), ((), ())), preferred_element_type=F32)


def times_transposed(left, block):
    return lax.dot_general(left, block, (((1,), (1,)), ((), ())), preferred_element_type=F32)


def every(row, stride=MIX, count=COL):
    return pl.ds(row, count, stride=stride)


def remote_products(rows_at, cols_at, held, blocks, h1, h2, h3, out, work):
    for step in range(1, STEPS):
        for k in range(SLOTS):
            slot = (step - 1) * SLOTS + k
            left = dense_block(held, rows_at[step, k])
            partial = times(left, blocks[step * SLOTS + k])
            work[every(2 * slot), :] = partial[:, :HALF]
            work[every(2 * slot + 1), :] = partial[:, HALF:]
    work[every(12), :] = jnp.concatenate([h1[...], h2[...]], axis=1).astype(F32)
    lane = lax.broadcasted_iota(jnp.int32, (COL, 64), 1)
    listed = jnp.zeros((COL, 64), jnp.int32)
    for step in range(STEPS):
        for k in range(SLOTS):
            at = step * SLOTS + k
            listed = jnp.where(lane == at, cols_at[step, k], listed)
    work[every(13), :] = jnp.concatenate([h3[...].astype(F32), listed.astype(F32)], axis=1)
    work[every(14), :] = jnp.zeros((COL, HALF), F32)
    work[every(15), :] = jnp.zeros((COL, HALF), F32)
    out[...] = work[...].astype(BF16)


def owners_turn(arrived, out, came, work):
    came[...] = arrived[...].astype(F32)
    asked = came[every(13), :]
    asked_t = jnp.transpose(asked)
    block_down = lax.broadcasted_iota(jnp.int32, (NBB, COL), 0).astype(F32)
    block_along = lax.broadcasted_iota(jnp.int32, (COL, NBB), 1).astype(F32)
    quarters_a = [came[pl.ds(12 + MIX * q, NBB, stride=4 * MIX), :] for q in range(4)]
    quarters_b = [came[pl.ds(13 + MIX * q, NBB, stride=4 * MIX), :] for q in range(4)]
    columns = [
        jnp.concatenate([q[:, :64] for q in quarters_a], axis=1),
        jnp.concatenate([q[:, 64:] for q in quarters_a], axis=1),
        jnp.concatenate([q[:, :64] for q in quarters_b], axis=1),
    ]
    sums = []
    for step in range(1, STEPS):
        total = None
        own = columns[step - 1].astype(BF16)
        for k in range(SLOTS):
            slot = (step - 1) * SLOTS + k
            lane = 64 + step * SLOTS + k
            partial = jnp.concatenate([came[every(2 * slot), :], came[every(2 * slot + 1), :]], axis=1)
            goes_to = (asked_t[lane : lane + 1, :] == block_down).astype(F32).astype(BF16)
            part = times(goes_to, partial.astype(BF16))
            total = part if total is None else total + part
            wants = (asked[:, lane : lane + 1] == block_along).astype(F32).astype(BF16)
            answer = times(wants, own)
            work[every(2 * slot), :] = answer[:, :HALF]
            work[every(2 * slot + 1), :] = answer[:, HALF:]
        sums.append(total)
    highs = [s.astype(BF16).astype(F32) for s in sums]
    lows = [s - h for s, h in zip(sums, highs)]
    for q in range(4):
        part = slice(64 * q, 64 * q + 64)
        for row, (s1, s2, s3) in ((12, highs), (14, lows)):
            work[pl.ds(row + MIX * q, NBB, stride=4 * MIX), :] = jnp.concatenate(
                [s1[:, part], s2[:, part]], axis=1
            )
            work[pl.ds(row + 1 + MIX * q, NBB, stride=4 * MIX), :] = jnp.concatenate(
                [s3[:, part], jnp.zeros((NBB, 64), F32)], axis=1
            )
    out[...] = work[...].astype(BF16)


def own_products(rows_at, cols_at, held, blocks, arrived, out, u1, u2, u3, came, total):
    came[...] = arrived[...].astype(F32)
    pair = came[every(12), :] + came[every(14), :]
    third = came[every(13), :] + came[every(15), :]
    u1[...] = pair[:, :64]
    u2[...] = pair[:, 64:]
    u3[...] = third[:, :64]
    total[...] = jnp.zeros_like(total)
    for k in range(SLOTS):
        row, col = rows_at[0, k], cols_at[0, k]
        total[row] += times_transposed(dense_block(held, col), blocks[k])
        total[col] += times(dense_block(held, row), blocks[k])
    for step in range(1, STEPS):
        for k in range(SLOTS):
            slot = (step - 1) * SLOTS + k
            right = jnp.concatenate([came[every(2 * slot), :], came[every(2 * slot + 1), :]], axis=1)
            total[rows_at[step, k]] += times_transposed(right.astype(BF16), blocks[step * SLOTS + k])
    for row in range(NBB):
        whole = total[row]
        for q in range(4):
            part = whole[:, 64 * q : 64 * q + 64]
            start = (row * 4 + q) * CHUNK
            out[start : start + CHUNK, :] = jnp.concatenate([part[:32], part[32:]], axis=1).astype(BF16)


def gathered_sum(arrived, r1, r2, r3, out):
    sums = [arrived[i * CHUNK : (i + 1) * CHUNK, :].astype(F32) for i in range(4)]
    for i in range(4, COL):
        sums[i % 4] += arrived[i * CHUNK : (i + 1) * CHUNK, :].astype(F32)
    packed = (sums[0] + sums[1]) + (sums[2] + sums[3])
    own = jnp.concatenate([packed[:, :64], packed[:, 64:]], axis=0)
    total = own + ((r1[...] + r2[...]) + r3[...])
    out[...] = jnp.transpose(jnp.concatenate([total, total], axis=1))[:64]


VM = pl.BlockSpec(memory_space=pltpu.VMEM)
SM = pl.BlockSpec(memory_space=pltpu.SMEM)
PARAMS = pltpu.CompilerParams(vmem_limit_bytes=24 * 1024 * 1024)


def shape_of(shape, dtype):
    return jax.ShapeDtypeStruct(shape, dtype)


def per_device(vectors, blocks, row_blocks, col_blocks):
    stored = blocks.reshape(STEPS * SLOTS, BS, BS)
    rows_at = row_blocks[0, 0]
    cols_at = col_blocks[0, 0]
    turned = vectors.T.astype(BF16)
    near = [passed_along(turned, "blk", step) for step in range(1, STEPS)]
    packed = jnp.concatenate([turned[:32], turned[32:]], axis=1)
    held = exchanged(jnp.broadcast_to(packed[None], (COL, CHUNK, HALF)), CHUNK)
    sent = pl.pallas_call(
        remote_products,
        out_shape=shape_of((COL * MIX, HALF), BF16),
        in_specs=[SM, SM, VM, VM, VM, VM, VM],
        out_specs=VM,
        scratch_shapes=[pltpu.VMEM((COL * MIX, HALF), F32)],
        compiler_params=PARAMS,
    )(rows_at, cols_at, held, stored, *near)
    arrived = exchanged(sent, MIX)
    answers = pl.pallas_call(
        owners_turn,
        out_shape=shape_of((COL * MIX, HALF), BF16),
        in_specs=[VM],
        out_specs=VM,
        scratch_shapes=[pltpu.VMEM((COL * MIX, HALF), F32), pltpu.VMEM((COL * MIX, HALF), F32)],
        compiler_params=PARAMS,
    )(arrived)
    answered = exchanged(answers, MIX)
    piece = shape_of((NV, 64), F32)
    partials, u1, u2, u3 = pl.pallas_call(
        own_products,
        out_shape=(shape_of((COL * CHUNK, HALF), BF16), piece, piece, piece),
        in_specs=[SM, SM, VM, VM, VM],
        out_specs=(VM, VM, VM, VM),
        scratch_shapes=[pltpu.VMEM((COL * MIX, HALF), F32), pltpu.VMEM((NBB, NV, BS), F32)],
        compiler_params=PARAMS,
    )(rows_at, cols_at, held, stored, answered)
    home = [passed_along(u, "blk", -step) for step, u in ((1, u1), (2, u2), (3, u3))]
    collected = exchanged(partials, CHUNK)
    return pl.pallas_call(
        gathered_sum,
        out_shape=shape_of((64, NV), F32),
        in_specs=[VM, VM, VM, VM],
        out_specs=VM,
        compiler_params=PARAMS,
    )(collected, *home)


def solution(mesh):
    return jax.shard_map(
        per_device,
        mesh=mesh,
        in_specs=(
            P(("blk", "col"), None),
            P("blk", "col", None, None, None, None),
            P("blk", "col", None, None),
            P("blk", "col", None, None),
        ),
        out_specs=P(("blk", "col"), None),
        check_vma=False,
    )
```

time: 1300 us -> 110 us (0.08)
  waiting for transfers between devices: 1130 us -> 11.2 us
  blocking collectives: 86.8 us -> 41.1 us
  starting transfers between devices: 35.2 us -> 49.9 us
  local copies, waits for them, and re-layouts: 16.3 us -> 2.68 us
  between operations: 13.5 us -> 0.13 us
    reduce_scatter x4 -> x0, waiting for transfers between devices: 1010 us -> none  [the longest x3 737 us: per_device(): lax.psum_scatter(transposed_part.reshape(count * size, width), 'col', sca...]
    ppermute x6, waiting for transfers between devices: 119 us -> 7.09 us  [passed_along(): lax.ppermute(block, axis, [((i - distance) % n, i) for i in range(n)])]
    all_gather x1 -> x0, blocking collectives: 86.8 us -> none  [per_device(): lax.all_gather(vectors.astype(jnp.bfloat16), 'col', axis=0, tiled=True)]
    all_to_all x0 -> x2, blocking collectives: none -> 41.1 us  [exchanged(): lax.all_to_all(flat.reshape(COL, rows, HALF), 'col', 0, 0, tiled=True)]
    all_to_all x0 -> x2, starting transfers between devices: none -> 20.6 us  [exchanged(): lax.all_to_all(flat.reshape(COL, rows, HALF), 'col', 0, 0, tiled=True)]
  transfers between devices with their start and end apart: 10 -> 8, of which waited for: 8 -> 4; matrix products, arithmetic and copies ran while one was open for 1% -> 0% of each run, Pallas kernels for 0% -> 0%
where the time goes in v1:
time: 110 us
  starting transfers between devices  49.9 us (45%)
  blocking collectives  41.1 us (37%)
  waiting for transfers between devices  11.2 us (10%)
  Pallas kernels  4.57 us (4%)
  local copies, waits for them, and re-layouts  2.68 us (2%)
    all_to_all x2, blocking collectives, exchanged(): lax.all_to_all(flat.reshape(COL, rows, HALF), 'col', 0, 0, tiled=True)  41.1 us
    ppermute x6, starting transfers between devices, passed_along(): lax.ppermute(block, axis, [((i - distance) % n, i) for i in range(n)])  29.3 us
    all_to_all x2, starting transfers between devices, exchanged(): lax.all_to_all(flat.reshape(COL, rows, HALF), 'col', 0, 0, tiled=True)  20.6 us
    ppermute x6, waiting for transfers between devices, passed_along(): lax.ppermute(block, axis, [((i - distance) % n, i) for i in range(n)])  7.09 us
    all_to_all x2, waiting for transfers between devices, exchanged(): lax.all_to_all(flat.reshape(COL, rows, HALF), 'col', 0, 0, tiled=True)  4.1 us
  transfers between devices with their start and end apart: 8, of which 4 were waited for; matrix products, arithmetic and copies ran while one was open for 0% of the time, Pallas kernels for 0%

profile of v1, /device:TPU:1, one launch (start us, length us, event | category | flops | bytes accessed | tf_op | source)
XLA Modules:
  0.0 109.6 jit_solution(18061962528541128410)
XLA Ops:
  0.0 0.9 copy.5
  0.9 0.1 pad_maximum_fusion
  1.0 0.9 broadcast_in_dim.2
  1.9 14.6 %all-to-all-start = ((bf16[64,32,128]{2,1,0:T(8,128)(2,1)}), bf16[64,32,128]{2,1,0:T(8,128)(2,1)S(1)}, u32[]{:S(2)}, u32[]{:S(2)}) async-start(bf16[64,32,128]{2,1,0:T(8,128)(2,1)} %broadcast_in_dim.2), calls=%async_computation | async-start | bytes 1048576 | tf_op jit(solution)/shard_map/all_to_all | solution.py:28
  16.5 11.6 %collective-permute-start.1 = (bf16[64,64]{1,0:T(8,128)(2,1)S(1)}, bf16[64,64]{1,0:T(8,128)(2,1)S(1)}, u32[]{:S(2)}, u32[]{:S(2)}) collective-permute-start(bf16[64,64]{1,0:T(8,128)(2,1)S(1)} %bitcast.23), channel_id=1, source_target_pairs={{640,0},{704,64},{0,128},{64,192},{128,256},{192,320},{256,384},{3... | collective-permute-start | bytes 24584 | tf_op jit(solution)/shard_map/ppermute | solution.py:24
  28.1 1.9 %collective-permute-start = (bf16[64,64]{1,0:T(8,128)(2,1)S(1)}, bf16[64,64]{1,0:T(8,128)(2,1)S(1)}, u32[]{:S(2)}, u32[]{:S(2)}) collective-permute-start(bf16[64,64]{1,0:T(8,128)(2,1)S(1)} %bitcast.24), channel_id=1, source_target_pairs={{704,0},{0,64},{64,128},{128,192},{192,256},{256,320},{320,384},{3... | collective-permute-start | bytes 24584 | tf_op jit(solution)/shard_map/ppermute | solution.py:24
  30.0 3.1 %collective-permute-start.2 = (bf16[64,64]{1,0:T(8,128)(2,1)S(1)}, bf16[64,64]{1,0:T(8,128)(2,1)S(1)}, u32[]{:S(2)}, u32[]{:S(2)}) collective-permute-start(bf16[64,64]{1,0:T(8,128)(2,1)S(1)} %bitcast.25), channel_id=1, source_target_pairs={{576,0},{640,64},{704,128},{0,192},{64,256},{128,320},{192,384},{2... | collective-permute-start | bytes 24584 | tf_op jit(solution)/shard_map/ppermute | solution.py:24
  33.2 0.1 copy.8.rows_at
  33.2 0.7 copy-done.2
  33.9 0.1 copy.9.cols_at
  34.0 4.7 %collective-permute-done.h1 = bf16[64,64]{1,0:T(8,128)(2,1)S(1)} collective-permute-done((bf16[64,64]{1,0:T(8,128)(2,1)S(1)}, bf16[64,64]{1,0:T(8,128)(2,1)S(1)}, u32[]{:S(2)}, u32[]{:S(2)}) %collective-permute-start) | collective-permute-done | bytes 8224 | tf_op jit(solution)/shard_map/ppermute | solution.py:24
  38.7 1.0 shard_map.46
  39.7 23.6 %all_to_all.20 = bf16[64,16,128]{2,1,0:T(8,128)(2,1)S(1)} all-to-all(bf16[64,16,128]{2,1,0:T(8,128)(2,1)S(1)} %bitcast.19), channel_id=1, replica_groups=mesh['blk'=12,'col'=64] {'col'}, dimensions={0} | all-to-all | bytes 524288 | tf_op jit(solution)/shard_map/all_to_all | solution.py:28
  63.3 0.6 shard_map.47
  63.9 17.4 %all_to_all.21 = bf16[64,16,128]{2,1,0:T(8,128)(2,1)S(1)} all-to-all(bf16[64,16,128]{2,1,0:T(8,128)(2,1)S(1)} %bitcast.21), channel_id=1, replica_groups=mesh['blk'=12,'col'=64] {'col'}, dimensions={0} | all-to-all | bytes 524288 | tf_op jit(solution)/shard_map/all_to_all | solution.py:28
  81.3 2.2 %shard_map.48 = (bf16[2048,128]{1,0:T(8,128)(2,1)}, f32[64,64]{1,0:T(8,128)S(1)}, f32[64,64]{1,0:T(8,128)S(1)}, f32[64,64]{1,0:T(8,128)S(1)}) custom-call(s32[4,2]{1,0:T(4,128)S(1)} %copy.8.rows_at, s32[4,2]{1,0:T(4,128)S(1)} %copy.9.cols_at, bf16[2048,128]{1,0:T(8,128)(2,1)S(1)} %bitcast.14, bf16[8,256,256]{2,1,0:T(8,128)(2,1)S(1)} %bitcast.16, ...), custom_call_target="tpu_custom_call" | custom-call | tf_op jit(solution)/shard_map/pallas_call | solution.py:191
  83.5 6.0 %all-to-all-start.3 = ((bf16[64,32,128]{2,1,0:T(8,128)(2,1)}), bf16[64,32,128]{2,1,0:T(8,128)(2,1)S(1)}, u32[]{:S(2)}, u32[]{:S(2)}) async-start(bf16[64,32,128]{2,1,0:T(8,128)(2,1)} %bitcast.9), calls=%async_computation.3 | async-start | bytes 1048576 | tf_op jit(solution)/shard_map/all_to_all | solution.py:28
  89.5 5.4 %collective-permute-start.3 = (f32[64,64]{1,0:T(8,128)S(1)}, f32[64,64]{1,0:T(8,128)S(1)}, u32[]{:S(2)}, u32[]{:S(2)}) collective-permute-start(f32[64,64]{1,0:T(8,128)S(1)} %get-tuple-element.10), channel_id=1, source_target_pairs={{64,0},{128,64},{192,128},{256,192},{320,256},{384,320},{448,384},... | collective-permute-start | bytes 49160 | tf_op jit(solution)/shard_map/ppermute | solution.py:24
  94.9 4.8 %collective-permute-start.4 = (f32[64,64]{1,0:T(8,128)S(1)}, f32[64,64]{1,0:T(8,128)S(1)}, u32[]{:S(2)}, u32[]{:S(2)}) collective-permute-start(f32[64,64]{1,0:T(8,128)S(1)} %get-tuple-element.11), channel_id=1, source_target_pairs={{128,0},{192,64},{256,128},{320,192},{384,256},{448,320},{512,384}... | collective-permute-start | bytes 49160 | tf_op jit(solution)/shard_map/ppermute | solution.py:24
  99.7 2.5 %collective-permute-start.5 = (f32[64,64]{1,0:T(8,128)S(1)}, f32[64,64]{1,0:T(8,128)S(1)}, u32[]{:S(2)}, u32[]{:S(2)}) collective-permute-start(f32[64,64]{1,0:T(8,128)S(1)} %get-tuple-element.12), channel_id=1, source_target_pairs={{192,0},{256,64},{320,128},{384,192},{448,256},{512,320},{576,384}... | collective-permute-start | bytes 49160 | tf_op jit(solution)/shard_map/ppermute | solution.py:24
  102.2 1.4 %collective-permute-done.4.r2 = f32[64,64]{1,0:T(8,128)S(1)} collective-permute-done((f32[64,64]{1,0:T(8,128)S(1)}, f32[64,64]{1,0:T(8,128)S(1)}, u32[]{:S(2)}, u32[]{:S(2)}) %collective-permute-start.4) | collective-permute-done | bytes 16416 | tf_op jit(solution)/shard_map/ppermute | solution.py:24
  103.6 1.0 collective-permute-done.5.r3
  104.6 4.1 %all-to-all-done.3 = bf16[64,32,128]{2,1,0:T(8,128)(2,1)S(1)} async-done(((bf16[64,32,128]{2,1,0:T(8,128)(2,1)}), bf16[64,32,128]{2,1,0:T(8,128)(2,1)S(1)}, u32[]{:S(2)}, u32[]{:S(2)}) %all-to-all-start.3) | async-done | bytes 524320 | tf_op jit(solution)/shard_map/all_to_all | solution.py:28
  108.7 0.9 shard_map.49
  (10 shorter events, 0.0 us)
Async XLA Ops:
  0.0 38.7 %copy-start = (bf16[1,1,4,2,256,256]{5,4,3,2,1,0:T(8,128)(2,1)S(1)}, bf16[1,1,4,2,256,256]{5,4,3,2,1,0:T(8,128)(2,1)}, u32[]{:S(2)}) copy-start(bf16[1,1,4,2,256,256]{5,4,3,2,1,0:T(8,128)(2,1)} %param.5) | copy-start | bytes 3145732
  1.9 36.8 %all-to-all-start = ((bf16[64,32,128]{2,1,0:T(8,128)(2,1)}), bf16[64,32,128]{2,1,0:T(8,128)(2,1)S(1)}, u32[]{:S(2)}, u32[]{:S(2)}) async-start(bf16[64,32,128]{2,1,0:T(8,128)(2,1)} %broadcast_in_dim.2), calls=%async_computation | async-start | bytes 1048576 | tf_op jit(solution)/shard_map/all_to_all | solution.py:28
  16.5 16.7 %copy-start.1 = (s32[1,1,4,2]{2,3,1,0:T(2,128)S(1)}, s32[1,1,4,2]{2,3,1,0:T(2,128)}, u32[]{:S(2)}) copy-start(s32[1,1,4,2]{2,3,1,0:T(2,128)} %param.6) | copy-start | bytes 100
  16.5 17.5 %collective-permute-start.1 = (bf16[64,64]{1,0:T(8,128)(2,1)S(1)}, bf16[64,64]{1,0:T(8,128)(2,1)S(1)}, u32[]{:S(2)}, u32[]{:S(2)}) collective-permute-start(bf16[64,64]{1,0:T(8,128)(2,1)S(1)} %bitcast.23), channel_id=1, source_target_pairs={{640,0},{704,64},{0,128},{64,192},{128,256},{192,320},{256,384},{3... | collective-permute-start | bytes 24584 | tf_op jit(solution)/shard_map/ppermute | solution.py:24
  28.1 10.6 %collective-permute-start = (bf16[64,64]{1,0:T(8,128)(2,1)S(1)}, bf16[64,64]{1,0:T(8,128)(2,1)S(1)}, u32[]{:S(2)}, u32[]{:S(2)}) collective-permute-start(bf16[64,64]{1,0:T(8,128)(2,1)S(1)} %bitcast.24), channel_id=1, source_target_pairs={{704,0},{0,64},{64,128},{128,192},{192,256},{256,320},{320,384},{3... | collective-permute-start | bytes 24584 | tf_op jit(solution)/shard_map/ppermute | solution.py:24
  30.0 8.7 %collective-permute-start.2 = (bf16[64,64]{1,0:T(8,128)(2,1)S(1)}, bf16[64,64]{1,0:T(8,128)(2,1)S(1)}, u32[]{:S(2)}, u32[]{:S(2)}) collective-permute-start(bf16[64,64]{1,0:T(8,128)(2,1)S(1)} %bitcast.25), channel_id=1, source_target_pairs={{576,0},{640,64},{704,128},{0,192},{64,256},{128,320},{192,384},{2... | collective-permute-start | bytes 24584 | tf_op jit(solution)/shard_map/ppermute | solution.py:24
  33.2 0.7 copy-start.2
  83.5 25.3 %all-to-all-start.3 = ((bf16[64,32,128]{2,1,0:T(8,128)(2,1)}), bf16[64,32,128]{2,1,0:T(8,128)(2,1)S(1)}, u32[]{:S(2)}, u32[]{:S(2)}) async-start(bf16[64,32,128]{2,1,0:T(8,128)(2,1)} %bitcast.9), calls=%async_computation.3 | async-start | bytes 1048576 | tf_op jit(solution)/shard_map/all_to_all | solution.py:28
  89.5 12.7 %collective-permute-start.3 = (f32[64,64]{1,0:T(8,128)S(1)}, f32[64,64]{1,0:T(8,128)S(1)}, u32[]{:S(2)}, u32[]{:S(2)}) collective-permute-start(f32[64,64]{1,0:T(8,128)S(1)} %get-tuple-element.10), channel_id=1, source_target_pairs={{64,0},{128,64},{192,128},{256,192},{320,256},{384,320},{448,384},... | collective-permute-start | bytes 49160 | tf_op jit(solution)/shard_map/ppermute | solution.py:24
  94.9 8.7 %collective-permute-start.4 = (f32[64,64]{1,0:T(8,128)S(1)}, f32[64,64]{1,0:T(8,128)S(1)}, u32[]{:S(2)}, u32[]{:S(2)}) collective-permute-start(f32[64,64]{1,0:T(8,128)S(1)} %get-tuple-element.11), channel_id=1, source_target_pairs={{128,0},{192,64},{256,128},{320,192},{384,256},{448,320},{512,384}... | collective-permute-start | bytes 49160 | tf_op jit(solution)/shard_map/ppermute | solution.py:24
  99.7 5.0 %collective-permute-start.5 = (f32[64,64]{1,0:T(8,128)S(1)}, f32[64,64]{1,0:T(8,128)S(1)}, u32[]{:S(2)}, u32[]{:S(2)}) collective-permute-start(f32[64,64]{1,0:T(8,128)S(1)} %get-tuple-element.12), channel_id=1, source_target_pairs={{192,0},{256,64},{320,128},{384,192},{448,256},{512,320},{576,384}... | collective-permute-start | bytes 49160 | tf_op jit(solution)/shard_map/ppermute | solution.py:24

commit v2 on v0

v2 whole, which is shorter than its diff:
```python
import jax
import jax.numpy as jnp
from jax import lax
from jax.experimental import pallas as pl
from jax.experimental.pallas import tpu as pltpu
from jax.sharding import PartitionSpec as P

BF16 = jnp.bfloat16
F32 = jnp.float32
COL = 64
NBB = 16
NV = 64
BS = 256
STEPS = 4
SLOTS = 2
HALF = 128
CHUNK = 32


def passed_along(block, axis, distance):
    n = lax.axis_size(axis)
    return lax.ppermute(block, axis, [((i - distance) % n, i) for i in range(n)])


def exchanged(flat, rows):
    pieces = lax.all_to_all(flat.reshape(COL, rows, HALF), "col", 0, 0, tiled=True)
    return pieces.reshape(COL * rows, HALF)


def dense_block(held, index):
    tops, bottoms = [], []
    for quarter in range(4):
        start = pl.multiple_of((index * 4 + quarter) * CHUNK, CHUNK)
        piece = held[pl.ds(start, CHUNK), :]
        tops.append(piece[:, :64])
        bottoms.append(piece[:, 64:])
    top = jnp.concatenate(tops, axis=1)
    bottom = jnp.concatenate(bottoms, axis=1)
    return jnp.concatenate([top, bottom], axis=0)


def times(left, block):
    return lax.dot_general(left, block, (((1,), (0,)), ((), ())), preferred_element_type=F32)


def times_transposed(left, block):
    return lax.dot_general(left, block, (((1,), (1,)), ((), ())), preferred_element_type=F32)


def neighbours_blocks(rows_at, cols_at, far1, far2, far3, held, blocks, *outs):
    picked, partials = outs[:3], outs[3:]
    for step, far in ((1, far1), (2, far2), (3, far3)):
        for k in range(SLOTS):
            picked[step - 1][NV * k : NV * (k + 1), :] = dense_block(held, far[step, k])
    for step in range(1, STEPS):
        for k in range(SLOTS):
            left = dense_block(held, rows_at[step, k])
            partial = times(left, blocks[step * SLOTS + k])
            partials[step - 1][NV * k : NV * (k + 1), :] = partial.astype(BF16)


def own_products(rows_at, cols_at, far1, far2, far3, held, blocks, g1, g2, g3, p1, p2, p3, out, total):
    total[...] = jnp.zeros_like(total)
    for k in range(SLOTS):
        row, col = rows_at[0, k], cols_at[0, k]
        total[row] += times_transposed(dense_block(held, col), blocks[k])
        total[col] += times(dense_block(held, row), blocks[k])
    for step, right, back, far in ((1, g1, p1, far1), (2, g2, p2, far2), (3, g3, p3, far3)):
        for k in range(SLOTS):
            part = slice(NV * k, NV * (k + 1))
            total[rows_at[step, k]] += times_transposed(right[part, :], blocks[step * SLOTS + k])
            total[far[step, k]] += back[part, :].astype(F32)
    for row in range(NBB):
        whole = total[row]
        for q in range(4):
            part = whole[:, 64 * q : 64 * q + 64]
            start = (row * 4 + q) * CHUNK
            out[start : start + CHUNK, :] = jnp.concatenate([part[:32], part[32:]], axis=1).astype(BF16)


def gathered_sum(arrived, out):
    sums = [arrived[i * CHUNK : (i + 1) * CHUNK, :].astype(F32) for i in range(4)]
    for i in range(4, COL):
        sums[i % 4] += arrived[i * CHUNK : (i + 1) * CHUNK, :].astype(F32)
    packed = (sums[0] + sums[1]) + (sums[2] + sums[3])
    own = jnp.concatenate([packed[:, :64], packed[:, 64:]], axis=0)
    out[...] = jnp.transpose(jnp.concatenate([own, own], axis=1))[:64]


VM = pl.BlockSpec(memory_space=pltpu.VMEM)
SM = pl.BlockSpec(memory_space=pltpu.SMEM)
PARAMS = pltpu.CompilerParams(vmem_limit_bytes=24 * 1024 * 1024)


def shape_of(shape, dtype):
    return jax.ShapeDtypeStruct(shape, dtype)


def per_device(vectors, blocks, row_blocks, col_blocks):
    stored = blocks.reshape(STEPS * SLOTS, BS, BS)
    rows_at = row_blocks[0, 0]
    cols_at = col_blocks[0, 0]
    turned = vectors.T.astype(BF16)
    far = [passed_along(cols_at, "blk", -step) for step in range(1, STEPS)]
    packed = jnp.concatenate([turned[:32], turned[32:]], axis=1)
    held = exchanged(jnp.broadcast_to(packed[None], (COL, CHUNK, HALF)), CHUNK)
    pair = shape_of((SLOTS * NV, BS), BF16)
    sent = pl.pallas_call(
        neighbours_blocks,
        out_shape=(pair,) * 6,
        in_specs=[SM] * 5 + [VM] * 2,
        out_specs=(VM,) * 6,
        compiler_params=PARAMS,
    )(rows_at, cols_at, *far, held, stored)
    right = [passed_along(sent[step - 1], "blk", step) for step in range(1, STEPS)]
    back = [passed_along(sent[step + 2], "blk", -step) for step in range(1, STEPS)]
    sums = pl.pallas_call(
        own_products,
        out_shape=shape_of((COL * CHUNK, HALF), BF16),
        in_specs=[SM] * 5 + [VM] * 8,
        out_specs=VM,
        scratch_shapes=[pltpu.VMEM((NBB, NV, BS), F32)],
        compiler_params=PARAMS,
    )(rows_at, cols_at, *far, held, stored, *right, *back)
    return pl.pallas_call(
        gathered_sum,
        out_shape=shape_of((64, NV), F32),
        in_specs=[VM],
        out_specs=VM,
        compiler_params=PARAMS,
    )(exchanged(sums, CHUNK))


def solution(mesh):
    return jax.shard_map(
        per_device,
        mesh=mesh,
        in_specs=(
            P(("blk", "col"), None),
            P("blk", "col", None, None, None, None),
            P("blk", "col", None, None),
            P("blk", "col", None, None),
        ),
        out_specs=P(("blk", "col"), None),
        check_vma=False,
    )
```

time: 1300 us -> 105 us (0.08)
  waiting for transfers between devices: 1130 us -> 7.8 us
  blocking collectives: 86.8 us -> 31.6 us
  starting transfers between devices: 35.2 us -> 58.6 us
  local copies, waits for them, and re-layouts: 16.3 us -> 2.67 us
  between operations: 13.5 us -> 0.15 us
    reduce_scatter x4 -> x0, waiting for transfers between devices: 1010 us -> none  [the longest x3 737 us: per_device(): lax.psum_scatter(transposed_part.reshape(count * size, width), 'col', sca...]
    ppermute x6 -> x9, waiting for transfers between devices: 119 us -> 7.79 us  [passed_along(): lax.ppermute(block, axis, [((i - distance) % n, i) for i in range(n)])]
    all_gather x1 -> x0, blocking collectives: 86.8 us -> none  [per_device(): lax.all_gather(vectors.astype(jnp.bfloat16), 'col', axis=0, tiled=True)]
    all_to_all x0 -> x1, blocking collectives: none -> 31.6 us  [exchanged(): lax.all_to_all(flat.reshape(COL, rows, HALF), 'col', 0, 0, tiled=True)]
    all_to_all x0 -> x1, starting transfers between devices: none -> 14.6 us  [exchanged(): lax.all_to_all(flat.reshape(COL, rows, HALF), 'col', 0, 0, tiled=True)]
    ppermute x6 -> x9, starting transfers between devices: 35 us -> 44 us  [passed_along(): lax.ppermute(block, axis, [((i - distance) % n, i) for i in range(n)])]
  transfers between devices with their start and end apart: 10 -> 10, of which waited for: 8 -> 4; matrix products, arithmetic and copies ran while one was open for 1% -> 0% of each run, Pallas kernels for 0% -> 0%
where the time goes in v2:
time: 105 us; the launch traced here: 104 us
  starting transfers between devices  58.6 us (56%)
  blocking collectives  31.6 us (30%)
  waiting for transfers between devices  7.8 us (7%)
  Pallas kernels  3.31 us (3%)
  local copies, waits for them, and re-layouts  2.67 us (3%)
    ppermute x9, starting transfers between devices, passed_along(): lax.ppermute(block, axis, [((i - distance) % n, i) for i in range(n)])  44 us
    all_to_all x1, blocking collectives, exchanged(): lax.all_to_all(flat.reshape(COL, rows, HALF), 'col', 0, 0, tiled=True)  31.6 us
    all_to_all x1, starting transfers between devices, exchanged(): lax.all_to_all(flat.reshape(COL, rows, HALF), 'col', 0, 0, tiled=True)  14.6 us
    ppermute x9, waiting for transfers between devices, passed_along(): lax.ppermute(block, axis, [((i - distance) % n, i) for i in range(n)])  7.79 us
  transfers between devices with their start and end apart: 10, of which 4 were waited for; matrix products, arithmetic and copies ran while one was open for 0% of the time, Pallas kernels for 0%

profile of v2, /device:TPU:1, one launch (start us, length us, event | category | flops | bytes accessed | tf_op | source)
XLA Modules:
  0.0 104.3 jit_solution(14273188918064921818)
XLA Ops:
  0.0 0.9 copy.16
  0.9 0.1 pad_maximum_fusion
  1.0 0.9 broadcast_in_dim.2
  1.9 14.6 %all-to-all-start = ((bf16[64,32,128]{2,1,0:T(8,128)(2,1)}), bf16[64,32,128]{2,1,0:T(8,128)(2,1)S(1)}, u32[]{:S(2)}, u32[]{:S(2)}) async-start(bf16[64,32,128]{2,1,0:T(8,128)(2,1)} %broadcast_in_dim.2), calls=%async_computation | async-start | bytes 1048576 | tf_op jit(solution)/shard_map/all_to_all | solution.py:26
  16.5 0.7 copy-done.1
  17.2 0.1 copy.20.cols_at
  17.3 4.5 %collective-permute-start.2 = (s32[4,2]{1,0:T(4,128)S(1)}, s32[4,2]{1,0:T(4,128)S(1)}, u32[]{:S(2)}, u32[]{:S(2)}) collective-permute-start(s32[4,2]{1,0:T(4,128)S(1)} %copy.20.cols_at), channel_id=1, source_target_pairs={{192,0},{256,64},{320,128},{384,192},{448,256},{512,320},{576,384}... | collective-permute-start | bytes 104 | tf_op jit(solution)/shard_map/ppermute | solution.py:22
  21.8 10.6 %collective-permute-start.1 = (s32[4,2]{1,0:T(4,128)S(1)}, s32[4,2]{1,0:T(4,128)S(1)}, u32[]{:S(2)}, u32[]{:S(2)}) collective-permute-start(s32[4,2]{1,0:T(4,128)S(1)} %copy.20.cols_at), channel_id=1, source_target_pairs={{128,0},{192,64},{256,128},{320,192},{384,256},{448,320},{512,384}... | collective-permute-start | bytes 104 | tf_op jit(solution)/shard_map/ppermute | solution.py:22
  32.4 3.2 %collective-permute-start = (s32[4,2]{1,0:T(4,128)S(1)}, s32[4,2]{1,0:T(4,128)S(1)}, u32[]{:S(2)}, u32[]{:S(2)}) collective-permute-start(s32[4,2]{1,0:T(4,128)S(1)} %copy.20.cols_at), channel_id=1, source_target_pairs={{64,0},{128,64},{192,128},{256,192},{320,256},{384,320},{448,384},... | collective-permute-start | bytes 104 | tf_op jit(solution)/shard_map/ppermute | solution.py:22
  35.6 0.1 copy.19.rows_at
  35.7 5.0 %collective-permute-done.far1 = s32[4,2]{1,0:T(4,128)S(1)} collective-permute-done((s32[4,2]{1,0:T(4,128)S(1)}, s32[4,2]{1,0:T(4,128)S(1)}, u32[]{:S(2)}, u32[]{:S(2)}) %collective-permute-start) | collective-permute-done | bytes 64 | tf_op jit(solution)/shard_map/ppermute | solution.py:22
  40.6 1.0 shard_map.46
  41.6 5.8 %collective-permute-start.3 = (bf16[128,256]{1,0:T(8,128)(2,1)S(1)}, bf16[128,256]{1,0:T(8,128)(2,1)S(1)}, u32[]{:S(2)}, u32[]{:S(2)}) collective-permute-start(bf16[128,256]{1,0:T(8,128)(2,1)S(1)} %get-tuple-element.11), channel_id=1, source_target_pairs={{704,0},{0,64},{64,128},{128,192},{192,256},{256,320},{320,384},{3... | collective-permute-start | bytes 196616 | tf_op jit(solution)/shard_map/ppermute | solution.py:22
  47.5 4.0 %collective-permute-start.4 = (bf16[128,256]{1,0:T(8,128)(2,1)S(1)}, bf16[128,256]{1,0:T(8,128)(2,1)S(1)}, u32[]{:S(2)}, u32[]{:S(2)}) collective-permute-start(bf16[128,256]{1,0:T(8,128)(2,1)S(1)} %get-tuple-element.12), channel_id=1, source_target_pairs={{640,0},{704,64},{0,128},{64,192},{128,256},{192,320},{256,384},{3... | collective-permute-start | bytes 196616 | tf_op jit(solution)/shard_map/ppermute | solution.py:22
  51.5 1.9 %collective-permute-start.5 = (bf16[128,256]{1,0:T(8,128)(2,1)S(1)}, bf16[128,256]{1,0:T(8,128)(2,1)S(1)}, u32[]{:S(2)}, u32[]{:S(2)}) collective-permute-start(bf16[128,256]{1,0:T(8,128)(2,1)S(1)} %get-tuple-element.13), channel_id=1, source_target_pairs={{576,0},{640,64},{704,128},{0,192},{64,256},{128,320},{192,384},{2... | collective-permute-start | bytes 196616 | tf_op jit(solution)/shard_map/ppermute | solution.py:22
  53.4 7.2 %collective-permute-start.6 = (bf16[128,256]{1,0:T(8,128)(2,1)S(1)}, bf16[128,256]{1,0:T(8,128)(2,1)S(1)}, u32[]{:S(2)}, u32[]{:S(2)}) collective-permute-start(bf16[128,256]{1,0:T(8,128)(2,1)S(1)} %get-tuple-element.14), channel_id=1, source_target_pairs={{64,0},{128,64},{192,128},{256,192},{320,256},{384,320},{448,384},... | collective-permute-start | bytes 196616 | tf_op jit(solution)/shard_map/ppermute | solution.py:22
  60.7 4.3 %collective-permute-start.7 = (bf16[128,256]{1,0:T(8,128)(2,1)S(1)}, bf16[128,256]{1,0:T(8,128)(2,1)S(1)}, u32[]{:S(2)}, u32[]{:S(2)}) collective-permute-start(bf16[128,256]{1,0:T(8,128)(2,1)S(1)} %get-tuple-element.15), channel_id=1, source_target_pairs={{128,0},{192,64},{256,128},{320,192},{384,256},{448,320},{512,384}... | collective-permute-start | bytes 196616 | tf_op jit(solution)/shard_map/ppermute | solution.py:22
  65.0 2.5 %collective-permute-start.8 = (bf16[128,256]{1,0:T(8,128)(2,1)S(1)}, bf16[128,256]{1,0:T(8,128)(2,1)S(1)}, u32[]{:S(2)}, u32[]{:S(2)}) collective-permute-start(bf16[128,256]{1,0:T(8,128)(2,1)S(1)} %get-tuple-element.16), channel_id=1, source_target_pairs={{192,0},{256,64},{320,128},{384,192},{448,256},{512,320},{576,384}... | collective-permute-start | bytes 196616 | tf_op jit(solution)/shard_map/ppermute | solution.py:22
  67.5 1.8 %collective-permute-done.6.p1 = bf16[128,256]{1,0:T(8,128)(2,1)S(1)} collective-permute-done((bf16[128,256]{1,0:T(8,128)(2,1)S(1)}, bf16[128,256]{1,0:T(8,128)(2,1)S(1)}, u32[]{:S(2)}, u32[]{:S(2)}) %collective-permute-start.6) | collective-permute-done | bytes 65568 | tf_op jit(solution)/shard_map/ppermute | solution.py:22
  69.3 0.4 collective-permute-done.7.p2
  69.8 0.5 collective-permute-done.8.p3
  70.3 1.4 %shard_map.47 = bf16[2048,128]{1,0:T(8,128)(2,1)S(1)} custom-call(s32[4,2]{1,0:T(4,128)S(1)} %copy.19.rows_at, s32[4,2]{1,0:T(4,128)S(1)} %copy.20.cols_at, s32[4,2]{1,0:T(4,128)S(1)} %collective-permute-done.far1, s32[4,2]{1,0:T(4,128)S(1)} %collective-permute-done.1.far2, s32[4,2]{1,0:T(4,128)S(1)} %collective-permute-done.2.far3, ...), custom_call_target="tpu_custom_call" | custom-call | tf_op jit(solution)/shard_map/pallas_call | solution.py:117
  71.7 31.6 %all_to_all.10 = bf16[64,32,128]{2,1,0:T(8,128)(2,1)S(1)} all-to-all(bf16[64,32,128]{2,1,0:T(8,128)(2,1)S(1)} %bitcast.14), channel_id=1, replica_groups=mesh['blk'=12,'col'=64] {'col'}, dimensions={0} | all-to-all | bytes 1048576 | tf_op jit(solution)/shard_map/all_to_all | solution.py:26
  103.4 0.9 shard_map.48
  (12 shorter events, 0.0 us)
Async XLA Ops:
  0.0 40.6 %copy-start = (bf16[1,1,4,2,256,256]{5,4,3,2,1,0:T(8,128)(2,1)S(1)}, bf16[1,1,4,2,256,256]{5,4,3,2,1,0:T(8,128)(2,1)}, u32[]{:S(2)}) copy-start(bf16[1,1,4,2,256,256]{5,4,3,2,1,0:T(8,128)(2,1)} %param.5) | copy-start | bytes 3145732
  1.9 38.7 %all-to-all-start = ((bf16[64,32,128]{2,1,0:T(8,128)(2,1)}), bf16[64,32,128]{2,1,0:T(8,128)(2,1)S(1)}, u32[]{:S(2)}, u32[]{:S(2)}) async-start(bf16[64,32,128]{2,1,0:T(8,128)(2,1)} %broadcast_in_dim.2), calls=%async_computation | async-start | bytes 1048576 | tf_op jit(solution)/shard_map/all_to_all | solution.py:26
  16.5 0.7 copy-start.1
  17.3 18.3 %copy-start.2 = (s32[1,1,4,2]{2,3,1,0:T(2,128)S(1)}, s32[1,1,4,2]{2,3,1,0:T(2,128)}, u32[]{:S(2)}) copy-start(s32[1,1,4,2]{2,3,1,0:T(2,128)} %param.6) | copy-start | bytes 100
  17.3 18.4 %collective-permute-start.2 = (s32[4,2]{1,0:T(4,128)S(1)}, s32[4,2]{1,0:T(4,128)S(1)}, u32[]{:S(2)}, u32[]{:S(2)}) collective-permute-start(s32[4,2]{1,0:T(4,128)S(1)} %copy.20.cols_at), channel_id=1, source_target_pairs={{192,0},{256,64},{320,128},{384,192},{448,256},{512,320},{576,384}... | collective-permute-start | bytes 104 | tf_op jit(solution)/shard_map/ppermute | solution.py:22
  21.8 13.9 %collective-permute-start.1 = (s32[4,2]{1,0:T(4,128)S(1)}, s32[4,2]{1,0:T(4,128)S(1)}, u32[]{:S(2)}, u32[]{:S(2)}) collective-permute-start(s32[4,2]{1,0:T(4,128)S(1)} %copy.20.cols_at), channel_id=1, source_target_pairs={{128,0},{192,64},{256,128},{320,192},{384,256},{448,320},{512,384}... | collective-permute-start | bytes 104 | tf_op jit(solution)/shard_map/ppermute | solution.py:22
  32.4 8.2 %collective-permute-start = (s32[4,2]{1,0:T(4,128)S(1)}, s32[4,2]{1,0:T(4,128)S(1)}, u32[]{:S(2)}, u32[]{:S(2)}) collective-permute-start(s32[4,2]{1,0:T(4,128)S(1)} %copy.20.cols_at), channel_id=1, source_target_pairs={{64,0},{128,64},{192,128},{256,192},{320,256},{384,320},{448,384},... | collective-permute-start | bytes 104 | tf_op jit(solution)/shard_map/ppermute | solution.py:22
  41.6 23.4 %collective-permute-start.3 = (bf16[128,256]{1,0:T(8,128)(2,1)S(1)}, bf16[128,256]{1,0:T(8,128)(2,1)S(1)}, u32[]{:S(2)}, u32[]{:S(2)}) collective-permute-start(bf16[128,256]{1,0:T(8,128)(2,1)S(1)} %get-tuple-element.11), channel_id=1, source_target_pairs={{704,0},{0,64},{64,128},{128,192},{192,256},{256,320},{320,384},{3... | collective-permute-start | bytes 196616 | tf_op jit(solution)/shard_map/ppermute | solution.py:22
  47.5 20.0 %collective-permute-start.4 = (bf16[128,256]{1,0:T(8,128)(2,1)S(1)}, bf16[128,256]{1,0:T(8,128)(2,1)S(1)}, u32[]{:S(2)}, u32[]{:S(2)}) collective-permute-start(bf16[128,256]{1,0:T(8,128)(2,1)S(1)} %get-tuple-element.12), channel_id=1, source_target_pairs={{640,0},{704,64},{0,128},{64,192},{128,256},{192,320},{256,384},{3... | collective-permute-start | bytes 196616 | tf_op jit(solution)/shard_map/ppermute | solution.py:22
  51.5 16.0 %collective-permute-start.5 = (bf16[128,256]{1,0:T(8,128)(2,1)S(1)}, bf16[128,256]{1,0:T(8,128)(2,1)S(1)}, u32[]{:S(2)}, u32[]{:S(2)}) collective-permute-start(bf16[128,256]{1,0:T(8,128)(2,1)S(1)} %get-tuple-element.13), channel_id=1, source_target_pairs={{576,0},{640,64},{704,128},{0,192},{64,256},{128,320},{192,384},{2... | collective-permute-start | bytes 196616 | tf_op jit(solution)/shard_map/ppermute | solution.py:22
  53.4 15.9 %collective-permute-start.6 = (bf16[128,256]{1,0:T(8,128)(2,1)S(1)}, bf16[128,256]{1,0:T(8,128)(2,1)S(1)}, u32[]{:S(2)}, u32[]{:S(2)}) collective-permute-start(bf16[128,256]{1,0:T(8,128)(2,1)S(1)} %get-tuple-element.14), channel_id=1, source_target_pairs={{64,0},{128,64},{192,128},{256,192},{320,256},{384,320},{448,384},... | collective-permute-start | bytes 196616 | tf_op jit(solution)/shard_map/ppermute | solution.py:22
  60.7 9.1 %collective-permute-start.7 = (bf16[128,256]{1,0:T(8,128)(2,1)S(1)}, bf16[128,256]{1,0:T(8,128)(2,1)S(1)}, u32[]{:S(2)}, u32[]{:S(2)}) collective-permute-start(bf16[128,256]{1,0:T(8,128)(2,1)S(1)} %get-tuple-element.15), channel_id=1, source_target_pairs={{128,0},{192,64},{256,128},{320,192},{384,256},{448,320},{512,384}... | collective-permute-start | bytes 196616 | tf_op jit(solution)/shard_map/ppermute | solution.py:22
  65.0 5.3 %collective-permute-start.8 = (bf16[128,256]{1,0:T(8,128)(2,1)S(1)}, bf16[128,256]{1,0:T(8,128)(2,1)S(1)}, u32[]{:S(2)}, u32[]{:S(2)}) collective-permute-start(bf16[128,256]{1,0:T(8,128)(2,1)S(1)} %get-tuple-element.16), channel_id=1, source_target_pairs={{192,0},{256,64},{320,128},{384,192},{448,256},{512,320},{576,384}... | collective-permute-start | bytes 196616 | tf_op jit(solution)/shard_map/ppermute | solution.py:22

commit v3 on v2

v3 whole, which is shorter than its diff:
```python
import jax
import jax.numpy as jnp
from jax import lax
from jax.experimental import pallas as pl
from jax.experimental.pallas import tpu as pltpu
from jax.sharding import Mesh, PartitionSpec as P

BF16 = jnp.bfloat16
F32 = jnp.float32
COL = 64
NBB = 16
NV = 64
BS = 256
STEPS = 4
AXES = ("blk", "pos", "core")
SLOTS = 2
HALF = 128
CHUNK = 32


def routed(block, near, far):
    sizes = [lax.axis_size(axis) for axis in AXES]
    n, positions, cores = sizes
    route = []
    for shard in range(n):
        for place in range(positions * cores):
            step = far if place % cores else near
            route.append((shard * positions * cores + place, (shard + step) % n * positions * cores + place))
    return lax.ppermute(block, AXES, route)


def exchanged(flat, rows):
    pieces = lax.all_to_all(flat.reshape(COL, rows, HALF), ("pos", "core"), 0, 0, tiled=True)
    return pieces.reshape(COL * rows, HALF)


def swapped(pair):
    return lax.all_to_all(pair, "core", 0, 0, tiled=True)


def dense_block(held, index):
    tops, bottoms = [], []
    for quarter in range(4):
        start = pl.multiple_of((index * 4 + quarter) * CHUNK, CHUNK)
        piece = held[pl.ds(start, CHUNK), :]
        tops.append(piece[:, :64])
        bottoms.append(piece[:, 64:])
    top = jnp.concatenate(tops, axis=1)
    bottom = jnp.concatenate(bottoms, axis=1)
    return jnp.concatenate([top, bottom], axis=0)


def times(left, block):
    return lax.dot_general(left, block, (((1,), (0,)), ((), ())), preferred_element_type=F32)


def times_transposed(left, block):
    return lax.dot_general(left, block, (((1,), (1,)), ((), ())), preferred_element_type=F32)


def neighbours_blocks(rows_at, far, far3, held, blocks, picked, picked3, partials, partials3):
    mine = 1 + lax.axis_index("core")
    for k in range(SLOTS):
        part = slice(NV * k, NV * (k + 1))
        for core in range(2):
            picked[core, part, :] = dense_block(held, far[core, mine, k])
        picked3[part, :] = dense_block(held, far3[3, k])
    for step in range(1, STEPS):
        for k in range(SLOTS):
            part = slice(NV * k, NV * (k + 1))
            left = dense_block(held, rows_at[step, k])
            partial = times(left, blocks[step * SLOTS + k]).astype(BF16)
            if step < 3:
                partials[step - 1, part, :] = partial
            else:
                partials3[part, :] = partial


def own_products(rows_at, cols_at, far, far3, held, blocks, right, right3, back, back3, out, total):
    mine = 1 + lax.axis_index("core")
    total[...] = jnp.zeros_like(total)
    for k in range(SLOTS):
        part = slice(NV * k, NV * (k + 1))
        row, col = rows_at[0, k], cols_at[0, k]
        total[row] += times_transposed(dense_block(held, col), blocks[k])
        total[col] += times(dense_block(held, row), blocks[k])
        for step in range(1, STEPS):
            came = right[step - 1, part, :] if step < 3 else right3[part, :]
            total[rows_at[step, k]] += times_transposed(came, blocks[step * SLOTS + k])
        for core in range(2):
            total[far[core, mine, k]] += back[core, part, :].astype(F32)
        total[far3[3, k]] += back3[part, :].astype(F32)
    for row in range(NBB):
        whole = total[row]
        for q in range(4):
            part = whole[:, 64 * q : 64 * q + 64]
            start = (row * 4 + q) * CHUNK
            out[start : start + CHUNK, :] = jnp.concatenate([part[:32], part[32:]], axis=1).astype(BF16)


def gathered_sum(arrived, out):
    sums = [arrived[i * CHUNK : (i + 1) * CHUNK, :].astype(F32) for i in range(4)]
    for i in range(4, COL):
        sums[i % 4] += arrived[i * CHUNK : (i + 1) * CHUNK, :].astype(F32)
    packed = (sums[0] + sums[1]) + (sums[2] + sums[3])
    own = jnp.concatenate([packed[:, :64], packed[:, 64:]], axis=0)
    out[...] = jnp.transpose(jnp.concatenate([own, own], axis=1))[:64]


VM = pl.BlockSpec(memory_space=pltpu.VMEM)
SM = pl.BlockSpec(memory_space=pltpu.SMEM)
PARAMS = pltpu.CompilerParams(vmem_limit_bytes=24 * 1024 * 1024)


def shape_of(shape, dtype):
    return jax.ShapeDtypeStruct(shape, dtype)


def per_device(vectors, blocks, row_blocks, col_blocks):
    stored = blocks.reshape(STEPS * SLOTS, BS, BS)
    rows_at = row_blocks[0, 0]
    cols_at = col_blocks[0, 0]
    turned = vectors.T.astype(BF16)
    far = routed(lax.all_gather(cols_at, "core"), -1, -2)
    far3 = routed(cols_at, -3, -3)
    packed = jnp.concatenate([turned[:32], turned[32:]], axis=1)
    held = exchanged(jnp.broadcast_to(packed[None], (COL, CHUNK, HALF)), CHUNK)
    one = shape_of((SLOTS * NV, BS), BF16)
    two = shape_of((2, SLOTS * NV, BS), BF16)
    picked, picked3, partials, partials3 = pl.pallas_call(
        neighbours_blocks,
        out_shape=(two, one, two, one),
        in_specs=[SM] * 3 + [VM] * 2,
        out_specs=(VM,) * 4,
        compiler_params=PARAMS,
    )(rows_at, far, far3, held, stored)
    right = swapped(routed(picked, 1, 2))
    right3 = routed(picked3, 3, 3)
    back = routed(swapped(partials), -1, -2)
    back3 = routed(partials3, -3, -3)
    sums = pl.pallas_call(
        own_products,
        out_shape=shape_of((COL * CHUNK, HALF), BF16),
        in_specs=[SM] * 4 + [VM] * 6,
        out_specs=VM,
        scratch_shapes=[pltpu.VMEM((NBB, NV, BS), F32)],
        compiler_params=PARAMS,
    )(rows_at, cols_at, far, far3, held, stored, right, right3, back, back3)
    return pl.pallas_call(
        gathered_sum,
        out_shape=shape_of((64, NV), F32),
        in_specs=[VM],
        out_specs=VM,
        compiler_params=PARAMS,
    )(exchanged(sums, CHUNK))


def solution(mesh):
    shards, places = mesh.devices.shape
    fine = Mesh(mesh.devices.reshape(shards, places // 2, 2), AXES)
    rest = ("pos", "core")
    return jax.shard_map(
        per_device,
        mesh=fine,
        in_specs=(
            P(AXES, None),
            P("blk", rest, None, None, None, None),
            P("blk", rest, None, None),
            P("blk", rest, None, None),
        ),
        out_specs=P(AXES, None),
        check_vma=False,
    )
```

time: 105 us -> 98.6 us (0.939)
  waiting for transfers between devices: 7.8 us -> 3.03 us
  starting transfers between devices: 58.6 us -> 55.5 us
  blocking collectives: 31.6 us -> 33.2 us
    ppermute x9 -> x6, starting transfers between devices: 44 us -> 37.5 us  [routed(): return lax.ppermute(block, AXES, route)]
    ppermute x9 -> x6, waiting for transfers between devices: 7.79 us -> 1.96 us  [routed(): return lax.ppermute(block, AXES, route)]
    all_to_all x1 -> x2, starting transfers between devices: 14.6 us -> 18 us  [the longest x1 14.6 us: exchanged(): lax.all_to_all(flat.reshape(COL, rows, HALF), ('pos', 'core'), 0, 0, tile...]
    all_gather x0 -> x1, blocking collectives: none -> 2.2 us  [per_device(): far = routed(lax.all_gather(cols_at, 'core'), -1, -2)]
    all_to_all x1 -> x2, waiting for transfers between devices: 0.01 us -> 1.08 us  [the longest x1 1.07 us: swapped(): return lax.all_to_all(pair, 'core', 0, 0, tiled=True)]
    all_to_all x1 -> x2, blocking collectives: 31.6 us -> 31 us  [the longest x1 27.5 us: exchanged(): lax.all_to_all(flat.reshape(COL, rows, HALF), ('pos', 'core'), 0, 0, tile...]
  transfers between devices with their start and end apart: 10 -> 8, of which waited for: 4 -> 2; matrix products, arithmetic and copies ran while one was open for 0% -> 0% of each run, Pallas kernels for 0% -> 0%
where the time goes in v3:
time: 98.6 us; the launch traced here: 98.1 us
  starting transfers between devices  55.5 us (56%)
  blocking collectives  33.2 us (34%)
  Pallas kernels  3.32 us (3%)
  waiting for transfers between devices  3.03 us (3%)
  local copies, waits for them, and re-layouts  2.77 us (3%)
    ppermute x6, starting transfers between devices, routed(): return lax.ppermute(block, AXES, route)  37.5 us
    all_to_all x1, blocking collectives, exchanged(): lax.all_to_all(flat.reshape(COL, rows, HALF), ('pos', 'core'), 0, 0, tile...  27.5 us
    all_to_all x1, starting transfers between devices, exchanged(): lax.all_to_all(flat.reshape(COL, rows, HALF), ('pos', 'core'), 0, 0, tile...  14.6 us
    all_to_all x1, blocking collectives, swapped(): return lax.all_to_all(pair, 'core', 0, 0, tiled=True)  3.5 us
    all_to_all x1, starting transfers between devices, swapped(): return lax.all_to_all(pair, 'core', 0, 0, tiled=True)  3.38 us
    all_gather x1, blocking collectives, per_device(): far = routed(lax.all_gather(cols_at, 'core'), -1, -2)  2.2 us
  transfers between devices with their start and end apart: 8, of which 2 were waited for; matrix products, arithmetic and copies ran while one was open for 0% of the time, Pallas kernels for 0%

profile of v3, /device:TPU:1, one launch (start us, length us, event | category | flops | bytes accessed | tf_op | source)
XLA Modules:
  0.0 98.1 jit_solution(569725851949926066)
XLA Ops:
  0.0 0.9 copy.13
  0.9 0.1 pad_maximum_fusion
  1.0 0.9 broadcast_in_dim.2
  1.9 14.6 %all-to-all-start = ((bf16[64,32,128]{2,1,0:T(8,128)(2,1)}), bf16[64,32,128]{2,1,0:T(8,128)(2,1)S(1)}, u32[]{:S(2)}, u32[]{:S(2)}) async-start(bf16[64,32,128]{2,1,0:T(8,128)(2,1)} %broadcast_in_dim.2), calls=%async_computation | async-start | bytes 1048576 | tf_op jit(solution)/shard_map/all_to_all | solution.py:33
  16.5 0.0 copy-start.1
  16.5 0.7 copy-done.1
  17.2 0.1 copy.16.cols_at
  17.3 4.4 %collective-permute-start.1 = (s32[4,2]{1,0:T(4,128)S(1)}, s32[4,2]{1,0:T(4,128)S(1)}, u32[]{:S(2)}, u32[]{:S(2)}) collective-permute-start(s32[4,2]{1,0:T(4,128)S(1)} %copy.16.cols_at), channel_id=1, source_target_pairs={{0,576},{1,577},{2,578},{3,579},{4,580},{5,581},{6,582},{7,583},{8... | collective-permute-start | bytes 104 | tf_op jit(solution)/shard_map/ppermute | solution.py:29
  21.6 2.2 %all-gather = s32[2,1,4,2]{2,3,1,0:T(2,128)S(1)} all-gather(s32[1,1,4,2]{2,3,1,0:T(2,128)S(1)} %copy-done.1), channel_id=2, replica_groups=mesh['blk'=12,'pos'=32,'core'=2] {'core'}, dimensions={0}, use_global_device_ids=true | all-gather | bytes 96 | tf_op jit(solution)/shard_map/all_gather | solution.py:124
  23.9 0.1 copy.11
  24.0 10.7 %collective-permute-start = (s32[2,4,2]{2,1,0:T(4,128)S(1)}, s32[2,4,2]{2,1,0:T(4,128)S(1)}, u32[]{:S(2)}, u32[]{:S(2)}) collective-permute-start(s32[2,4,2]{2,1,0:T(4,128)S(1)} %copy.11), channel_id=1, source_target_pairs={{0,704},{1,641},{2,706},{3,643},{4,708},{5,645},{6,710},{7,647},{8... | collective-permute-start | bytes 200 | tf_op jit(solution)/shard_map/ppermute | solution.py:29
  34.7 0.1 copy.15.rows_at
  34.8 1.9 %collective-permute-done.far = s32[2,4,2]{2,1,0:T(4,128)S(1)} collective-permute-done((s32[2,4,2]{2,1,0:T(4,128)S(1)}, s32[2,4,2]{2,1,0:T(4,128)S(1)}, u32[]{:S(2)}, u32[]{:S(2)}) %collective-permute-start) | collective-permute-done | bytes 96 | tf_op jit(solution)/shard_map/ppermute | solution.py:29
  36.7 1.0 shard_map.46
  37.7 8.8 %collective-permute-start.2 = (bf16[2,128,256]{2,1,0:T(8,128)(2,1)S(1)}, bf16[2,128,256]{2,1,0:T(8,128)(2,1)}, u32[]{:S(2)}, u32[]{:S(2)}) collective-permute-start(bf16[2,128,256]{2,1,0:T(8,128)(2,1)S(1)} %get-tuple-element.9), channel_id=1, source_target_pairs={{0,64},{1,129},{2,66},{3,131},{4,68},{5,133},{6,70},{7,135},{8,72}... | collective-permute-start | bytes 393224 | tf_op jit(solution)/shard_map/ppermute | solution.py:29
  46.5 3.5 %all_to_all.20 = bf16[2,128,256]{2,1,0:T(8,128)(2,1)S(1)} all-to-all(bf16[2,128,256]{2,1,0:T(8,128)(2,1)S(1)} %get-tuple-element.11), channel_id=1, replica_groups=mesh['blk'=12,'pos'=32,'core'=2] {'core'}, dimensions={0} | all-to-all | bytes 262144 | tf_op jit(solution)/shard_map/all_to_all | solution.py:38
  50.0 7.1 %collective-permute-start.4 = (bf16[2,128,256]{2,1,0:T(8,128)(2,1)S(1)}, bf16[2,128,256]{2,1,0:T(8,128)(2,1)S(1)}, u32[]{:S(2)}, u32[]{:S(2)}) collective-permute-start(bf16[2,128,256]{2,1,0:T(8,128)(2,1)S(1)} %all_to_all.20), channel_id=1, source_target_pairs={{0,704},{1,641},{2,706},{3,643},{4,708},{5,645},{6,710},{7,647},{8... | collective-permute-start | bytes 393224 | tf_op jit(solution)/shard_map/ppermute | solution.py:29
  57.1 1.9 %collective-permute-start.3 = (bf16[128,256]{1,0:T(8,128)(2,1)S(1)}, bf16[128,256]{1,0:T(8,128)(2,1)S(1)}, u32[]{:S(2)}, u32[]{:S(2)}) collective-permute-start(bf16[128,256]{1,0:T(8,128)(2,1)S(1)} %get-tuple-element.10), channel_id=1, source_target_pairs={{0,192},{1,193},{2,194},{3,195},{4,196},{5,197},{6,198},{7,199},{8... | collective-permute-start | bytes 196616 | tf_op jit(solution)/shard_map/ppermute | solution.py:29
  59.1 4.6 %collective-permute-start.5 = (bf16[128,256]{1,0:T(8,128)(2,1)S(1)}, bf16[128,256]{1,0:T(8,128)(2,1)S(1)}, u32[]{:S(2)}, u32[]{:S(2)}) collective-permute-start(bf16[128,256]{1,0:T(8,128)(2,1)S(1)} %get-tuple-element.12), channel_id=1, source_target_pairs={{0,576},{1,577},{2,578},{3,579},{4,580},{5,581},{6,582},{7,583},{8... | collective-permute-start | bytes 196616 | tf_op jit(solution)/shard_map/ppermute | solution.py:29
  63.7 3.4 %all-to-all-start.1 = ((bf16[2,128,256]{2,1,0:T(8,128)(2,1)}), bf16[2,128,256]{2,1,0:T(8,128)(2,1)S(1)}, u32[]{:S(2)}, u32[]{:S(2)}) async-start(bf16[2,128,256]{2,1,0:T(8,128)(2,1)} %collective-permute-done.2), calls=%async_computation.1 | async-start | bytes 262144 | tf_op jit(solution)/shard_map/all_to_all | solution.py:38
  67.1 1.1 %all-to-all-done.1.right = bf16[2,128,256]{2,1,0:T(8,128)(2,1)S(1)} async-done(((bf16[2,128,256]{2,1,0:T(8,128)(2,1)}), bf16[2,128,256]{2,1,0:T(8,128)(2,1)S(1)}, u32[]{:S(2)}, u32[]{:S(2)}) %all-to-all-start.1) | async-done | bytes 131104 | tf_op jit(solution)/shard_map/all_to_all | solution.py:38
  68.2 1.5 %shard_map.47 = bf16[2048,128]{1,0:T(8,128)(2,1)S(1)} custom-call(s32[4,2]{1,0:T(4,128)S(1)} %copy.15.rows_at, s32[4,2]{1,0:T(4,128)S(1)} %copy.16.cols_at, s32[2,4,2]{2,1,0:T(4,128)S(1)} %collective-permute-done.far, s32[4,2]{1,0:T(4,128)S(1)} %collective-permute-done.1.far3, bf16[2048,128]{1,0:T(8,128)(2,1)S(1)} %bitcast.11, ...), custom_call_target="tpu_custom_call" | custom-call | tf_op jit(solution)/shard_map/pallas_call | solution.py:141
  69.6 27.5 %all_to_all.21 = bf16[64,32,128]{2,1,0:T(8,128)(2,1)S(1)} all-to-all(bf16[64,32,128]{2,1,0:T(8,128)(2,1)S(1)} %bitcast.15), channel_id=1, replica_groups=mesh['blk'=12,'pos'=32,'core'=2] {'pos','core'}, dimensions={0} | all-to-all | bytes 1048576 | tf_op jit(solution)/shard_map/all_to_all | solution.py:33
  97.2 0.9 shard_map.48
  (11 shorter events, 0.0 us)
Async XLA Ops:
  0.0 36.7 %copy-start = (bf16[1,1,4,2,256,256]{5,4,3,2,1,0:T(8,128)(2,1)S(1)}, bf16[1,1,4,2,256,256]{5,4,3,2,1,0:T(8,128)(2,1)}, u32[]{:S(2)}) copy-start(bf16[1,1,4,2,256,256]{5,4,3,2,1,0:T(8,128)(2,1)} %param.5) | copy-start | bytes 3145732
  1.9 34.8 %all-to-all-start = ((bf16[64,32,128]{2,1,0:T(8,128)(2,1)}), bf16[64,32,128]{2,1,0:T(8,128)(2,1)S(1)}, u32[]{:S(2)}, u32[]{:S(2)}) async-start(bf16[64,32,128]{2,1,0:T(8,128)(2,1)} %broadcast_in_dim.2), calls=%async_computation | async-start | bytes 1048576 | tf_op jit(solution)/shard_map/all_to_all | solution.py:33
  16.5 0.7 copy-start.1
  17.3 17.5 %collective-permute-start.1 = (s32[4,2]{1,0:T(4,128)S(1)}, s32[4,2]{1,0:T(4,128)S(1)}, u32[]{:S(2)}, u32[]{:S(2)}) collective-permute-start(s32[4,2]{1,0:T(4,128)S(1)} %copy.16.cols_at), channel_id=1, source_target_pairs={{0,576},{1,577},{2,578},{3,579},{4,580},{5,581},{6,582},{7,583},{8... | collective-permute-start | bytes 104 | tf_op jit(solution)/shard_map/ppermute | solution.py:29
  23.9 10.7 %copy-start.2 = (s32[1,1,4,2]{2,3,1,0:T(2,128)S(1)}, s32[1,1,4,2]{2,3,1,0:T(2,128)}, u32[]{:S(2)}) copy-start(s32[1,1,4,2]{2,3,1,0:T(2,128)} %param.6) | copy-start | bytes 100
  24.0 12.8 %collective-permute-start = (s32[2,4,2]{2,1,0:T(4,128)S(1)}, s32[2,4,2]{2,1,0:T(4,128)S(1)}, u32[]{:S(2)}, u32[]{:S(2)}) collective-permute-start(s32[2,4,2]{2,1,0:T(4,128)S(1)} %copy.11), channel_id=1, source_target_pairs={{0,704},{1,641},{2,706},{3,643},{4,708},{5,645},{6,710},{7,647},{8... | collective-permute-start | bytes 200 | tf_op jit(solution)/shard_map/ppermute | solution.py:29
  37.7 25.9 %collective-permute-start.2 = (bf16[2,128,256]{2,1,0:T(8,128)(2,1)S(1)}, bf16[2,128,256]{2,1,0:T(8,128)(2,1)}, u32[]{:S(2)}, u32[]{:S(2)}) collective-permute-start(bf16[2,128,256]{2,1,0:T(8,128)(2,1)S(1)} %get-tuple-element.9), channel_id=1, source_target_pairs={{0,64},{1,129},{2,66},{3,131},{4,68},{5,133},{6,70},{7,135},{8,72}... | collective-permute-start | bytes 393224 | tf_op jit(solution)/shard_map/ppermute | solution.py:29
  50.0 17.1 %collective-permute-start.4 = (bf16[2,128,256]{2,1,0:T(8,128)(2,1)S(1)}, bf16[2,128,256]{2,1,0:T(8,128)(2,1)S(1)}, u32[]{:S(2)}, u32[]{:S(2)}) collective-permute-start(bf16[2,128,256]{2,1,0:T(8,128)(2,1)S(1)} %all_to_all.20), channel_id=1, source_target_pairs={{0,704},{1,641},{2,706},{3,643},{4,708},{5,645},{6,710},{7,647},{8... | collective-permute-start | bytes 393224 | tf_op jit(solution)/shard_map/ppermute | solution.py:29
  57.1 9.9 %collective-permute-start.3 = (bf16[128,256]{1,0:T(8,128)(2,1)S(1)}, bf16[128,256]{1,0:T(8,128)(2,1)S(1)}, u32[]{:S(2)}, u32[]{:S(2)}) collective-permute-start(bf16[128,256]{1,0:T(8,128)(2,1)S(1)} %get-tuple-element.10), channel_id=1, source_target_pairs={{0,192},{1,193},{2,194},{3,195},{4,196},{5,197},{6,198},{7,199},{8... | collective-permute-start | bytes 196616 | tf_op jit(solution)/shard_map/ppermute | solution.py:29
  59.1 8.0 %collective-permute-start.5 = (bf16[128,256]{1,0:T(8,128)(2,1)S(1)}, bf16[128,256]{1,0:T(8,128)(2,1)S(1)}, u32[]{:S(2)}, u32[]{:S(2)}) collective-permute-start(bf16[128,256]{1,0:T(8,128)(2,1)S(1)} %get-tuple-element.12), channel_id=1, source_target_pairs={{0,576},{1,577},{2,578},{3,579},{4,580},{5,581},{6,582},{7,583},{8... | collective-permute-start | bytes 196616 | tf_op jit(solution)/shard_map/ppermute | solution.py:29
  63.7 4.5 %all-to-all-start.1 = ((bf16[2,128,256]{2,1,0:T(8,128)(2,1)}), bf16[2,128,256]{2,1,0:T(8,128)(2,1)S(1)}, u32[]{:S(2)}, u32[]{:S(2)}) async-start(bf16[2,128,256]{2,1,0:T(8,128)(2,1)} %collective-permute-done.2), calls=%async_computation.1 | async-start | bytes 262144 | tf_op jit(solution)/shard_map/all_to_all | solution.py:38

commit v4 on v3

--- a/solution.py
+++ b/solution.py
@@ -34,10 +34,6 @@
     return pieces.reshape(COL * rows, HALF)
 
 
-def swapped(pair):
-    return lax.all_to_all(pair, "core", 0, 0, tiled=True)
-
-
 def dense_block(held, index):
     tops, bottoms = [], []
     for quarter in range(4):
@@ -58,38 +54,54 @@
     return lax.dot_general(left, block, (((1,), (1,)), ((), ())), preferred_element_type=F32)
 
 
-def neighbours_blocks(rows_at, far, far3, held, blocks, picked, picked3, partials, partials3):
-    mine = 1 + lax.axis_index("core")
+def prepared(vectors, out):
+    rows = vectors[...]
+    turned = jnp.transpose(jnp.concatenate([rows, rows], axis=1))
+    packed = jnp.concatenate([turned[:32], turned[32:64]], axis=1).astype(BF16)
+    for i in range(COL):
+        out[i * CHUNK : (i + 1) * CHUNK, :] = packed
+
+
+def shared_block(blocks, other, me, core, k):
+    if core == 0:
+        return blocks[(1 + me) * SLOTS + k]
+    return other[k]
+
+
+def transposed_products(lists, held, blocks, other, partials, partials3):
+    me = lax.axis_index("core")
     for k in range(SLOTS):
         part = slice(NV * k, NV * (k + 1))
-        for core in range(2):
-            picked[core, part, :] = dense_block(held, far[core, mine, k])
-        picked3[part, :] = dense_block(held, far3[3, k])
-    for step in range(1, STEPS):
-        for k in range(SLOTS):
-            part = slice(NV * k, NV * (k + 1))
-            left = dense_block(held, rows_at[step, k])
-            partial = times(left, blocks[step * SLOTS + k]).astype(BF16)
-            if step < 3:
-                partials[step - 1, part, :] = partial
-            else:
-                partials3[part, :] = partial
+        for core, owner in enumerate((me, 1 - me)):
+            left = dense_block(held, lists[owner, 0, 1 + me, k])
+            partials[core, part, :] = times(left, shared_block(blocks, other, me, core, k)).astype(BF16)
+        left = dense_block(held, lists[me, 0, 3, k])
+        partials3[part, :] = times(left, blocks[3 * SLOTS + k]).astype(BF16)
 
 
-def own_products(rows_at, cols_at, far, far3, held, blocks, right, right3, back, back3, out, total):
-    mine = 1 + lax.axis_index("core")
+def asked_blocks(far, far3, held, picked, picked3):
+    me = lax.axis_index("core")
+    for k in range(SLOTS):
+        part = slice(NV * k, NV * (k + 1))
+        for core, owner in enumerate((me, 1 - me)):
+            picked[core, part, :] = dense_block(held, far[owner, 1, 1 + me, k])
+        picked3[part, :] = dense_block(held, far3[me, 1, 3, k])
+
+
+def own_products(lists, far, far3, held, blocks, other, right, right3, back, back3, out, total):
+    me = lax.axis_index("core")
     total[...] = jnp.zeros_like(total)
     for k in range(SLOTS):
         part = slice(NV * k, NV * (k + 1))
-        row, col = rows_at[0, k], cols_at[0, k]
+        row, col = lists[me, 0, 0, k], lists[me, 1, 0, k]
         total[row] += times_transposed(dense_block(held, col), blocks[k])
         total[col] += times(dense_block(held, row), blocks[k])
-        for step in range(1, STEPS):
-            came = right[step - 1, part, :] if step < 3 else right3[part, :]
-            total[rows_at[step, k]] += times_transposed(came, blocks[step * SLOTS + k])
-        for core in range(2):
-            total[far[core, mine, k]] += back[core, part, :].astype(F32)
-        total[far3[3, k]] += back3[part, :].astype(F32)
+        for core, owner in enumerate((me, 1 - me)):
+            block = shared_block(blocks, other, me, core, k)
+            total[lists[owner, 0, 1 + me, k]] += times_transposed(right[core, part, :], block)
+            total[far[owner, 1, 1 + me, k]] += back[core, part, :].astype(F32)
+        total[lists[me, 0, 3, k]] += times_transposed(right3[part, :], blocks[3 * SLOTS + k])
+        total[far3[me, 1, 3, k]] += back3[part, :].astype(F32)
     for row in range(NBB):
         whole = total[row]
         for q in range(4):
@@ -118,34 +130,48 @@
 
 def per_device(vectors, blocks, row_blocks, col_blocks):
     stored = blocks.reshape(STEPS * SLOTS, BS, BS)
-    rows_at = row_blocks[0, 0]
-    cols_at = col_blocks[0, 0]
-    turned = vectors.T.astype(BF16)
-    far = routed(lax.all_gather(cols_at, "core"), -1, -2)
-    far3 = routed(cols_at, -3, -3)
-    packed = jnp.concatenate([turned[:32], turned[32:]], axis=1)
-    held = exchanged(jnp.broadcast_to(packed[None], (COL, CHUNK, HALF)), CHUNK)
+    lists = lax.all_gather(jnp.stack([row_blocks[0, 0], col_blocks[0, 0]]), "core")
+    far = routed(lists, -1, -2)
+    far3 = routed(lists, -3, -3)
+    me = lax.axis_index("core")
+    given = lax.dynamic_slice_in_dim(stored, (2 - me) * SLOTS, SLOTS, 0)
+    other = lax.ppermute(given, "core", [(0, 1), (1, 0)])
+    mine = pl.pallas_call(
+        prepared,
+        out_shape=shape_of((COL * CHUNK, HALF), BF16),
+        in_specs=[VM],
+        out_specs=VM,
+        compiler_params=PARAMS,
+    )(vectors)
+    held = exchanged(mine, CHUNK)
     one = shape_of((SLOTS * NV, BS), BF16)
     two = shape_of((2, SLOTS * NV, BS), BF16)
-    picked, picked3, partials, partials3 = pl.pallas_call(
-        neighbours_blocks,
-        out_shape=(two, one, two, one),
-        in_specs=[SM] * 3 + [VM] * 2,
-        out_specs=(VM,) * 4,
+    partials, partials3 = pl.pallas_call(
+        transposed_products,
+        out_shape=(two, one),
+        in_specs=[SM] + [VM] * 3,
+        out_specs=(VM, VM),
         compiler_params=PARAMS,
-    )(rows_at, far, far3, held, stored)
-    right = swapped(routed(picked, 1, 2))
+    )(lists, held, stored, other)
+    back = routed(partials, -1, -2)
+    back3 = routed(partials3, -3, -3)
+    picked, picked3 = pl.pallas_call(
+        asked_blocks,
+        out_shape=(two, one),
+        in_specs=[SM, SM, VM],
+        out_specs=(VM, VM),
+        compiler_params=PARAMS,
+    )(far, far3, held)
+    right = routed(picked, 1, 2)
     right3 = routed(picked3, 3, 3)
-    back = routed(swapped(partials), -1, -2)
-    back3 = routed(partials3, -3, -3)
     sums = pl.pallas_call(
         own_products,
         out_shape=shape_of((COL * CHUNK, HALF), BF16),
-        in_specs=[SM] * 4 + [VM] * 6,
+        in_specs=[SM] * 3 + [VM] * 7,
         out_specs=VM,
         scratch_shapes=[pltpu.VMEM((NBB, NV, BS), F32)],
         compiler_params=PARAMS,
-    )(rows_at, cols_at, far, far3, held, stored, right, right3, back, back3)
+    )(lists, far, far3, held, stored, other, right, right3, back, back3)
     return pl.pallas_call(
         gathered_sum,
         out_shape=shape_of((64, NV), F32),

time: 98.6 us -> 92.8 us (0.941)
  starting transfers between devices: 55.5 us -> 48.9 us
  blocking collectives: 33.2 us -> 28.6 us
  waiting for transfers between devices: 3.03 us -> 7.55 us
  Pallas kernels: 3.32 us -> 5.53 us
  local copies, waits for them, and re-layouts: 2.77 us -> 1.65 us
    ppermute x6, starting transfers between devices: 37.5 us -> 31.8 us  [routed(): return lax.ppermute(block, AXES, route)]
    ppermute x6, waiting for transfers between devices: 1.96 us -> 7.55 us  [routed(): return lax.ppermute(block, AXES, route)]
    all_to_all x1 -> x0, blocking collectives: 3.5 us -> none  [swapped(): return lax.all_to_all(pair, 'core', 0, 0, tiled=True)]
    all_to_all x1 -> x0, starting transfers between devices: 3.38 us -> none  [swapped(): return lax.all_to_all(pair, 'core', 0, 0, tiled=True)]
    ppermute x0 -> x1, starting transfers between devices: none -> 2.47 us  [per_device(): other = lax.ppermute(given, 'core', [(0, 1), (1, 0)])]
    pallas_call x1 -> x3, Pallas kernels: 0.97 us -> 2.94 us  [the longest x1 1.04 us: per_device(): pl.pallas_call(prepared, out_shape=shape_of((COL * CHUNK, HALF), BF16), i...]
    all_to_all x1 -> x0, waiting for transfers between devices: 1.07 us -> none  [swapped(): return lax.all_to_all(pair, 'core', 0, 0, tiled=True)]
  transfers between devices with their start and end apart: 8 -> 8, of which waited for: 2 -> 2; matrix products, arithmetic and copies ran while one was open for 0% -> 0% of each run, Pallas kernels for 0% -> 2%
where the time goes in v4:
time: 92.8 us; the launch traced here: 92.3 us
  starting transfers between devices  48.9 us (53%)
  blocking collectives  28.6 us (31%)
  waiting for transfers between devices  7.55 us (8%)
  Pallas kernels  5.53 us (6%)
  local copies, waits for them, and re-layouts  1.65 us (2%)
    ppermute x6, starting transfers between devices, routed(): return lax.ppermute(block, AXES, route)  31.8 us
    all_to_all x1, blocking collectives, exchanged(): lax.all_to_all(flat.reshape(COL, rows, HALF), ('pos', 'core'), 0, 0, tile...  26.8 us
    all_to_all x1, starting transfers between devices, exchanged(): lax.all_to_all(flat.reshape(COL, rows, HALF), ('pos', 'core'), 0, 0, tile...  14.6 us
    ppermute x6, waiting for transfers between devices, routed(): return lax.ppermute(block, AXES, route)  7.55 us
    ppermute x1, starting transfers between devices, per_device(): other = lax.ppermute(given, 'core', [(0, 1), (1, 0)])  2.47 us
  transfers between devices with their start and end apart: 8, of which 2 were waited for; matrix products, arithmetic and copies ran while one was open for 0% of the time, Pallas kernels for 2%

profile of v4, /device:TPU:1, one launch (start us, length us, event | category | flops | bytes accessed | tf_op | source)
XLA Modules:
  0.0 92.3 jit_solution(7281617367568253720)
XLA Ops:
  0.0 0.8 copy-done.1
  0.8 1.0 %shard_map.46 = bf16[2048,128]{1,0:T(8,128)(2,1)} custom-call(f32[64,64]{1,0:T(8,128)S(1)} %copy-done.1), custom_call_target="tpu_custom_call" | custom-call | tf_op jit(solution)/shard_map/pallas_call | solution.py:139
  1.9 14.6 %all-to-all-start = ((bf16[64,32,128]{2,1,0:T(8,128)(2,1)}), bf16[64,32,128]{2,1,0:T(8,128)(2,1)S(1)}, u32[]{:S(2)}, u32[]{:S(2)}) async-start(bf16[64,32,128]{2,1,0:T(8,128)(2,1)} %bitcast.3), calls=%async_computation | async-start | bytes 1048576 | tf_op jit(solution)/shard_map/all_to_all | solution.py:33
  16.5 0.0 copy-start.3
  16.5 2.5 %collective-permute-start.2 = (bf16[2,256,256]{2,1,0:T(8,128)(2,1)S(1)}, bf16[2,256,256]{2,1,0:T(8,128)(2,1)S(1)}, u32[]{:S(2)}, u32[]{:S(2)}) collective-permute-start(bf16[2,256,256]{2,1,0:T(8,128)(2,1)S(1)} %constant_dynamic-slice_fusion), channel_id=1, source_target_pairs={{0,1},{1,0},{2,3},{3,2},{4,5},{5,4},{6,7},{7,6},{8,9},{9,8},{10,11... | collective-permute-start | bytes 786440 | tf_op jit(solution)/shard_map/ppermute | solution.py:138
  19.0 0.0 copy-start.2
  19.0 0.7 copy-done.2
  19.7 1.8 %all-gather = s32[4,4,2]{1,2,0:T(2,128)S(1)} all-gather(s32[2,4,2]{1,2,0:T(2,128)S(1)} %pad_add_fusion), channel_id=2, replica_groups=mesh['blk'=12,'pos'=32,'core'=2] {'core'}, dimensions={0}, use_global_device_ids=true | all-gather | bytes 192 | tf_op jit(solution)/shard_map/all_gather | solution.py:133
  21.5 0.1 copy.12.lists
  21.6 4.3 %collective-permute-start.1 = (s32[2,2,4,2]{3,2,1,0:T(4,128)S(1)}, s32[2,2,4,2]{3,2,1,0:T(4,128)S(1)}, u32[]{:S(2)}, u32[]{:S(2)}) collective-permute-start(s32[2,2,4,2]{3,2,1,0:T(4,128)S(1)} %copy.12.lists), channel_id=1, source_target_pairs={{0,576},{1,577},{2,578},{3,579},{4,580},{5,581},{6,582},{7,583},{8... | collective-permute-start | bytes 392 | tf_op jit(solution)/shard_map/ppermute | solution.py:29
  25.9 10.6 %collective-permute-start = (s32[2,2,4,2]{3,2,1,0:T(4,128)S(1)}, s32[2,2,4,2]{3,2,1,0:T(4,128)S(1)}, u32[]{:S(2)}, u32[]{:S(2)}) collective-permute-start(s32[2,2,4,2]{3,2,1,0:T(4,128)S(1)} %copy.12.lists), channel_id=1, source_target_pairs={{0,704},{1,641},{2,706},{3,643},{4,708},{5,645},{6,710},{7,647},{8... | collective-permute-start | bytes 392 | tf_op jit(solution)/shard_map/ppermute | solution.py:29
  36.5 0.0 collective-permute-done.2.other
  36.5 1.0 %shard_map.48 = (bf16[2,128,256]{2,1,0:T(8,128)(2,1)S(1)}, bf16[128,256]{1,0:T(8,128)(2,1)S(1)}) custom-call(s32[2,2,4,2]{3,2,1,0:T(4,128)S(1)} %copy.12.lists, bf16[2048,128]{1,0:T(8,128)(2,1)S(1)} %bitcast.8, bf16[8,256,256]{2,1,0:T(8,128)(2,1)S(1)} %bitcast.12, bf16[2,256,256]{2,1,0:T(8,128)(2,1)S(1)} %collective-permute-done.2.other), custom_call_target="tpu_custom_call" | custom-call | tf_op jit(solution)/shard_map/pallas_call | solution.py:149
  37.5 9.7 %collective-permute-start.5 = (bf16[2,128,256]{2,1,0:T(8,128)(2,1)S(1)}, bf16[2,128,256]{2,1,0:T(8,128)(2,1)S(1)}, u32[]{:S(2)}, u32[]{:S(2)}) collective-permute-start(bf16[2,128,256]{2,1,0:T(8,128)(2,1)S(1)} %get-tuple-element.11), channel_id=1, source_target_pairs={{0,704},{1,641},{2,706},{3,643},{4,708},{5,645},{6,710},{7,647},{8... | collective-permute-start | bytes 393224 | tf_op jit(solution)/shard_map/ppermute | solution.py:29
  47.2 0.0 collective-permute-done.1.far3
  47.2 0.9 shard_map.47
  48.1 1.9 %collective-permute-start.3 = (bf16[2,128,256]{2,1,0:T(8,128)(2,1)S(1)}, bf16[2,128,256]{2,1,0:T(8,128)(2,1)S(1)}, u32[]{:S(2)}, u32[]{:S(2)}) collective-permute-start(bf16[2,128,256]{2,1,0:T(8,128)(2,1)S(1)} %get-tuple-element.9), channel_id=1, source_target_pairs={{0,64},{1,129},{2,66},{3,131},{4,68},{5,133},{6,70},{7,135},{8,72}... | collective-permute-start | bytes 393224 | tf_op jit(solution)/shard_map/ppermute | solution.py:29
  50.0 3.4 %collective-permute-start.6 = (bf16[128,256]{1,0:T(8,128)(2,1)S(1)}, bf16[128,256]{1,0:T(8,128)(2,1)S(1)}, u32[]{:S(2)}, u32[]{:S(2)}) collective-permute-start(bf16[128,256]{1,0:T(8,128)(2,1)S(1)} %get-tuple-element.12), channel_id=1, source_target_pairs={{0,576},{1,577},{2,578},{3,579},{4,580},{5,581},{6,582},{7,583},{8... | collective-permute-start | bytes 196616 | tf_op jit(solution)/shard_map/ppermute | solution.py:29
  53.5 1.9 %collective-permute-start.4 = (bf16[128,256]{1,0:T(8,128)(2,1)S(1)}, bf16[128,256]{1,0:T(8,128)(2,1)S(1)}, u32[]{:S(2)}, u32[]{:S(2)}) collective-permute-start(bf16[128,256]{1,0:T(8,128)(2,1)S(1)} %get-tuple-element.10), channel_id=1, source_target_pairs={{0,192},{1,193},{2,194},{3,195},{4,196},{5,197},{6,198},{7,199},{8... | collective-permute-start | bytes 196616 | tf_op jit(solution)/shard_map/ppermute | solution.py:29
  55.4 5.0 %collective-permute-done.4.right3 = bf16[128,256]{1,0:T(8,128)(2,1)S(1)} collective-permute-done((bf16[128,256]{1,0:T(8,128)(2,1)S(1)}, bf16[128,256]{1,0:T(8,128)(2,1)S(1)}, u32[]{:S(2)}, u32[]{:S(2)}) %collective-permute-start.4) | collective-permute-done | bytes 65568 | tf_op jit(solution)/shard_map/ppermute | solution.py:29
  60.4 2.6 %collective-permute-done.3.right = bf16[2,128,256]{2,1,0:T(8,128)(2,1)S(1)} collective-permute-done((bf16[2,128,256]{2,1,0:T(8,128)(2,1)S(1)}, bf16[2,128,256]{2,1,0:T(8,128)(2,1)S(1)}, u32[]{:S(2)}, u32[]{:S(2)}) %collective-permute-start.3) | collective-permute-done | bytes 131104 | tf_op jit(solution)/shard_map/ppermute | solution.py:29
  62.9 1.7 %shard_map.49 = bf16[2048,128]{1,0:T(8,128)(2,1)S(1)} custom-call(s32[2,2,4,2]{3,2,1,0:T(4,128)S(1)} %copy.12.lists, s32[2,2,4,2]{3,2,1,0:T(4,128)S(1)} %collective-permute-done.far, s32[2,2,4,2]{3,2,1,0:T(4,128)S(1)} %collective-permute-done.1.far3, bf16[2048,128]{1,0:T(8,128)(2,1)S(1)} %bitcast.10, bf16[8,256,256]{2,1,0:T(8,128)(2,1)S(1)} %bitcast.13, ...), custom_call_target="tpu_custom_call" | custom-call | tf_op jit(solution)/shard_map/pallas_call | solution.py:167
  64.7 26.8 %all_to_all.10 = bf16[64,32,128]{2,1,0:T(8,128)(2,1)S(1)} all-to-all(bf16[64,32,128]{2,1,0:T(8,128)(2,1)S(1)} %bitcast.15), channel_id=1, replica_groups=mesh['blk'=12,'pos'=32,'core'=2] {'pos','core'}, dimensions={0} | all-to-all | bytes 1048576 | tf_op jit(solution)/shard_map/all_to_all | solution.py:33
  91.4 0.9 shard_map.50
  (10 shorter events, 0.0 us)
Async XLA Ops:
  0.0 16.5 %copy-start = (bf16[1,1,4,2,256,256]{5,4,3,2,1,0:T(8,128)(2,1)S(1)}, bf16[1,1,4,2,256,256]{5,4,3,2,1,0:T(8,128)(2,1)}, u32[]{:S(2)}) copy-start(bf16[1,1,4,2,256,256]{5,4,3,2,1,0:T(8,128)(2,1)} %param.5) | copy-start | bytes 3145732
  0.0 0.8 copy-start.1
  1.9 34.6 %all-to-all-start = ((bf16[64,32,128]{2,1,0:T(8,128)(2,1)}), bf16[64,32,128]{2,1,0:T(8,128)(2,1)S(1)}, u32[]{:S(2)}, u32[]{:S(2)}) async-start(bf16[64,32,128]{2,1,0:T(8,128)(2,1)} %bitcast.3), calls=%async_computation | async-start | bytes 1048576 | tf_op jit(solution)/shard_map/all_to_all | solution.py:33
  16.5 2.5 %copy-start.3 = (s32[1,1,4,2]{2,3,1,0:T(2,128)S(1)}, s32[1,1,4,2]{2,3,1,0:T(2,128)}, u32[]{:S(2)}) copy-start(s32[1,1,4,2]{2,3,1,0:T(2,128)} %param.6) | copy-start | bytes 100
  16.5 19.9 %collective-permute-start.2 = (bf16[2,256,256]{2,1,0:T(8,128)(2,1)S(1)}, bf16[2,256,256]{2,1,0:T(8,128)(2,1)S(1)}, u32[]{:S(2)}, u32[]{:S(2)}) collective-permute-start(bf16[2,256,256]{2,1,0:T(8,128)(2,1)S(1)} %constant_dynamic-slice_fusion), channel_id=1, source_target_pairs={{0,1},{1,0},{2,3},{3,2},{4,5},{5,4},{6,7},{7,6},{8,9},{9,8},{10,11... | collective-permute-start | bytes 786440 | tf_op jit(solution)/shard_map/ppermute | solution.py:138
  19.0 0.7 copy-start.2
  21.6 25.6 %collective-permute-start.1 = (s32[2,2,4,2]{3,2,1,0:T(4,128)S(1)}, s32[2,2,4,2]{3,2,1,0:T(4,128)S(1)}, u32[]{:S(2)}, u32[]{:S(2)}) collective-permute-start(s32[2,2,4,2]{3,2,1,0:T(4,128)S(1)} %copy.12.lists), channel_id=1, source_target_pairs={{0,576},{1,577},{2,578},{3,579},{4,580},{5,581},{6,582},{7,583},{8... | collective-permute-start | bytes 392 | tf_op jit(solution)/shard_map/ppermute | solution.py:29
  25.9 21.3 %collective-permute-start = (s32[2,2,4,2]{3,2,1,0:T(4,128)S(1)}, s32[2,2,4,2]{3,2,1,0:T(4,128)S(1)}, u32[]{:S(2)}, u32[]{:S(2)}) collective-permute-start(s32[2,2,4,2]{3,2,1,0:T(4,128)S(1)} %copy.12.lists), channel_id=1, source_target_pairs={{0,704},{1,641},{2,706},{3,643},{4,708},{5,645},{6,710},{7,647},{8... | collective-permute-start | bytes 392 | tf_op jit(solution)/shard_map/ppermute | solution.py:29
  37.5 22.9 %collective-permute-start.5 = (bf16[2,128,256]{2,1,0:T(8,128)(2,1)S(1)}, bf16[2,128,256]{2,1,0:T(8,128)(2,1)S(1)}, u32[]{:S(2)}, u32[]{:S(2)}) collective-permute-start(bf16[2,128,256]{2,1,0:T(8,128)(2,1)S(1)} %get-tuple-element.11), channel_id=1, source_target_pairs={{0,704},{1,641},{2,706},{3,643},{4,708},{5,645},{6,710},{7,647},{8... | collective-permute-start | bytes 393224 | tf_op jit(solution)/shard_map/ppermute | solution.py:29
  48.1 14.8 %collective-permute-start.3 = (bf16[2,128,256]{2,1,0:T(8,128)(2,1)S(1)}, bf16[2,128,256]{2,1,0:T(8,128)(2,1)S(1)}, u32[]{:S(2)}, u32[]{:S(2)}) collective-permute-start(bf16[2,128,256]{2,1,0:T(8,128)(2,1)S(1)} %get-tuple-element.9), channel_id=1, source_target_pairs={{0,64},{1,129},{2,66},{3,131},{4,68},{5,133},{6,70},{7,135},{8,72}... | collective-permute-start | bytes 393224 | tf_op jit(solution)/shard_map/ppermute | solution.py:29
  50.0 5.4 %collective-permute-start.6 = (bf16[128,256]{1,0:T(8,128)(2,1)S(1)}, bf16[128,256]{1,0:T(8,128)(2,1)S(1)}, u32[]{:S(2)}, u32[]{:S(2)}) collective-permute-start(bf16[128,256]{1,0:T(8,128)(2,1)S(1)} %get-tuple-element.12), channel_id=1, source_target_pairs={{0,576},{1,577},{2,578},{3,579},{4,580},{5,581},{6,582},{7,583},{8... | collective-permute-start | bytes 196616 | tf_op jit(solution)/shard_map/ppermute | solution.py:29
  53.5 6.9 %collective-permute-start.4 = (bf16[128,256]{1,0:T(8,128)(2,1)S(1)}, bf16[128,256]{1,0:T(8,128)(2,1)S(1)}, u32[]{:S(2)}, u32[]{:S(2)}) collective-permute-start(bf16[128,256]{1,0:T(8,128)(2,1)S(1)} %get-tuple-element.10), channel_id=1, source_target_pairs={{0,192},{1,193},{2,194},{3,195},{4,196},{5,197},{6,198},{7,199},{8... | collective-permute-start | bytes 196616 | tf_op jit(solution)/shard_map/ppermute | solution.py:29

commit v5 on v4

--- a/solution.py
+++ b/solution.py
@@ -29,9 +29,9 @@
     return lax.ppermute(block, AXES, route)
 
 
-def exchanged(flat, rows):
-    pieces = lax.all_to_all(flat.reshape(COL, rows, HALF), ("pos", "core"), 0, 0, tiled=True)
-    return pieces.reshape(COL * rows, HALF)
+def exchanged(flat, rows, axes):
+    pieces = lax.all_to_all(flat.reshape(-1, rows, HALF), axes, 0, 0, tiled=True)
+    return pieces.reshape(-1, HALF)
 
 
 def dense_block(held, index):
@@ -62,33 +62,44 @@
         out[i * CHUNK : (i + 1) * CHUNK, :] = packed
 
 
-def shared_block(blocks, other, me, core, k):
+def shared_block(blocks, other, step, core, at):
     if core == 0:
-        return blocks[(1 + me) * SLOTS + k]
-    return other[k]
-
-
-def transposed_products(lists, held, blocks, other, partials, partials3):
+        return blocks[step * SLOTS + at % SLOTS]
+    return other[at]
+
+
+def transposed_products(lists, held, blocks, other, partials):
     me = lax.axis_index("core")
     for k in range(SLOTS):
         part = slice(NV * k, NV * (k + 1))
         for core, owner in enumerate((me, 1 - me)):
             left = dense_block(held, lists[owner, 0, 1 + me, k])
-            partials[core, part, :] = times(left, shared_block(blocks, other, me, core, k)).astype(BF16)
-        left = dense_block(held, lists[me, 0, 3, k])
-        partials3[part, :] = times(left, blocks[3 * SLOTS + k]).astype(BF16)
-
-
-def asked_blocks(far, far3, held, picked, picked3):
+            partials[core, part, :] = times(left, shared_block(blocks, other, 1 + me, core, k)).astype(BF16)
+
+
+def asked_blocks(lists, far, far3, held, blocks, other, picked, third):
     me = lax.axis_index("core")
     for k in range(SLOTS):
         part = slice(NV * k, NV * (k + 1))
         for core, owner in enumerate((me, 1 - me)):
             picked[core, part, :] = dense_block(held, far[owner, 1, 1 + me, k])
-        picked3[part, :] = dense_block(held, far3[me, 1, 3, k])
-
-
-def own_products(lists, far, far3, held, blocks, other, right, right3, back, back3, out, total):
+
+    @pl.when(me == 0)
+    def _():
+        for k in range(SLOTS):
+            for core in range(2):
+                third[core, NV * k : NV * (k + 1), :] = dense_block(held, far3[core, 1, 3, k])
+
+    @pl.when(me == 1)
+    def _():
+        for k in range(SLOTS):
+            for core in range(2):
+                left = dense_block(held, lists[1 - core, 0, 3, k])
+                product = times(left, shared_block(blocks, other, 3, core, SLOTS + k))
+                third[1 - core, NV * k : NV * (k + 1), :] = product.astype(BF16)
+
+
+def own_products(lists, far, far3, held, blocks, other, right, back, third, out, total):
     me = lax.axis_index("core")
     total[...] = jnp.zeros_like(total)
     for k in range(SLOTS):
@@ -97,22 +108,39 @@
         total[row] += times_transposed(dense_block(held, col), blocks[k])
         total[col] += times(dense_block(held, row), blocks[k])
         for core, owner in enumerate((me, 1 - me)):
-            block = shared_block(blocks, other, me, core, k)
+            block = shared_block(blocks, other, 1 + me, core, k)
             total[lists[owner, 0, 1 + me, k]] += times_transposed(right[core, part, :], block)
             total[far[owner, 1, 1 + me, k]] += back[core, part, :].astype(F32)
-        total[lists[me, 0, 3, k]] += times_transposed(right3[part, :], blocks[3 * SLOTS + k])
-        total[far3[me, 1, 3, k]] += back3[part, :].astype(F32)
+
+    @pl.when(me == 0)
+    def _():
+        for k in range(SLOTS):
+            for core in range(2):
+                came = third[core, NV * k : NV * (k + 1), :]
+                block = shared_block(blocks, other, 3, core, SLOTS + k)
+                total[lists[core, 0, 3, k]] += times_transposed(came, block)
+
+    @pl.when(me == 1)
+    def _():
+        for k in range(SLOTS):
+            for core in range(2):
+                total[far3[core, 1, 3, k]] += third[core, NV * k : NV * (k + 1), :].astype(F32)
+
     for row in range(NBB):
         whole = total[row]
         for q in range(4):
             part = whole[:, 64 * q : 64 * q + 64]
-            start = (row * 4 + q) * CHUNK
-            out[start : start + CHUNK, :] = jnp.concatenate([part[:32], part[32:]], axis=1).astype(BF16)
+            start = ((q % 2) * (COL // 2) + row * 2 + q // 2) * CHUNK
+            out[start : start + CHUNK, :] = jnp.concatenate([part[:32], part[32:]], axis=1)
+
+
+def both_cores(pair, out):
+    out[...] = (pair[: COL // 2 * CHUNK, :] + pair[COL // 2 * CHUNK :, :]).astype(BF16)
 
 
 def gathered_sum(arrived, out):
     sums = [arrived[i * CHUNK : (i + 1) * CHUNK, :].astype(F32) for i in range(4)]
-    for i in range(4, COL):
+    for i in range(4, COL // 2):
         sums[i % 4] += arrived[i * CHUNK : (i + 1) * CHUNK, :].astype(F32)
     packed = (sums[0] + sums[1]) + (sums[2] + sums[3])
     own = jnp.concatenate([packed[:, :64], packed[:, 64:]], axis=0)
@@ -135,6 +163,7 @@
     far3 = routed(lists, -3, -3)
     me = lax.axis_index("core")
     given = lax.dynamic_slice_in_dim(stored, (2 - me) * SLOTS, SLOTS, 0)
+    given = jnp.concatenate([given, stored[3 * SLOTS :]], axis=0)
     other = lax.ppermute(given, "core", [(0, 1), (1, 0)])
     mine = pl.pallas_call(
         prepared,
@@ -143,42 +172,47 @@
         out_specs=VM,
         compiler_params=PARAMS,
     )(vectors)
-    held = exchanged(mine, CHUNK)
-    one = shape_of((SLOTS * NV, BS), BF16)
+    held = exchanged(mine, CHUNK, ("pos", "core"))
     two = shape_of((2, SLOTS * NV, BS), BF16)
-    partials, partials3 = pl.pallas_call(
+    partials = pl.pallas_call(
         transposed_products,
-        out_shape=(two, one),
+        out_shape=two,
         in_specs=[SM] + [VM] * 3,
-        out_specs=(VM, VM),
+        out_specs=VM,
         compiler_params=PARAMS,
     )(lists, held, stored, other)
     back = routed(partials, -1, -2)
-    back3 = routed(partials3, -3, -3)
-    picked, picked3 = pl.pallas_call(
+    picked, third = pl.pallas_call(
         asked_blocks,
-        out_shape=(two, one),
-        in_specs=[SM, SM, VM],
+        out_shape=(two, two),
+        in_specs=[SM] * 3 + [VM] * 3,
         out_specs=(VM, VM),
         compiler_params=PARAMS,
-    )(far, far3, held)
+    )(lists, far, far3, held, stored, other)
     right = routed(picked, 1, 2)
-    right3 = routed(picked3, 3, 3)
+    third = routed(third, 3, -3)
     sums = pl.pallas_call(
         own_products,
-        out_shape=shape_of((COL * CHUNK, HALF), BF16),
-        in_specs=[SM] * 3 + [VM] * 7,
+        out_shape=shape_of((COL * CHUNK, HALF), F32),
+        in_specs=[SM] * 3 + [VM] * 6,
         out_specs=VM,
         scratch_shapes=[pltpu.VMEM((NBB, NV, BS), F32)],
         compiler_params=PARAMS,
-    )(lists, far, far3, held, stored, other, right, right3, back, back3)
+    )(lists, far, far3, held, stored, other, right, back, third)
+    chips = pl.pallas_call(
+        both_cores,
+        out_shape=shape_of((COL // 2 * CHUNK, HALF), BF16),
+        in_specs=[VM],
+        out_specs=VM,
+        compiler_params=PARAMS,
+    )(exchanged(sums, COL // 2 * CHUNK, "core"))
     return pl.pallas_call(
         gathered_sum,
         out_shape=shape_of((64, NV), F32),
         in_specs=[VM],
         out_specs=VM,
         compiler_params=PARAMS,
-    )(exchanged(sums, CHUNK))
+    )(exchanged(chips, CHUNK, "pos"))
 
 
 def solution(mesh):

time: 92.8 us -> 91.5 us (0.986)
  blocking collectives: 28.6 us -> 26.2 us
  starting transfers between devices: 48.9 us -> 46.9 us
  waiting for transfers between devices: 7.55 us -> 9.52 us
    all_to_all x1 -> x2, blocking collectives: 26.8 us -> 24.4 us  [exchanged(): lax.all_to_all(flat.reshape(-1, rows, HALF), axes, 0, 0, tiled=True)]
    ppermute x6 -> x5, starting transfers between devices: 31.8 us -> 29.8 us  [routed(): return lax.ppermute(block, AXES, route)]
    ppermute x6 -> x5, waiting for transfers between devices: 7.55 us -> 9.52 us  [routed(): return lax.ppermute(block, AXES, route)]
    pallas_call x3 -> x4, Pallas kernels: 3.6 us -> 4.02 us  [the longest x1 1.75 us: per_device(): pl.pallas_call(own_products, out_shape=shape_of((COL * CHUNK, HALF), F32)...]
  transfers between devices with their start and end apart: 8 -> 7, of which waited for: 2 -> 1; matrix products, arithmetic and copies ran while one was open for 0% -> 0% of each run, Pallas kernels for 2% -> 2%
where the time goes in v5:
time: 91.5 us; the launch traced here: 90.4 us
  starting transfers between devices  46.9 us (51%)
  blocking collectives  26.2 us (29%)
  waiting for transfers between devices  9.52 us (10%)
  Pallas kernels  5.94 us (6%)
  local copies, waits for them, and re-layouts  1.67 us (2%)
    ppermute x5, starting transfers between devices, routed(): return lax.ppermute(block, AXES, route)  29.8 us
    all_to_all x2, blocking collectives, exchanged(): lax.all_to_all(flat.reshape(-1, rows, HALF), axes, 0, 0, tiled=True)  24.4 us
    all_to_all x1, starting transfers between devices, exchanged(): lax.all_to_all(flat.reshape(-1, rows, HALF), axes, 0, 0, tiled=True)  14.6 us
    ppermute x5, waiting for transfers between devices, routed(): return lax.ppermute(block, AXES, route)  9.52 us
    ppermute x1, starting transfers between devices, per_device(): other = lax.ppermute(given, 'core', [(0, 1), (1, 0)])  2.47 us
  transfers between devices with their start and end apart: 7, of which 1 were waited for; matrix products, arithmetic and copies ran while one was open for 0% of the time, Pallas kernels for 2%

profile of v5, /device:TPU:1, one launch (start us, length us, event | category | flops | bytes accessed | tf_op | source)
XLA Modules:
  0.0 90.4 jit_solution(6173023400396959926)
XLA Ops:
  0.0 0.8 copy-done.1
  0.8 1.1 %shard_map.46 = bf16[2048,128]{1,0:T(8,128)(2,1)} custom-call(f32[64,64]{1,0:T(8,128)S(1)} %copy-done.1), custom_call_target="tpu_custom_call" | custom-call | tf_op jit(solution)/shard_map/pallas_call | solution.py:168
  1.9 14.6 %all-to-all-start = ((bf16[64,32,128]{2,1,0:T(8,128)(2,1)}), bf16[64,32,128]{2,1,0:T(8,128)(2,1)S(1)}, u32[]{:S(2)}, u32[]{:S(2)}) async-start(bf16[64,32,128]{2,1,0:T(8,128)(2,1)} %bitcast.3), calls=%async_computation | async-start | bytes 1048576 | tf_op jit(solution)/shard_map/all_to_all | solution.py:33
  16.6 0.0 copy-start.3
  16.6 2.5 %collective-permute-start.2 = (bf16[4,256,256]{2,1,0:T(8,128)(2,1)S(1)}, bf16[4,256,256]{2,1,0:T(8,128)(2,1)S(1)}, u32[]{:S(2)}, u32[]{:S(2)}) collective-permute-start(bf16[4,256,256]{2,1,0:T(8,128)(2,1)S(1)} %pad_maximum_fusion), channel_id=1, source_target_pairs={{0,1},{1,0},{2,3},{3,2},{4,5},{5,4},{6,7},{7,6},{8,9},{9,8},{10,11... | collective-permute-start | bytes 1572872 | tf_op jit(solution)/shard_map/ppermute | solution.py:167
  19.1 0.0 copy-start.2
  19.1 0.7 copy-done.2
  19.8 1.8 %all-gather = s32[4,4,2]{1,2,0:T(2,128)S(1)} all-gather(s32[2,4,2]{1,2,0:T(2,128)S(1)} %pad_add_fusion), channel_id=2, replica_groups=mesh['blk'=12,'pos'=32,'core'=2] {'core'}, dimensions={0}, use_global_device_ids=true | all-gather | bytes 192 | tf_op jit(solution)/shard_map/all_gather | solution.py:161
  21.6 0.1 copy.14.lists
  21.7 4.3 %collective-permute-start.1 = (s32[2,2,4,2]{3,2,1,0:T(4,128)S(1)}, s32[2,2,4,2]{3,2,1,0:T(4,128)S(1)}, u32[]{:S(2)}, u32[]{:S(2)}) collective-permute-start(s32[2,2,4,2]{3,2,1,0:T(4,128)S(1)} %copy.14.lists), channel_id=1, source_target_pairs={{0,576},{1,577},{2,578},{3,579},{4,580},{5,581},{6,582},{7,583},{8... | collective-permute-start | bytes 392 | tf_op jit(solution)/shard_map/ppermute | solution.py:29
  26.0 10.6 %collective-permute-start = (s32[2,2,4,2]{3,2,1,0:T(4,128)S(1)}, s32[2,2,4,2]{3,2,1,0:T(4,128)S(1)}, u32[]{:S(2)}, u32[]{:S(2)}) collective-permute-start(s32[2,2,4,2]{3,2,1,0:T(4,128)S(1)} %copy.14.lists), channel_id=1, source_target_pairs={{0,704},{1,641},{2,706},{3,643},{4,708},{5,645},{6,710},{7,647},{8... | collective-permute-start | bytes 392 | tf_op jit(solution)/shard_map/ppermute | solution.py:29
  36.6 0.9 %shard_map.48 = bf16[2,128,256]{2,1,0:T(8,128)(2,1)S(1)} custom-call(s32[2,2,4,2]{3,2,1,0:T(4,128)S(1)} %copy.14.lists, bf16[2048,128]{1,0:T(8,128)(2,1)S(1)} %bitcast.16, bf16[8,256,256]{2,1,0:T(8,128)(2,1)S(1)} %bitcast.13, bf16[4,256,256]{2,1,0:T(8,128)(2,1)S(1)} %collective-permute-done.2.other), custom_call_target="tpu_custom_call" | custom-call | tf_op jit(solution)/shard_map/pallas_call | solution.py:177
  37.5 9.6 %collective-permute-start.4 = (bf16[2,128,256]{2,1,0:T(8,128)(2,1)S(1)}, bf16[2,128,256]{2,1,0:T(8,128)(2,1)S(1)}, u32[]{:S(2)}, u32[]{:S(2)}) collective-permute-start(bf16[2,128,256]{2,1,0:T(8,128)(2,1)S(1)} %shard_map.48), channel_id=1, source_target_pairs={{0,704},{1,641},{2,706},{3,643},{4,708},{5,645},{6,710},{7,647},{8... | collective-permute-start | bytes 393224 | tf_op jit(solution)/shard_map/ppermute | solution.py:29
  47.1 0.0 collective-permute-done.1.far3
  47.1 0.0 collective-permute-done.far
  47.1 1.3 %shard_map.47 = (bf16[2,128,256]{2,1,0:T(8,128)(2,1)S(1)}, bf16[2,128,256]{2,1,0:T(8,128)(2,1)S(1)}) custom-call(s32[2,2,4,2]{3,2,1,0:T(4,128)S(1)} %copy.14.lists, s32[2,2,4,2]{3,2,1,0:T(4,128)S(1)} %collective-permute-done.far, s32[2,2,4,2]{3,2,1,0:T(4,128)S(1)} %collective-permute-done.1.far3, bf16[2048,128]{1,0:T(8,128)(2,1)S(1)} %bitcast.17, ...), custom_call_target="tpu_custom_call" | custom-call | tf_op jit(solution)/shard_map/pallas_call | solution.py:185
  48.5 1.9 %collective-permute-start.3 = (bf16[2,128,256]{2,1,0:T(8,128)(2,1)S(1)}, bf16[2,128,256]{2,1,0:T(8,128)(2,1)S(1)}, u32[]{:S(2)}, u32[]{:S(2)}) collective-permute-start(bf16[2,128,256]{2,1,0:T(8,128)(2,1)S(1)} %get-tuple-element.7), channel_id=1, source_target_pairs={{0,64},{1,129},{2,66},{3,131},{4,68},{5,133},{6,70},{7,135},{8,72}... | collective-permute-start | bytes 393224 | tf_op jit(solution)/shard_map/ppermute | solution.py:29
  50.4 3.4 %collective-permute-start.5 = (bf16[2,128,256]{2,1,0:T(8,128)(2,1)S(1)}, bf16[2,128,256]{2,1,0:T(8,128)(2,1)S(1)}, u32[]{:S(2)}, u32[]{:S(2)}) collective-permute-start(bf16[2,128,256]{2,1,0:T(8,128)(2,1)S(1)} %get-tuple-element.8), channel_id=1, source_target_pairs={{0,192},{1,577},{2,194},{3,579},{4,196},{5,581},{6,198},{7,583},{8... | collective-permute-start | bytes 393224 | tf_op jit(solution)/shard_map/ppermute | solution.py:29
  53.8 0.0 collective-permute-done.4.back
  53.8 9.5 %collective-permute-done.3.right = bf16[2,128,256]{2,1,0:T(8,128)(2,1)S(1)} collective-permute-done((bf16[2,128,256]{2,1,0:T(8,128)(2,1)S(1)}, bf16[2,128,256]{2,1,0:T(8,128)(2,1)S(1)}, u32[]{:S(2)}, u32[]{:S(2)}) %collective-permute-start.3) | collective-permute-done | bytes 131104 | tf_op jit(solution)/shard_map/ppermute | solution.py:29
  63.3 1.7 %shard_map.49 = f32[2048,128]{1,0:T(8,128)S(1)} custom-call(s32[2,2,4,2]{3,2,1,0:T(4,128)S(1)} %copy.14.lists, s32[2,2,4,2]{3,2,1,0:T(4,128)S(1)} %collective-permute-done.far, s32[2,2,4,2]{3,2,1,0:T(4,128)S(1)} %collective-permute-done.1.far3, bf16[2048,128]{1,0:T(8,128)(2,1)S(1)} %bitcast.18, bf16[8,256,256]{2,1,0:T(8,128)(2,1)S(1)} %bitcast.15, ...), custom_call_target="tpu_custom_call" | custom-call | tf_op jit(solution)/shard_map/pallas_call | solution.py:194
  65.1 5.7 %all_to_all.15 = f32[2,1024,128]{2,1,0:T(8,128)S(1)} all-to-all(f32[2,1024,128]{2,1,0:T(8,128)S(1)} %bitcast.19), channel_id=1, replica_groups=mesh['blk'=12,'pos'=32,'core'=2] {'core'}, dimensions={0} | all-to-all | bytes 2097152 | tf_op jit(solution)/shard_map/all_to_all | solution.py:33
  70.9 18.7 %all_to_all.16 = bf16[32,32,128]{2,1,0:T(8,128)(2,1)S(1)} all-to-all(bf16[32,32,128]{2,1,0:T(8,128)(2,1)S(1)} %bitcast.21), channel_id=1, replica_groups=mesh['blk'=12,'pos'=32,'core'=2] {'pos'}, dimensions={0} | all-to-all | bytes 524288 | tf_op jit(solution)/shard_map/all_to_all | solution.py:33
  89.6 0.9 shard_map.51
  (12 shorter events, 0.2 us)
Async XLA Ops:
  0.0 16.5 %copy-start = (bf16[1,1,4,2,256,256]{5,4,3,2,1,0:T(8,128)(2,1)S(1)}, bf16[1,1,4,2,256,256]{5,4,3,2,1,0:T(8,128)(2,1)}, u32[]{:S(2)}) copy-start(bf16[1,1,4,2,256,256]{5,4,3,2,1,0:T(8,128)(2,1)} %param.5) | copy-start | bytes 3145732
  0.0 0.8 copy-start.1
  1.9 34.7 %all-to-all-start = ((bf16[64,32,128]{2,1,0:T(8,128)(2,1)}), bf16[64,32,128]{2,1,0:T(8,128)(2,1)S(1)}, u32[]{:S(2)}, u32[]{:S(2)}) async-start(bf16[64,32,128]{2,1,0:T(8,128)(2,1)} %bitcast.3), calls=%async_computation | async-start | bytes 1048576 | tf_op jit(solution)/shard_map/all_to_all | solution.py:33
  16.6 2.6 %copy-start.3 = (s32[1,1,4,2]{2,3,1,0:T(2,128)S(1)}, s32[1,1,4,2]{2,3,1,0:T(2,128)}, u32[]{:S(2)}) copy-start(s32[1,1,4,2]{2,3,1,0:T(2,128)} %param.6) | copy-start | bytes 100
  16.6 19.9 %collective-permute-start.2 = (bf16[4,256,256]{2,1,0:T(8,128)(2,1)S(1)}, bf16[4,256,256]{2,1,0:T(8,128)(2,1)S(1)}, u32[]{:S(2)}, u32[]{:S(2)}) collective-permute-start(bf16[4,256,256]{2,1,0:T(8,128)(2,1)S(1)} %pad_maximum_fusion), channel_id=1, source_target_pairs={{0,1},{1,0},{2,3},{3,2},{4,5},{5,4},{6,7},{7,6},{8,9},{9,8},{10,11... | collective-permute-start | bytes 1572872 | tf_op jit(solution)/shard_map/ppermute | solution.py:167
  19.1 0.7 copy-start.2
  21.7 25.4 %collective-permute-start.1 = (s32[2,2,4,2]{3,2,1,0:T(4,128)S(1)}, s32[2,2,4,2]{3,2,1,0:T(4,128)S(1)}, u32[]{:S(2)}, u32[]{:S(2)}) collective-permute-start(s32[2,2,4,2]{3,2,1,0:T(4,128)S(1)} %copy.14.lists), channel_id=1, source_target_pairs={{0,576},{1,577},{2,578},{3,579},{4,580},{5,581},{6,582},{7,583},{8... | collective-permute-start | bytes 392 | tf_op jit(solution)/shard_map/ppermute | solution.py:29
  26.0 21.2 %collective-permute-start = (s32[2,2,4,2]{3,2,1,0:T(4,128)S(1)}, s32[2,2,4,2]{3,2,1,0:T(4,128)S(1)}, u32[]{:S(2)}, u32[]{:S(2)}) collective-permute-start(s32[2,2,4,2]{3,2,1,0:T(4,128)S(1)} %copy.14.lists), channel_id=1, source_target_pairs={{0,704},{1,641},{2,706},{3,643},{4,708},{5,645},{6,710},{7,647},{8... | collective-permute-start | bytes 392 | tf_op jit(solution)/shard_map/ppermute | solution.py:29
  37.5 16.3 %collective-permute-start.4 = (bf16[2,128,256]{2,1,0:T(8,128)(2,1)S(1)}, bf16[2,128,256]{2,1,0:T(8,128)(2,1)S(1)}, u32[]{:S(2)}, u32[]{:S(2)}) collective-permute-start(bf16[2,128,256]{2,1,0:T(8,128)(2,1)S(1)} %shard_map.48), channel_id=1, source_target_pairs={{0,704},{1,641},{2,706},{3,643},{4,708},{5,645},{6,710},{7,647},{8... | collective-permute-start | bytes 393224 | tf_op jit(solution)/shard_map/ppermute | solution.py:29
  48.5 14.9 %collective-permute-start.3 = (bf16[2,128,256]{2,1,0:T(8,128)(2,1)S(1)}, bf16[2,128,256]{2,1,0:T(8,128)(2,1)S(1)}, u32[]{:S(2)}, u32[]{:S(2)}) collective-permute-start(bf16[2,128,256]{2,1,0:T(8,128)(2,1)S(1)} %get-tuple-element.7), channel_id=1, source_target_pairs={{0,64},{1,129},{2,66},{3,131},{4,68},{5,133},{6,70},{7,135},{8,72}... | collective-permute-start | bytes 393224 | tf_op jit(solution)/shard_map/ppermute | solution.py:29
  50.4 13.0 %collective-permute-start.5 = (bf16[2,128,256]{2,1,0:T(8,128)(2,1)S(1)}, bf16[2,128,256]{2,1,0:T(8,128)(2,1)S(1)}, u32[]{:S(2)}, u32[]{:S(2)}) collective-permute-start(bf16[2,128,256]{2,1,0:T(8,128)(2,1)S(1)} %get-tuple-element.8), channel_id=1, source_target_pairs={{0,192},{1,577},{2,194},{3,579},{4,196},{5,581},{6,198},{7,583},{8... | collective-permute-start | bytes 393224 | tf_op jit(solution)/shard_map/ppermute | solution.py:29

commit v6 on v5

--- a/solution.py
+++ b/solution.py
@@ -37,7 +37,8 @@
 def dense_block(held, index):
     tops, bottoms = [], []
     for quarter in range(4):
-        start = pl.multiple_of((index * 4 + quarter) * CHUNK, CHUNK)
+        place = (quarter % 2) * (COL // 2) + index * 2 + quarter // 2
+        start = pl.multiple_of(place * CHUNK, CHUNK)
         piece = held[pl.ds(start, CHUNK), :]
         tops.append(piece[:, :64])
         bottoms.append(piece[:, 64:])
@@ -58,7 +59,7 @@
     rows = vectors[...]
     turned = jnp.transpose(jnp.concatenate([rows, rows], axis=1))
     packed = jnp.concatenate([turned[:32], turned[32:64]], axis=1).astype(BF16)
-    for i in range(COL):
+    for i in range(COL // 2):
         out[i * CHUNK : (i + 1) * CHUNK, :] = packed
 
 
@@ -99,7 +100,7 @@
                 third[1 - core, NV * k : NV * (k + 1), :] = product.astype(BF16)
 
 
-def own_products(lists, far, far3, held, blocks, other, right, back, third, out, total):
+def early_sums(lists, far, held, blocks, back, total):
     me = lax.axis_index("core")
     total[...] = jnp.zeros_like(total)
     for k in range(SLOTS):
@@ -108,34 +109,52 @@
         total[row] += times_transposed(dense_block(held, col), blocks[k])
         total[col] += times(dense_block(held, row), blocks[k])
         for core, owner in enumerate((me, 1 - me)):
-            block = shared_block(blocks, other, 1 + me, core, k)
-            total[lists[owner, 0, 1 + me, k]] += times_transposed(right[core, part, :], block)
             total[far[owner, 1, 1 + me, k]] += back[core, part, :].astype(F32)
 
-    @pl.when(me == 0)
-    def _():
-        for k in range(SLOTS):
-            for core in range(2):
-                came = third[core, NV * k : NV * (k + 1), :]
-                block = shared_block(blocks, other, 3, core, SLOTS + k)
-                total[lists[core, 0, 3, k]] += times_transposed(came, block)
-
-    @pl.when(me == 1)
-    def _():
-        for k in range(SLOTS):
-            for core in range(2):
-                total[far3[core, 1, 3, k]] += third[core, NV * k : NV * (k + 1), :].astype(F32)
-
+
+def packed_rows(total, *outs):
     for row in range(NBB):
         whole = total[row]
         for q in range(4):
             part = whole[:, 64 * q : 64 * q + 64]
-            start = ((q % 2) * (COL // 2) + row * 2 + q // 2) * CHUNK
-            out[start : start + CHUNK, :] = jnp.concatenate([part[:32], part[32:]], axis=1)
-
-
-def both_cores(pair, out):
-    out[...] = (pair[: COL // 2 * CHUNK, :] + pair[COL // 2 * CHUNK :, :]).astype(BF16)
+            start = (row * 2 + q // 2) * CHUNK
+            outs[q % 2][start : start + CHUNK, :] = jnp.concatenate([part[:32], part[32:]], axis=1)
+
+
+def late_sums(lists, far3, early, blocks, other, right, third, kept, given, total):
+    me = lax.axis_index("core")
+    total[...] = early[...]
+    for k in range(SLOTS):
+        part = slice(NV * k, NV * (k + 1))
+        for core, owner in enumerate((me, 1 - me)):
+            block = shared_block(blocks, other, 1 + me, core, k)
+            total[lists[owner, 0, 1 + me, k]] += times_transposed(right[core, part, :], block)
+
+    @pl.when(me == 0)
+    def _():
+        for k in range(SLOTS):
+            for core in range(2):
+                came = third[core, NV * k : NV * (k + 1), :]
+                block = shared_block(blocks, other, 3, core, SLOTS + k)
+                total[lists[core, 0, 3, k]] += times_transposed(came, block)
+
+    @pl.when(me == 1)
+    def _():
+        for k in range(SLOTS):
+            for core in range(2):
+                total[far3[core, 1, 3, k]] += third[core, NV * k : NV * (k + 1), :].astype(F32)
+
+    @pl.when(me == 0)
+    def _():
+        packed_rows(total, kept, given)
+
+    @pl.when(me == 1)
+    def _():
+        packed_rows(total, given, kept)
+
+
+def both_cores(kept, got, out):
+    out[...] = (kept[...] + got[...]).astype(BF16)
 
 
 def gathered_sum(arrived, out):
@@ -167,12 +186,12 @@
     other = lax.ppermute(given, "core", [(0, 1), (1, 0)])
     mine = pl.pallas_call(
         prepared,
-        out_shape=shape_of((COL * CHUNK, HALF), BF16),
+        out_shape=shape_of((COL // 2 * CHUNK, HALF), BF16),
         in_specs=[VM],
         out_specs=VM,
         compiler_params=PARAMS,
     )(vectors)
-    held = exchanged(mine, CHUNK, ("pos", "core"))
+    held = lax.all_gather(exchanged(mine, CHUNK, "pos"), "core", tiled=True)
     two = shape_of((2, SLOTS * NV, BS), BF16)
     partials = pl.pallas_call(
         transposed_products,
@@ -191,21 +210,29 @@
     )(lists, far, far3, held, stored, other)
     right = routed(picked, 1, 2)
     third = routed(third, 3, -3)
-    sums = pl.pallas_call(
-        own_products,
-        out_shape=shape_of((COL * CHUNK, HALF), F32),
-        in_specs=[SM] * 3 + [VM] * 6,
-        out_specs=VM,
+    early = pl.pallas_call(
+        early_sums,
+        out_shape=shape_of((NBB, NV, BS), F32),
+        in_specs=[SM] * 2 + [VM] * 3,
+        out_specs=VM,
+        compiler_params=PARAMS,
+    )(lists, far, held, stored, back)
+    half = shape_of((COL // 2 * CHUNK, HALF), F32)
+    kept, given = pl.pallas_call(
+        late_sums,
+        out_shape=(half, half),
+        in_specs=[SM] * 2 + [VM] * 5,
+        out_specs=(VM, VM),
         scratch_shapes=[pltpu.VMEM((NBB, NV, BS), F32)],
         compiler_params=PARAMS,
-    )(lists, far, far3, held, stored, other, right, back, third)
+    )(lists, far3, early, stored, other, right, third)
     chips = pl.pallas_call(
         both_cores,
         out_shape=shape_of((COL // 2 * CHUNK, HALF), BF16),
-        in_specs=[VM],
-        out_specs=VM,
-        compiler_params=PARAMS,
-    )(exchanged(sums, COL // 2 * CHUNK, "core"))
+        in_specs=[VM, VM],
+        out_specs=VM,
+        compiler_params=PARAMS,
+    )(kept, lax.ppermute(given, "core", [(0, 1), (1, 0)]))
     return pl.pallas_call(
         gathered_sum,
         out_shape=shape_of((64, NV), F32),

time: 91.5 us -> 91.3 us (level)
  waiting for transfers between devices: 9.52 us -> 7.12 us
  blocking collectives: 26.2 us -> 27.3 us
  local copies, waits for them, and re-layouts: 1.67 us -> 2.62 us
    ppermute x5, waiting for transfers between devices: 9.52 us -> 5.6 us  [routed(): return lax.ppermute(block, AXES, route)]
    all_gather x0 -> x1, blocking collectives: none -> 3.81 us  [per_device(): held = lax.all_gather(exchanged(mine, CHUNK, 'pos'), 'core', tiled=True)]
    ppermute x0 -> x1, starting transfers between devices: none -> 3.67 us  [per_device(): lax.ppermute(given, 'core', [(0, 1), (1, 0)])]
    ppermute x5, starting transfers between devices: 29.8 us -> 26.3 us  [routed(): return lax.ppermute(block, AXES, route)]
    all_to_all x2 -> x1, blocking collectives: 24.4 us -> 21.7 us  [exchanged(): lax.all_to_all(flat.reshape(-1, rows, HALF), axes, 0, 0, tiled=True)]
    ppermute x0 -> x1, waiting for transfers between devices: none -> 1.51 us  [per_device(): lax.ppermute(given, 'core', [(0, 1), (1, 0)])]
    all_to_all x1, starting transfers between devices: 14.6 us -> 13.5 us  [exchanged(): lax.all_to_all(flat.reshape(-1, rows, HALF), axes, 0, 0, tiled=True)]
    dynamic_slice x1, local copies, waits for them, and re-layouts: 0.02 us -> 0.97 us  [per_device(): given = lax.dynamic_slice_in_dim(stored, (2 - me) * SLOTS, SLOTS, 0)]
  transfers between devices with their start and end apart: 7 -> 8, of which waited for: 1 -> 2; matrix products, arithmetic and copies ran while one was open for 0% -> 1% of each run, Pallas kernels for 2% -> 4%
where the time goes in v6:
time: 91.3 us; the launch traced here: 90.2 us
  starting transfers between devices  46.3 us (51%)
  blocking collectives  27.3 us (30%)
  waiting for transfers between devices  7.12 us (8%)
  Pallas kernels  6.63 us (7%)
  local copies, waits for them, and re-layouts  2.62 us (3%)
    ppermute x5, starting transfers between devices, routed(): return lax.ppermute(block, AXES, route)  26.3 us
    all_to_all x1, blocking collectives, exchanged(): lax.all_to_all(flat.reshape(-1, rows, HALF), axes, 0, 0, tiled=True)  21.7 us
    all_to_all x1, starting transfers between devices, exchanged(): lax.all_to_all(flat.reshape(-1, rows, HALF), axes, 0, 0, tiled=True)  13.5 us
    ppermute x5, waiting for transfers between devices, routed(): return lax.ppermute(block, AXES, route)  5.6 us
    all_gather x1, blocking collectives, per_device(): held = lax.all_gather(exchanged(mine, CHUNK, 'pos'), 'core', tiled=True)  3.81 us
    ppermute x1, starting transfers between devices, per_device(): lax.ppermute(given, 'core', [(0, 1), (1, 0)])  3.67 us
    ppermute x1, starting transfers between devices, per_device(): other = lax.ppermute(given, 'core', [(0, 1), (1, 0)])  2.86 us
  transfers between devices with their start and end apart: 8, of which 2 were waited for; matrix products, arithmetic and copies ran while one was open for 1% of the time, Pallas kernels for 4%

profile of v6, /device:TPU:1, one launch (start us, length us, event | category | flops | bytes accessed | tf_op | source)
XLA Modules:
  0.0 90.2 jit_solution(13277902466723380921)
XLA Ops:
  0.0 0.8 copy-done.1
  0.8 0.9 %shard_map.46 = bf16[1024,128]{1,0:T(8,128)(2,1)} custom-call(f32[64,64]{1,0:T(8,128)S(1)} %copy-done.1), custom_call_target="tpu_custom_call" | custom-call | tf_op jit(solution)/shard_map/pallas_call | solution.py:187
  1.8 13.5 %all-to-all-start = ((bf16[32,32,128]{2,1,0:T(8,128)(2,1)}), bf16[32,32,128]{2,1,0:T(8,128)(2,1)S(1)}, u32[]{:S(2)}, u32[]{:S(2)}) async-start(bf16[32,32,128]{2,1,0:T(8,128)(2,1)} %bitcast.3), calls=%async_computation | async-start | bytes 524288 | tf_op jit(solution)/shard_map/all_to_all | solution.py:33
  15.3 1.0 %constant_dynamic-slice_fusion = bf16[2,256,256]{2,1,0:T(8,128)(2,1)S(1)} fusion(bf16[8,256,256]{2,1,0:T(8,128)(2,1)} %bitcast.10, s32[]{:T(128)S(6)} %select_n.3), kind=kLoop, calls=%fused_computation.3 | loop fusion | bytes 524292 | tf_op jit(solution)/shard_map/dynamic_slice | solution.py:184
  16.3 2.9 %collective-permute-start.2 = (bf16[4,256,256]{2,1,0:T(8,128)(2,1)S(1)}, bf16[4,256,256]{2,1,0:T(8,128)(2,1)S(1)}, u32[]{:S(2)}, u32[]{:S(2)}) collective-permute-start(bf16[4,256,256]{2,1,0:T(8,128)(2,1)S(1)} %pad_maximum_fusion), channel_id=1, source_target_pairs={{0,1},{1,0},{2,3},{3,2},{4,5},{5,4},{6,7},{7,6},{8,9},{9,8},{10,11... | collective-permute-start | bytes 1572872 | tf_op jit(solution)/shard_map/ppermute | solution.py:186
  19.2 0.0 copy-start.2
  19.2 0.7 copy-done.2
  19.9 1.8 %all-gather = s32[4,4,2]{1,2,0:T(2,128)S(1)} all-gather(s32[2,4,2]{1,2,0:T(2,128)S(1)} %pad_add_fusion), channel_id=2, replica_groups=mesh['blk'=12,'pos'=32,'core'=2] {'core'}, dimensions={0}, use_global_device_ids=true | all-gather | bytes 192 | tf_op jit(solution)/shard_map/all_gather | solution.py:180
  21.7 0.1 copy.16.lists
  21.8 12.5 %collective-permute-start.1 = (s32[2,2,4,2]{3,2,1,0:T(4,128)S(1)}, s32[2,2,4,2]{3,2,1,0:T(4,128)S(1)}, u32[]{:S(2)}, u32[]{:S(2)}) collective-permute-start(s32[2,2,4,2]{3,2,1,0:T(4,128)S(1)} %copy.16.lists), channel_id=1, source_target_pairs={{0,704},{1,641},{2,706},{3,643},{4,708},{5,645},{6,710},{7,647},{8... | collective-permute-start | bytes 392 | tf_op jit(solution)/shard_map/ppermute | solution.py:29
  34.3 2.5 %collective-permute-start = (s32[2,2,4,2]{3,2,1,0:T(4,128)S(1)}, s32[2,2,4,2]{3,2,1,0:T(4,128)S(1)}, u32[]{:S(2)}, u32[]{:S(2)}) collective-permute-start(s32[2,2,4,2]{3,2,1,0:T(4,128)S(1)} %copy.16.lists), channel_id=1, source_target_pairs={{0,576},{1,577},{2,578},{3,579},{4,580},{5,581},{6,582},{7,583},{8... | collective-permute-start | bytes 392 | tf_op jit(solution)/shard_map/ppermute | solution.py:29
  36.8 3.8 %all_gather.11.held = bf16[2048,128]{1,0:T(8,128)(2,1)S(1)} all-gather(bf16[1024,128]{1,0:T(8,128)(2,1)S(1)} %bitcast.17), channel_id=1, replica_groups=mesh['blk'=12,'pos'=32,'core'=2] {'core'}, dimensions={0}, use_global_device_ids=true | all-gather | bytes 786432 | tf_op jit(solution)/shard_map/all_gather | solution.py:194
  40.6 0.9 %shard_map.47 = bf16[2,128,256]{2,1,0:T(8,128)(2,1)S(1)} custom-call(s32[2,2,4,2]{3,2,1,0:T(4,128)S(1)} %copy.16.lists, bf16[2048,128]{1,0:T(8,128)(2,1)S(1)} %all_gather.11.held, bf16[8,256,256]{2,1,0:T(8,128)(2,1)S(1)} %bitcast.11, bf16[4,256,256]{2,1,0:T(8,128)(2,1)S(1)} %collective-permute-done.2.other), custom_call_target="tpu_custom_call" | custom-call | tf_op jit(solution)/shard_map/pallas_call | solution.py:196
  41.5 4.2 %collective-permute-start.3 = (bf16[2,128,256]{2,1,0:T(8,128)(2,1)S(1)}, bf16[2,128,256]{2,1,0:T(8,128)(2,1)S(1)}, u32[]{:S(2)}, u32[]{:S(2)}) collective-permute-start(bf16[2,128,256]{2,1,0:T(8,128)(2,1)S(1)} %shard_map.47), channel_id=1, source_target_pairs={{0,704},{1,641},{2,706},{3,643},{4,708},{5,645},{6,710},{7,647},{8... | collective-permute-start | bytes 393224 | tf_op jit(solution)/shard_map/ppermute | solution.py:29
  45.7 1.3 %shard_map.49 = (bf16[2,128,256]{2,1,0:T(8,128)(2,1)S(1)}, bf16[2,128,256]{2,1,0:T(8,128)(2,1)S(1)}) custom-call(s32[2,2,4,2]{3,2,1,0:T(4,128)S(1)} %copy.16.lists, s32[2,2,4,2]{3,2,1,0:T(4,128)S(1)} %collective-permute-done.1.far, s32[2,2,4,2]{3,2,1,0:T(4,128)S(1)} %collective-permute-done.far3, bf16[2048,128]{1,0:T(8,128)(2,1)S(1)} %all_gather.11.held, ...), custom_call_target="tpu_custom_call" | custom-call | tf_op jit(solution)/shard_map/pallas_call | solution.py:204
  47.0 5.0 %collective-permute-start.4 = (bf16[2,128,256]{2,1,0:T(8,128)(2,1)S(1)}, bf16[2,128,256]{2,1,0:T(8,128)(2,1)S(1)}, u32[]{:S(2)}, u32[]{:S(2)}) collective-permute-start(bf16[2,128,256]{2,1,0:T(8,128)(2,1)S(1)} %get-tuple-element.9), channel_id=1, source_target_pairs={{0,64},{1,129},{2,66},{3,131},{4,68},{5,133},{6,70},{7,135},{8,72}... | collective-permute-start | bytes 393224 | tf_op jit(solution)/shard_map/ppermute | solution.py:29
  52.1 2.2 %collective-permute-start.5 = (bf16[2,128,256]{2,1,0:T(8,128)(2,1)S(1)}, bf16[2,128,256]{2,1,0:T(8,128)(2,1)S(1)}, u32[]{:S(2)}, u32[]{:S(2)}) collective-permute-start(bf16[2,128,256]{2,1,0:T(8,128)(2,1)S(1)} %get-tuple-element.10), channel_id=1, source_target_pairs={{0,192},{1,577},{2,194},{3,579},{4,196},{5,581},{6,198},{7,583},{8... | collective-permute-start | bytes 393224 | tf_op jit(solution)/shard_map/ppermute | solution.py:29
  54.3 1.1 %shard_map.48.early = f32[16,64,256]{2,1,0:T(8,128)S(1)} custom-call(s32[2,2,4,2]{3,2,1,0:T(4,128)S(1)} %copy.16.lists, s32[2,2,4,2]{3,2,1,0:T(4,128)S(1)} %collective-permute-done.1.far, bf16[2048,128]{1,0:T(8,128)(2,1)S(1)} %all_gather.11.held, bf16[8,256,256]{2,1,0:T(8,128)(2,1)S(1)} %bitcast.13, bf16[2,128,256]{2,1,0:T(8,128)(2,1)S(1)} %collective-permute-done.3.back), custom_call_target="tpu_custom_call" | custom-call | tf_op jit(solution)/shard_map/pallas_call | solution.py:213
  55.4 5.6 %collective-permute-done.4.right = bf16[2,128,256]{2,1,0:T(8,128)(2,1)S(1)} collective-permute-done((bf16[2,128,256]{2,1,0:T(8,128)(2,1)S(1)}, bf16[2,128,256]{2,1,0:T(8,128)(2,1)S(1)}, u32[]{:S(2)}, u32[]{:S(2)}) %collective-permute-start.4) | collective-permute-done | bytes 131104 | tf_op jit(solution)/shard_map/ppermute | solution.py:29
  61.0 1.5 %shard_map.50 = (f32[1024,128]{1,0:T(8,128)S(1)}, f32[1024,128]{1,0:T(8,128)S(1)}) custom-call(s32[2,2,4,2]{3,2,1,0:T(4,128)S(1)} %copy.16.lists, s32[2,2,4,2]{3,2,1,0:T(4,128)S(1)} %collective-permute-done.far3, f32[16,64,256]{2,1,0:T(8,128)S(1)} %shard_map.48.early, bf16[8,256,256]{2,1,0:T(8,128)(2,1)S(1)} %bitcast.14, ...), custom_call_target="tpu_custom_call" | custom-call | tf_op jit(solution)/shard_map/pallas_call | solution.py:221
  62.4 3.7 %collective-permute-start.6 = (f32[1024,128]{1,0:T(8,128)S(1)}, f32[1024,128]{1,0:T(8,128)S(1)}, u32[]{:S(2)}, u32[]{:S(2)}) collective-permute-start(f32[1024,128]{1,0:T(8,128)S(1)} %get-tuple-element.12), channel_id=1, source_target_pairs={{0,1},{1,0},{2,3},{3,2},{4,5},{5,4},{6,7},{7,6},{8,9},{9,8},{10,11... | collective-permute-start | bytes 1572872 | tf_op jit(solution)/shard_map/ppermute | solution.py:235
  66.1 1.5 %collective-permute-done.6.got = f32[1024,128]{1,0:T(8,128)S(1)} collective-permute-done((f32[1024,128]{1,0:T(8,128)S(1)}, f32[1024,128]{1,0:T(8,128)S(1)}, u32[]{:S(2)}, u32[]{:S(2)}) %collective-permute-start.6) | collective-permute-done | bytes 524320 | tf_op jit(solution)/shard_map/ppermute | solution.py:235
  67.7 21.7 %all_to_all.10 = bf16[32,32,128]{2,1,0:T(8,128)(2,1)S(1)} all-to-all(bf16[32,32,128]{2,1,0:T(8,128)(2,1)S(1)} %bitcast.15), channel_id=1, replica_groups=mesh['blk'=12,'pos'=32,'core'=2] {'pos'}, dimensions={0} | all-to-all | bytes 524288 | tf_op jit(solution)/shard_map/all_to_all | solution.py:33
  89.4 0.9 shard_map.52
  (15 shorter events, 0.1 us)
Async XLA Ops:
  0.0 16.2 %copy-start = (bf16[1,1,4,2,256,256]{5,4,3,2,1,0:T(8,128)(2,1)S(1)}, bf16[1,1,4,2,256,256]{5,4,3,2,1,0:T(8,128)(2,1)}, u32[]{:S(2)}) copy-start(bf16[1,1,4,2,256,256]{5,4,3,2,1,0:T(8,128)(2,1)} %param.5) | copy-start | bytes 3145732
  0.0 0.8 copy-start.1
  1.8 35.0 %all-to-all-start = ((bf16[32,32,128]{2,1,0:T(8,128)(2,1)}), bf16[32,32,128]{2,1,0:T(8,128)(2,1)S(1)}, u32[]{:S(2)}, u32[]{:S(2)}) async-start(bf16[32,32,128]{2,1,0:T(8,128)(2,1)} %bitcast.3), calls=%async_computation | async-start | bytes 524288 | tf_op jit(solution)/shard_map/all_to_all | solution.py:33
  16.3 3.0 %copy-start.3 = (s32[1,1,4,2]{2,3,1,0:T(2,128)S(1)}, s32[1,1,4,2]{2,3,1,0:T(2,128)}, u32[]{:S(2)}) copy-start(s32[1,1,4,2]{2,3,1,0:T(2,128)} %param.6) | copy-start | bytes 100
  16.3 24.3 %collective-permute-start.2 = (bf16[4,256,256]{2,1,0:T(8,128)(2,1)S(1)}, bf16[4,256,256]{2,1,0:T(8,128)(2,1)S(1)}, u32[]{:S(2)}, u32[]{:S(2)}) collective-permute-start(bf16[4,256,256]{2,1,0:T(8,128)(2,1)S(1)} %pad_maximum_fusion), channel_id=1, source_target_pairs={{0,1},{1,0},{2,3},{3,2},{4,5},{5,4},{6,7},{7,6},{8,9},{9,8},{10,11... | collective-permute-start | bytes 1572872 | tf_op jit(solution)/shard_map/ppermute | solution.py:186
  19.2 0.7 copy-start.2
  21.8 23.9 %collective-permute-start.1 = (s32[2,2,4,2]{3,2,1,0:T(4,128)S(1)}, s32[2,2,4,2]{3,2,1,0:T(4,128)S(1)}, u32[]{:S(2)}, u32[]{:S(2)}) collective-permute-start(s32[2,2,4,2]{3,2,1,0:T(4,128)S(1)} %copy.16.lists), channel_id=1, source_target_pairs={{0,704},{1,641},{2,706},{3,643},{4,708},{5,645},{6,710},{7,647},{8... | collective-permute-start | bytes 392 | tf_op jit(solution)/shard_map/ppermute | solution.py:29
  34.3 11.4 %collective-permute-start = (s32[2,2,4,2]{3,2,1,0:T(4,128)S(1)}, s32[2,2,4,2]{3,2,1,0:T(4,128)S(1)}, u32[]{:S(2)}, u32[]{:S(2)}) collective-permute-start(s32[2,2,4,2]{3,2,1,0:T(4,128)S(1)} %copy.16.lists), channel_id=1, source_target_pairs={{0,576},{1,577},{2,578},{3,579},{4,580},{5,581},{6,582},{7,583},{8... | collective-permute-start | bytes 392 | tf_op jit(solution)/shard_map/ppermute | solution.py:29
  41.5 12.7 %collective-permute-start.3 = (bf16[2,128,256]{2,1,0:T(8,128)(2,1)S(1)}, bf16[2,128,256]{2,1,0:T(8,128)(2,1)S(1)}, u32[]{:S(2)}, u32[]{:S(2)}) collective-permute-start(bf16[2,128,256]{2,1,0:T(8,128)(2,1)S(1)} %shard_map.47), channel_id=1, source_target_pairs={{0,704},{1,641},{2,706},{3,643},{4,708},{5,645},{6,710},{7,647},{8... | collective-permute-start | bytes 393224 | tf_op jit(solution)/shard_map/ppermute | solution.py:29
  47.0 13.9 %collective-permute-start.4 = (bf16[2,128,256]{2,1,0:T(8,128)(2,1)S(1)}, bf16[2,128,256]{2,1,0:T(8,128)(2,1)S(1)}, u32[]{:S(2)}, u32[]{:S(2)}) collective-permute-start(bf16[2,128,256]{2,1,0:T(8,128)(2,1)S(1)} %get-tuple-element.9), channel_id=1, source_target_pairs={{0,64},{1,129},{2,66},{3,131},{4,68},{5,133},{6,70},{7,135},{8,72}... | collective-permute-start | bytes 393224 | tf_op jit(solution)/shard_map/ppermute | solution.py:29
  52.1 8.9 %collective-permute-start.5 = (bf16[2,128,256]{2,1,0:T(8,128)(2,1)S(1)}, bf16[2,128,256]{2,1,0:T(8,128)(2,1)S(1)}, u32[]{:S(2)}, u32[]{:S(2)}) collective-permute-start(bf16[2,128,256]{2,1,0:T(8,128)(2,1)S(1)} %get-tuple-element.10), channel_id=1, source_target_pairs={{0,192},{1,577},{2,194},{3,579},{4,196},{5,581},{6,198},{7,583},{8... | collective-permute-start | bytes 393224 | tf_op jit(solution)/shard_map/ppermute | solution.py:29
  62.4 5.2 %collective-permute-start.6 = (f32[1024,128]{1,0:T(8,128)S(1)}, f32[1024,128]{1,0:T(8,128)S(1)}, u32[]{:S(2)}, u32[]{:S(2)}) collective-permute-start(f32[1024,128]{1,0:T(8,128)S(1)} %get-tuple-element.12), channel_id=1, source_target_pairs={{0,1},{1,0},{2,3},{3,2},{4,5},{5,4},{6,7},{7,6},{8,9},{9,8},{10,11... | collective-permute-start | bytes 1572872 | tf_op jit(solution)/shard_map/ppermute | solution.py:235

commit v7 on v6

--- a/solution.py
+++ b/solution.py
@@ -63,10 +63,8 @@
         out[i * CHUNK : (i + 1) * CHUNK, :] = packed
 
 
-def shared_block(blocks, other, step, core, at):
-    if core == 0:
-        return blocks[step * SLOTS + at % SLOTS]
-    return other[at]
+def shared_block(blocks, other, step, core, k):
+    return other[(step - 1) * SLOTS + k] if core else blocks[step * SLOTS + k]
 
 
 def transposed_products(lists, held, blocks, other, partials):
@@ -78,12 +76,15 @@
             partials[core, part, :] = times(left, shared_block(blocks, other, 1 + me, core, k)).astype(BF16)
 
 
-def asked_blocks(lists, far, far3, held, blocks, other, picked, third):
-    me = lax.axis_index("core")
-    for k in range(SLOTS):
-        part = slice(NV * k, NV * (k + 1))
-        for core, owner in enumerate((me, 1 - me)):
-            picked[core, part, :] = dense_block(held, far[owner, 1, 1 + me, k])
+def asked_blocks(far, held, picked):
+    me = lax.axis_index("core")
+    for k in range(SLOTS):
+        for core, owner in enumerate((me, 1 - me)):
+            picked[core, NV * k : NV * (k + 1), :] = dense_block(held, far[owner, 1, 1 + me, k])
+
+
+def third_blocks(lists, far3, held, blocks, other, third):
+    me = lax.axis_index("core")
 
     @pl.when(me == 0)
     def _():
@@ -96,7 +97,7 @@
         for k in range(SLOTS):
             for core in range(2):
                 left = dense_block(held, lists[1 - core, 0, 3, k])
-                product = times(left, shared_block(blocks, other, 3, core, SLOTS + k))
+                product = times(left, shared_block(blocks, other, 3, core, k))
                 third[1 - core, NV * k : NV * (k + 1), :] = product.astype(BF16)
 
 
@@ -123,7 +124,6 @@
 
 def late_sums(lists, far3, early, blocks, other, right, third, kept, given, total):
     me = lax.axis_index("core")
-    total[...] = early[...]
     for k in range(SLOTS):
         part = slice(NV * k, NV * (k + 1))
         for core, owner in enumerate((me, 1 - me)):
@@ -135,7 +135,7 @@
         for k in range(SLOTS):
             for core in range(2):
                 came = third[core, NV * k : NV * (k + 1), :]
-                block = shared_block(blocks, other, 3, core, SLOTS + k)
+                block = shared_block(blocks, other, 3, core, k)
                 total[lists[core, 0, 3, k]] += times_transposed(came, block)
 
     @pl.when(me == 1)
@@ -177,13 +177,6 @@
 
 def per_device(vectors, blocks, row_blocks, col_blocks):
     stored = blocks.reshape(STEPS * SLOTS, BS, BS)
-    lists = lax.all_gather(jnp.stack([row_blocks[0, 0], col_blocks[0, 0]]), "core")
-    far = routed(lists, -1, -2)
-    far3 = routed(lists, -3, -3)
-    me = lax.axis_index("core")
-    given = lax.dynamic_slice_in_dim(stored, (2 - me) * SLOTS, SLOTS, 0)
-    given = jnp.concatenate([given, stored[3 * SLOTS :]], axis=0)
-    other = lax.ppermute(given, "core", [(0, 1), (1, 0)])
     mine = pl.pallas_call(
         prepared,
         out_shape=shape_of((COL // 2 * CHUNK, HALF), BF16),
@@ -191,7 +184,11 @@
         out_specs=VM,
         compiler_params=PARAMS,
     )(vectors)
-    held = lax.all_gather(exchanged(mine, CHUNK, "pos"), "core", tiled=True)
+    arriving = exchanged(mine, CHUNK, "pos")
+    lists = lax.all_gather(jnp.stack([row_blocks[0, 0], col_blocks[0, 0]]), "core")
+    far = routed(lists, -1, -2)
+    other = lax.ppermute(stored[SLOTS:], "core", [(0, 1), (1, 0)])
+    held = lax.all_gather(arriving, "core", tiled=True)
     two = shape_of((2, SLOTS * NV, BS), BF16)
     partials = pl.pallas_call(
         transposed_products,
@@ -201,14 +198,23 @@
         compiler_params=PARAMS,
     )(lists, held, stored, other)
     back = routed(partials, -1, -2)
-    picked, third = pl.pallas_call(
+    later_lists, later_far, _ = lax.optimization_barrier((lists, far, partials))
+    far3 = routed(later_lists, -3, -3)
+    picked = pl.pallas_call(
         asked_blocks,
-        out_shape=(two, two),
-        in_specs=[SM] * 3 + [VM] * 3,
-        out_specs=(VM, VM),
-        compiler_params=PARAMS,
-    )(lists, far, far3, held, stored, other)
+        out_shape=two,
+        in_specs=[SM, VM],
+        out_specs=VM,
+        compiler_params=PARAMS,
+    )(later_far, held)
     right = routed(picked, 1, 2)
+    third = pl.pallas_call(
+        third_blocks,
+        out_shape=two,
+        in_specs=[SM, SM] + [VM] * 3,
+        out_specs=VM,
+        compiler_params=PARAMS,
+    )(lists, far3, held, stored, other)
     third = routed(third, 3, -3)
     early = pl.pallas_call(
         early_sums,
@@ -218,12 +224,12 @@
         compiler_params=PARAMS,
     )(lists, far, held, stored, back)
     half = shape_of((COL // 2 * CHUNK, HALF), F32)
-    kept, given = pl.pallas_call(
+    kept, given, _ = pl.pallas_call(
         late_sums,
-        out_shape=(half, half),
+        out_shape=(half, half, shape_of((NBB, NV, BS), F32)),
         in_specs=[SM] * 2 + [VM] * 5,
-        out_specs=(VM, VM),
-        scratch_shapes=[pltpu.VMEM((NBB, NV, BS), F32)],
+        out_specs=(VM,) * 3,
+        input_output_aliases={2: 2},
         compiler_params=PARAMS,
     )(lists, far3, early, stored, other, right, third)
     chips = pl.pallas_call(

time: 91.3 us -> 91.9 us (level)
  blocking collectives: 27.3 us -> 24.3 us
  starting transfers between devices: 46.3 us -> 49.1 us
    ppermute x1, starting transfers between devices: 3.67 us -> 6.42 us  [per_device(): lax.ppermute(given, 'core', [(0, 1), (1, 0)])]
    all_to_all x1, blocking collectives: 21.7 us -> 19 us  [exchanged(): lax.all_to_all(flat.reshape(-1, rows, HALF), axes, 0, 0, tiled=True)]
    slice x1, local copies, waits for them, and re-layouts: 0.02 us -> 1.27 us  [per_device(): other = lax.ppermute(stored[SLOTS:], 'core', [(0, 1), (1, 0)])]
    dynamic_slice x1 -> x0, local copies, waits for them, and re-layouts: 0.97 us -> none  [per_device(): given = lax.dynamic_slice_in_dim(stored, (2 - me) * SLOTS, SLOTS, 0)]
    pallas_call x2 -> x3, Pallas kernels: 2.76 us -> 3.3 us  [the longest x1 1.46 us: per_device(): pl.pallas_call(late_sums, out_shape=(half, half, shape_of((NBB, NV, BS),...]
  transfers between devices with their start and end apart: 8 -> 8, of which waited for: 2 -> 2; matrix products, arithmetic and copies ran while one was open for 1% -> 2% of each run, Pallas kernels for 4% -> 4%
where the time goes in v7:
time: 91.9 us; the launch traced here: 90.8 us
  starting transfers between devices  49.1 us (53%)
  blocking collectives  24.3 us (26%)
  waiting for transfers between devices  7.18 us (8%)
  Pallas kernels  7.17 us (8%)
  local copies, waits for them, and re-layouts  2.93 us (3%)
    ppermute x5, starting transfers between devices, routed(): return lax.ppermute(block, AXES, route)  26.3 us
    all_to_all x1, blocking collectives, exchanged(): lax.all_to_all(flat.reshape(-1, rows, HALF), axes, 0, 0, tiled=True)  19 us
    all_to_all x1, starting transfers between devices, exchanged(): lax.all_to_all(flat.reshape(-1, rows, HALF), axes, 0, 0, tiled=True)  13.5 us
    ppermute x1, starting transfers between devices, per_device(): lax.ppermute(given, 'core', [(0, 1), (1, 0)])  6.42 us
    ppermute x5, waiting for transfers between devices, routed(): return lax.ppermute(block, AXES, route)  5.66 us
    all_gather x1, blocking collectives, per_device(): held = lax.all_gather(arriving, 'core', tiled=True)  3.53 us
    ppermute x1, starting transfers between devices, per_device(): other = lax.ppermute(stored[SLOTS:], 'core', [(0, 1), (1, 0)])  2.86 us
  transfers between devices with their start and end apart: 8, of which 2 were waited for; matrix products, arithmetic and copies ran while one was open for 2% of the time, Pallas kernels for 4%

profile of v7, /device:TPU:1, one launch (start us, length us, event | category | flops | bytes accessed | tf_op | source)
XLA Modules:
  0.0 90.8 jit_solution(3403775313615450042)
XLA Ops:
  0.0 0.8 copy-done.1
  0.8 0.9 %shard_map.46 = bf16[1024,128]{1,0:T(8,128)(2,1)} custom-call(f32[64,64]{1,0:T(8,128)S(1)} %copy-done.1), custom_call_target="tpu_custom_call" | custom-call | tf_op jit(solution)/shard_map/pallas_call | solution.py:180
  1.7 13.5 %all-to-all-start = ((bf16[32,32,128]{2,1,0:T(8,128)(2,1)}), bf16[32,32,128]{2,1,0:T(8,128)(2,1)S(1)}, u32[]{:S(2)}, u32[]{:S(2)}) async-start(bf16[32,32,128]{2,1,0:T(8,128)(2,1)} %bitcast.3), calls=%async_computation | async-start | bytes 524288 | tf_op jit(solution)/shard_map/all_to_all | solution.py:33
  15.2 1.3 %slice.6 = bf16[1,1,3,2,256,256]{5,4,3,2,1,0:T(8,128)(2,1)S(1)} slice(bf16[1,1,4,2,256,256]{5,4,3,2,1,0:T(8,128)(2,1)} %param.5), slice={[0:1], [0:1], [1:4], [0:2], [0:256], [0:256]} | slice | bytes 1572864 | tf_op jit(solution)/shard_map/slice | solution.py:190
  16.5 2.9 %collective-permute-start.1 = (bf16[6,256,256]{2,1,0:T(8,128)(2,1)S(1)}, bf16[6,256,256]{2,1,0:T(8,128)(2,1)S(1)}, u32[]{:S(2)}, u32[]{:S(2)}) collective-permute-start(bf16[6,256,256]{2,1,0:T(8,128)(2,1)S(1)} %bitcast.16), channel_id=1, source_target_pairs={{0,1},{1,0},{2,3},{3,2},{4,5},{5,4},{6,7},{7,6},{8,9},{9,8},{10,11... | collective-permute-start | bytes 2359304 | tf_op jit(solution)/shard_map/ppermute | solution.py:190
  19.4 0.7 copy-done.2
  20.0 1.8 %all-gather = s32[4,4,2]{1,2,0:T(2,128)S(1)} all-gather(s32[2,4,2]{1,2,0:T(2,128)S(1)} %pad_add_fusion), channel_id=2, replica_groups=mesh['blk'=12,'pos'=32,'core'=2] {'core'}, dimensions={0}, use_global_device_ids=true | all-gather | bytes 192 | tf_op jit(solution)/shard_map/all_gather | solution.py:188
  21.9 12.5 %collective-permute-start = (s32[2,2,4,2]{3,2,1,0:T(4,128)S(1)}, s32[2,2,4,2]{3,2,1,0:T(4,128)S(1)}, u32[]{:S(2)}, u32[]{:S(2)}) collective-permute-start(s32[2,2,4,2]{3,2,1,0:T(4,128)S(1)} %copy.17.lists), channel_id=1, source_target_pairs={{0,704},{1,641},{2,706},{3,643},{4,708},{5,645},{6,710},{7,647},{8... | collective-permute-start | bytes 392 | tf_op jit(solution)/shard_map/ppermute | solution.py:29
  34.4 3.5 %all_gather.11.held = bf16[2048,128]{1,0:T(8,128)(2,1)S(1)} all-gather(bf16[1024,128]{1,0:T(8,128)(2,1)S(1)} %bitcast.15), channel_id=1, replica_groups=mesh['blk'=12,'pos'=32,'core'=2] {'core'}, dimensions={0}, use_global_device_ids=true | all-gather | bytes 786432 | tf_op jit(solution)/shard_map/all_gather | solution.py:191
  38.0 0.9 %shard_map.47 = bf16[2,128,256]{2,1,0:T(8,128)(2,1)S(1)} custom-call(s32[2,2,4,2]{3,2,1,0:T(4,128)S(1)} %copy.17.lists, bf16[2048,128]{1,0:T(8,128)(2,1)S(1)} %all_gather.11.held, bf16[8,256,256]{2,1,0:T(8,128)(2,1)S(1)} %bitcast.9, bf16[6,256,256]{2,1,0:T(8,128)(2,1)S(1)} %collective-permute-done.1.other), custom_call_target="tpu_custom_call" | custom-call | tf_op jit(solution)/shard_map/pallas_call | solution.py:193
  38.9 4.7 %collective-permute-start.3 = (bf16[2,128,256]{2,1,0:T(8,128)(2,1)S(1)}, bf16[2,128,256]{2,1,0:T(8,128)(2,1)S(1)}, u32[]{:S(2)}, u32[]{:S(2)}) collective-permute-start(bf16[2,128,256]{2,1,0:T(8,128)(2,1)S(1)} %shard_map.47), channel_id=1, source_target_pairs={{0,704},{1,641},{2,706},{3,643},{4,708},{5,645},{6,710},{7,647},{8... | collective-permute-start | bytes 393224 | tf_op jit(solution)/shard_map/ppermute | solution.py:29
  43.7 0.1 copy.14
  43.8 2.2 %collective-permute-start.2 = (s32[2,2,4,2]{3,2,1,0:T(4,128)S(1)}, s32[2,2,4,2]{3,2,1,0:T(4,128)S(1)}, u32[]{:S(2)}, u32[]{:S(2)}) collective-permute-start(s32[2,2,4,2]{3,2,1,0:T(4,128)S(1)} %copy.14), channel_id=1, source_target_pairs={{0,576},{1,577},{2,578},{3,579},{4,580},{5,581},{6,582},{7,583},{8... | collective-permute-start | bytes 392 | tf_op jit(solution)/shard_map/ppermute | solution.py:29
  46.0 0.8 shard_map.49
  46.7 4.7 %collective-permute-start.4 = (bf16[2,128,256]{2,1,0:T(8,128)(2,1)S(1)}, bf16[2,128,256]{2,1,0:T(8,128)(2,1)S(1)}, u32[]{:S(2)}, u32[]{:S(2)}) collective-permute-start(bf16[2,128,256]{2,1,0:T(8,128)(2,1)S(1)} %shard_map.49), channel_id=1, source_target_pairs={{0,64},{1,129},{2,66},{3,131},{4,68},{5,133},{6,70},{7,135},{8,72}... | collective-permute-start | bytes 393224 | tf_op jit(solution)/shard_map/ppermute | solution.py:29
  51.5 1.1 %shard_map.50 = bf16[2,128,256]{2,1,0:T(8,128)(2,1)S(1)} custom-call(s32[2,2,4,2]{3,2,1,0:T(4,128)S(1)} %copy.17.lists, s32[2,2,4,2]{3,2,1,0:T(4,128)S(1)} %collective-permute-done.2.far3, bf16[2048,128]{1,0:T(8,128)(2,1)S(1)} %all_gather.11.held, bf16[8,256,256]{2,1,0:T(8,128)(2,1)S(1)} %bitcast.10, bf16[6,256,256]{2,1,0:T(8,128)(2,1)S(1)} %collective-permute-done.1.other), custom_call_target="tpu_custom_call" | custom-call | tf_op jit(solution)/shard_map/pallas_call | solution.py:211
  52.6 2.2 %collective-permute-start.5 = (bf16[2,128,256]{2,1,0:T(8,128)(2,1)S(1)}, bf16[2,128,256]{2,1,0:T(8,128)(2,1)S(1)}, u32[]{:S(2)}, u32[]{:S(2)}) collective-permute-start(bf16[2,128,256]{2,1,0:T(8,128)(2,1)S(1)} %shard_map.50), channel_id=1, source_target_pairs={{0,192},{1,577},{2,194},{3,579},{4,196},{5,581},{6,198},{7,583},{8... | collective-permute-start | bytes 393224 | tf_op jit(solution)/shard_map/ppermute | solution.py:29
  54.7 1.1 %shard_map.48.early = f32[16,64,256]{2,1,0:T(8,128)S(1)} custom-call(s32[2,2,4,2]{3,2,1,0:T(4,128)S(1)} %copy.17.lists, s32[2,2,4,2]{3,2,1,0:T(4,128)S(1)} %collective-permute-done.far, bf16[2048,128]{1,0:T(8,128)(2,1)S(1)} %all_gather.11.held, bf16[8,256,256]{2,1,0:T(8,128)(2,1)S(1)} %bitcast.11, bf16[2,128,256]{2,1,0:T(8,128)(2,1)S(1)} %collective-permute-done.3.back), custom_call_target="tpu_custom_call" | custom-call | tf_op jit(solution)/shard_map/pallas_call | solution.py:219
  55.9 5.6 %collective-permute-done.4.right = bf16[2,128,256]{2,1,0:T(8,128)(2,1)S(1)} collective-permute-done((bf16[2,128,256]{2,1,0:T(8,128)(2,1)S(1)}, bf16[2,128,256]{2,1,0:T(8,128)(2,1)S(1)}, u32[]{:S(2)}, u32[]{:S(2)}) %collective-permute-start.4) | collective-permute-done | bytes 131104 | tf_op jit(solution)/shard_map/ppermute | solution.py:29
  61.5 1.5 %shard_map.51 = (f32[1024,128]{1,0:T(8,128)S(1)}, f32[1024,128]{1,0:T(8,128)S(1)}, f32[16,64,256]{2,1,0:T(8,128)S(1)}) custom-call(s32[2,2,4,2]{3,2,1,0:T(4,128)S(1)} %copy.17.lists, s32[2,2,4,2]{3,2,1,0:T(4,128)S(1)} %collective-permute-done.2.far3, f32[16,64,256]{2,1,0:T(8,128)S(1)} %shard_map.48.early, ...), custom_call_target="tpu_custom_call", output_to_operand_aliasing={{2}: (2, {})} | custom-call | tf_op jit(solution)/shard_map/pallas_call | solution.py:227
  63.0 6.4 %collective-permute-start.6 = (f32[1024,128]{1,0:T(8,128)S(1)}, f32[1024,128]{1,0:T(8,128)S(1)}, u32[]{:S(2)}, u32[]{:S(2)}) collective-permute-start(f32[1024,128]{1,0:T(8,128)S(1)} %get-tuple-element.12), channel_id=1, source_target_pairs={{0,1},{1,0},{2,3},{3,2},{4,5},{5,4},{6,7},{7,6},{8,9},{9,8},{10,11... | collective-permute-start | bytes 1572872 | tf_op jit(solution)/shard_map/ppermute | solution.py:241
  69.4 1.5 %collective-permute-done.6.got = f32[1024,128]{1,0:T(8,128)S(1)} collective-permute-done((f32[1024,128]{1,0:T(8,128)S(1)}, f32[1024,128]{1,0:T(8,128)S(1)}, u32[]{:S(2)}, u32[]{:S(2)}) %collective-permute-start.6) | collective-permute-done | bytes 524320 | tf_op jit(solution)/shard_map/ppermute | solution.py:241
  71.0 19.0 %all_to_all.10 = bf16[32,32,128]{2,1,0:T(8,128)(2,1)S(1)} all-to-all(bf16[32,32,128]{2,1,0:T(8,128)(2,1)S(1)} %bitcast.13), channel_id=1, replica_groups=mesh['blk'=12,'pos'=32,'core'=2] {'pos'}, dimensions={0} | all-to-all | bytes 524288 | tf_op jit(solution)/shard_map/all_to_all | solution.py:33
  89.9 0.9 shard_map.53
  (15 shorter events, 0.2 us)
Async XLA Ops:
  0.0 0.8 copy-start.1
  1.7 32.8 %all-to-all-start = ((bf16[32,32,128]{2,1,0:T(8,128)(2,1)}), bf16[32,32,128]{2,1,0:T(8,128)(2,1)S(1)}, u32[]{:S(2)}, u32[]{:S(2)}) async-start(bf16[32,32,128]{2,1,0:T(8,128)(2,1)} %bitcast.3), calls=%async_computation | async-start | bytes 524288 | tf_op jit(solution)/shard_map/all_to_all | solution.py:33
  15.2 4.2 %copy-start.3 = (s32[1,1,4,2]{2,3,1,0:T(2,128)S(1)}, s32[1,1,4,2]{2,3,1,0:T(2,128)}, u32[]{:S(2)}) copy-start(s32[1,1,4,2]{2,3,1,0:T(2,128)} %param.6) | copy-start | bytes 100
  15.2 22.8 %copy-start = (bf16[1,1,4,2,256,256]{5,4,3,2,1,0:T(8,128)(2,1)S(1)}, bf16[1,1,4,2,256,256]{5,4,3,2,1,0:T(8,128)(2,1)}, u32[]{:S(2)}) copy-start(bf16[1,1,4,2,256,256]{5,4,3,2,1,0:T(8,128)(2,1)} %param.5) | copy-start | bytes 3145732
  16.5 21.5 %collective-permute-start.1 = (bf16[6,256,256]{2,1,0:T(8,128)(2,1)S(1)}, bf16[6,256,256]{2,1,0:T(8,128)(2,1)S(1)}, u32[]{:S(2)}, u32[]{:S(2)}) collective-permute-start(bf16[6,256,256]{2,1,0:T(8,128)(2,1)S(1)} %bitcast.16), channel_id=1, source_target_pairs={{0,1},{1,0},{2,3},{3,2},{4,5},{5,4},{6,7},{7,6},{8,9},{9,8},{10,11... | collective-permute-start | bytes 2359304 | tf_op jit(solution)/shard_map/ppermute | solution.py:190
  19.3 0.7 copy-start.2
  21.9 21.8 %collective-permute-start = (s32[2,2,4,2]{3,2,1,0:T(4,128)S(1)}, s32[2,2,4,2]{3,2,1,0:T(4,128)S(1)}, u32[]{:S(2)}, u32[]{:S(2)}) collective-permute-start(s32[2,2,4,2]{3,2,1,0:T(4,128)S(1)} %copy.17.lists), channel_id=1, source_target_pairs={{0,704},{1,641},{2,706},{3,643},{4,708},{5,645},{6,710},{7,647},{8... | collective-permute-start | bytes 392 | tf_op jit(solution)/shard_map/ppermute | solution.py:29
  38.9 15.8 %collective-permute-start.3 = (bf16[2,128,256]{2,1,0:T(8,128)(2,1)S(1)}, bf16[2,128,256]{2,1,0:T(8,128)(2,1)S(1)}, u32[]{:S(2)}, u32[]{:S(2)}) collective-permute-start(bf16[2,128,256]{2,1,0:T(8,128)(2,1)S(1)} %shard_map.47), channel_id=1, source_target_pairs={{0,704},{1,641},{2,706},{3,643},{4,708},{5,645},{6,710},{7,647},{8... | collective-permute-start | bytes 393224 | tf_op jit(solution)/shard_map/ppermute | solution.py:29
  43.8 7.7 %collective-permute-start.2 = (s32[2,2,4,2]{3,2,1,0:T(4,128)S(1)}, s32[2,2,4,2]{3,2,1,0:T(4,128)S(1)}, u32[]{:S(2)}, u32[]{:S(2)}) collective-permute-start(s32[2,2,4,2]{3,2,1,0:T(4,128)S(1)} %copy.14), channel_id=1, source_target_pairs={{0,576},{1,577},{2,578},{3,579},{4,580},{5,581},{6,582},{7,583},{8... | collective-permute-start | bytes 392 | tf_op jit(solution)/shard_map/ppermute | solution.py:29
  46.7 14.8 %collective-permute-start.4 = (bf16[2,128,256]{2,1,0:T(8,128)(2,1)S(1)}, bf16[2,128,256]{2,1,0:T(8,128)(2,1)S(1)}, u32[]{:S(2)}, u32[]{:S(2)}) collective-permute-start(bf16[2,128,256]{2,1,0:T(8,128)(2,1)S(1)} %shard_map.49), channel_id=1, source_target_pairs={{0,64},{1,129},{2,66},{3,131},{4,68},{5,133},{6,70},{7,135},{8,72}... | collective-permute-start | bytes 393224 | tf_op jit(solution)/shard_map/ppermute | solution.py:29
  52.6 8.9 %collective-permute-start.5 = (bf16[2,128,256]{2,1,0:T(8,128)(2,1)S(1)}, bf16[2,128,256]{2,1,0:T(8,128)(2,1)S(1)}, u32[]{:S(2)}, u32[]{:S(2)}) collective-permute-start(bf16[2,128,256]{2,1,0:T(8,128)(2,1)S(1)} %shard_map.50), channel_id=1, source_target_pairs={{0,192},{1,577},{2,194},{3,579},{4,196},{5,581},{6,198},{7,583},{8... | collective-permute-start | bytes 393224 | tf_op jit(solution)/shard_map/ppermute | solution.py:29
  63.0 7.9 %collective-permute-start.6 = (f32[1024,128]{1,0:T(8,128)S(1)}, f32[1024,128]{1,0:T(8,128)S(1)}, u32[]{:S(2)}, u32[]{:S(2)}) collective-permute-start(f32[1024,128]{1,0:T(8,128)S(1)} %get-tuple-element.12), channel_id=1, source_target_pairs={{0,1},{1,0},{2,3},{3,2},{4,5},{5,4},{6,7},{7,6},{8,9},{9,8},{10,11... | collective-permute-start | bytes 1572872 | tf_op jit(solution)/shard_map/ppermute | solution.py:241

commit v8 on v7

--- a/solution.py
+++ b/solution.py
@@ -64,7 +64,7 @@
 
 
 def shared_block(blocks, other, step, core, k):
-    return other[(step - 1) * SLOTS + k] if core else blocks[step * SLOTS + k]
+    return (other if core else blocks)[step * SLOTS + k]
 
 
 def transposed_products(lists, held, blocks, other, partials):
@@ -187,7 +187,7 @@
     arriving = exchanged(mine, CHUNK, "pos")
     lists = lax.all_gather(jnp.stack([row_blocks[0, 0], col_blocks[0, 0]]), "core")
     far = routed(lists, -1, -2)
-    other = lax.ppermute(stored[SLOTS:], "core", [(0, 1), (1, 0)])
+    other = lax.ppermute(stored, "core", [(0, 1), (1, 0)])
     held = lax.all_gather(arriving, "core", tiled=True)
     two = shape_of((2, SLOTS * NV, BS), BF16)
     partials = pl.pallas_call(
@@ -198,8 +198,8 @@
         compiler_params=PARAMS,
     )(lists, held, stored, other)
     back = routed(partials, -1, -2)
-    later_lists, later_far, _ = lax.optimization_barrier((lists, far, partials))
-    far3 = routed(later_lists, -3, -3)
+    later_far, _ = lax.optimization_barrier((far, partials))
+    far3 = routed(lists, -3, -3)
     picked = pl.pallas_call(
         asked_blocks,
         out_shape=two,
@@ -215,6 +215,7 @@
         out_specs=VM,
         compiler_params=PARAMS,
     )(lists, far3, held, stored, other)
+    third_sent = third
     third = routed(third, 3, -3)
     early = pl.pallas_call(
         early_sums,
@@ -222,7 +223,7 @@
         in_specs=[SM] * 2 + [VM] * 3,
         out_specs=VM,
         compiler_params=PARAMS,
-    )(lists, far, held, stored, back)
+    )(lists, far, lax.optimization_barrier((held, third_sent))[0], stored, back)
     half = shape_of((COL // 2 * CHUNK, HALF), F32)
     kept, given, _ = pl.pallas_call(
         late_sums,

time: 91.9 us -> 89.8 us (0.977)
  starting transfers between devices: 49.1 us -> 45.6 us
  local copies, waits for them, and re-layouts: 2.93 us -> 0.86 us
  waiting for transfers between devices: 7.18 us -> 8.67 us
  blocking collectives: 24.3 us -> 25.5 us
    ppermute x1, starting transfers between devices: 2.86 us -> 12.5 us  [per_device(): other = lax.ppermute(stored, 'core', [(0, 1), (1, 0)])]
    all_to_all x1, starting transfers between devices: 13.5 us -> 3.87 us  [exchanged(): lax.all_to_all(flat.reshape(-1, rows, HALF), axes, 0, 0, tiled=True)]
    ppermute x1, starting transfers between devices: 6.42 us -> 3.12 us  [per_device(): lax.ppermute(given, 'core', [(0, 1), (1, 0)])]
    ppermute x5, waiting for transfers between devices: 5.66 us -> 7.15 us  [routed(): return lax.ppermute(block, AXES, route)]
    slice x1 -> x0, local copies, waits for them, and re-layouts: 1.27 us -> none  [per_device(): other = lax.ppermute(stored[SLOTS:], 'core', [(0, 1), (1, 0)])]
  transfers between devices with their start and end apart: 8 -> 8, of which waited for: 2 -> 2; matrix products, arithmetic and copies ran while one was open for 2% -> 1% of each run, Pallas kernels for 4% -> 5%
where the time goes in v8:
time: 89.8 us; the launch traced here: 88.7 us
  starting transfers between devices  45.6 us (51%)
  blocking collectives  25.5 us (28%)
  waiting for transfers between devices  8.67 us (10%)
  Pallas kernels  7.17 us (8%)
    ppermute x5, starting transfers between devices, routed(): return lax.ppermute(block, AXES, route)  26.1 us
    all_to_all x1, blocking collectives, exchanged(): lax.all_to_all(flat.reshape(-1, rows, HALF), axes, 0, 0, tiled=True)  19.8 us
    ppermute x1, starting transfers between devices, per_device(): other = lax.ppermute(stored, 'core', [(0, 1), (1, 0)])  12.5 us
    ppermute x5, waiting for transfers between devices, routed(): return lax.ppermute(block, AXES, route)  7.15 us
    all_gather x1, blocking collectives, per_device(): held = lax.all_gather(arriving, 'core', tiled=True)  3.9 us
    all_to_all x1, starting transfers between devices, exchanged(): lax.all_to_all(flat.reshape(-1, rows, HALF), axes, 0, 0, tiled=True)  3.87 us
    ppermute x1, starting transfers between devices, per_device(): lax.ppermute(given, 'core', [(0, 1), (1, 0)])  3.12 us
  transfers between devices with their start and end apart: 8, of which 2 were waited for; matrix products, arithmetic and copies ran while one was open for 1% of the time, Pallas kernels for 5%

profile of v8, /device:TPU:1, one launch (start us, length us, event | category | flops | bytes accessed | tf_op | source)
XLA Modules:
  0.0 88.7 jit_solution(8082499270743049392)
XLA Ops:
  0.0 12.5 %collective-permute-start.2 = (bf16[8,256,256]{2,1,0:T(8,128)(2,1)}, bf16[8,256,256]{2,1,0:T(8,128)(2,1)S(1)}, u32[]{:S(2)}, u32[]{:S(2)}) collective-permute-start(bf16[8,256,256]{2,1,0:T(8,128)(2,1)} %bitcast.8), channel_id=1, source_target_pairs={{0,1},{1,0},{2,3},{3,2},{4,5},{5,4},{6,7},{7,6},{8,9},{9,8},{10,11... | collective-permute-start | bytes 3145736 | tf_op jit(solution)/shard_map/ppermute | solution.py:190
  12.6 0.7 copy-done.1
  13.3 0.9 %shard_map.46 = bf16[1024,128]{1,0:T(8,128)(2,1)} custom-call(f32[64,64]{1,0:T(8,128)S(1)} %copy-done.1), custom_call_target="tpu_custom_call" | custom-call | tf_op jit(solution)/shard_map/pallas_call | solution.py:180
  14.3 3.9 %all-to-all-start = ((bf16[32,32,128]{2,1,0:T(8,128)(2,1)}), bf16[32,32,128]{2,1,0:T(8,128)(2,1)S(1)}, u32[]{:S(2)}, u32[]{:S(2)}) async-start(bf16[32,32,128]{2,1,0:T(8,128)(2,1)} %bitcast.3), calls=%async_computation | async-start | bytes 524288 | tf_op jit(solution)/shard_map/all_to_all | solution.py:33
  18.1 0.7 pad_add_fusion
  18.8 1.8 %all-gather = s32[4,4,2]{1,2,0:T(2,128)S(1)} all-gather(s32[2,4,2]{1,2,0:T(2,128)S(1)} %pad_add_fusion), channel_id=2, replica_groups=mesh['blk'=12,'pos'=32,'core'=2] {'core'}, dimensions={0}, use_global_device_ids=true | all-gather | bytes 192 | tf_op jit(solution)/shard_map/all_gather | solution.py:188
  20.6 0.1 copy.17.lists
  20.7 12.3 %collective-permute-start.1 = (s32[2,2,4,2]{3,2,1,0:T(4,128)S(1)}, s32[2,2,4,2]{3,2,1,0:T(4,128)S(1)}, u32[]{:S(2)}, u32[]{:S(2)}) collective-permute-start(s32[2,2,4,2]{3,2,1,0:T(4,128)S(1)} %copy.17.lists), channel_id=1, source_target_pairs={{0,704},{1,641},{2,706},{3,643},{4,708},{5,645},{6,710},{7,647},{8... | collective-permute-start | bytes 392 | tf_op jit(solution)/shard_map/ppermute | solution.py:29
  33.0 2.5 %collective-permute-start = (s32[2,2,4,2]{3,2,1,0:T(4,128)S(1)}, s32[2,2,4,2]{3,2,1,0:T(4,128)S(1)}, u32[]{:S(2)}, u32[]{:S(2)}) collective-permute-start(s32[2,2,4,2]{3,2,1,0:T(4,128)S(1)} %copy.17.lists), channel_id=1, source_target_pairs={{0,576},{1,577},{2,578},{3,579},{4,580},{5,581},{6,582},{7,583},{8... | collective-permute-start | bytes 392 | tf_op jit(solution)/shard_map/ppermute | solution.py:29
  35.5 3.9 %all_gather.11.held = bf16[2048,128]{1,0:T(8,128)(2,1)S(1)} all-gather(bf16[1024,128]{1,0:T(8,128)(2,1)S(1)} %bitcast.15), channel_id=1, replica_groups=mesh['blk'=12,'pos'=32,'core'=2] {'core'}, dimensions={0}, use_global_device_ids=true | all-gather | bytes 786432 | tf_op jit(solution)/shard_map/all_gather | solution.py:191
  39.4 0.0 collective-permute-done.2.other
  39.4 0.9 %shard_map.48 = bf16[2,128,256]{2,1,0:T(8,128)(2,1)S(1)} custom-call(s32[2,2,4,2]{3,2,1,0:T(4,128)S(1)} %copy.17.lists, bf16[2048,128]{1,0:T(8,128)(2,1)S(1)} %all_gather.11.held, bf16[8,256,256]{2,1,0:T(8,128)(2,1)S(1)} %bitcast.9, bf16[8,256,256]{2,1,0:T(8,128)(2,1)S(1)} %collective-permute-done.2.other), custom_call_target="tpu_custom_call" | custom-call | tf_op jit(solution)/shard_map/pallas_call | solution.py:193
  40.3 5.7 %collective-permute-start.3 = (bf16[2,128,256]{2,1,0:T(8,128)(2,1)S(1)}, bf16[2,128,256]{2,1,0:T(8,128)(2,1)S(1)}, u32[]{:S(2)}, u32[]{:S(2)}) collective-permute-start(bf16[2,128,256]{2,1,0:T(8,128)(2,1)S(1)} %shard_map.48), channel_id=1, source_target_pairs={{0,704},{1,641},{2,706},{3,643},{4,708},{5,645},{6,710},{7,647},{8... | collective-permute-start | bytes 393224 | tf_op jit(solution)/shard_map/ppermute | solution.py:29
  46.1 0.8 shard_map.50
  46.8 3.5 %collective-permute-start.4 = (bf16[2,128,256]{2,1,0:T(8,128)(2,1)S(1)}, bf16[2,128,256]{2,1,0:T(8,128)(2,1)S(1)}, u32[]{:S(2)}, u32[]{:S(2)}) collective-permute-start(bf16[2,128,256]{2,1,0:T(8,128)(2,1)S(1)} %shard_map.50), channel_id=1, source_target_pairs={{0,64},{1,129},{2,66},{3,131},{4,68},{5,133},{6,70},{7,135},{8,72}... | collective-permute-start | bytes 393224 | tf_op jit(solution)/shard_map/ppermute | solution.py:29
  50.3 1.1 %shard_map.47 = bf16[2,128,256]{2,1,0:T(8,128)(2,1)S(1)} custom-call(s32[2,2,4,2]{3,2,1,0:T(4,128)S(1)} %copy.17.lists, s32[2,2,4,2]{3,2,1,0:T(4,128)S(1)} %collective-permute-done.far3, bf16[2048,128]{1,0:T(8,128)(2,1)S(1)} %all_gather.11.held, bf16[8,256,256]{2,1,0:T(8,128)(2,1)S(1)} %bitcast.10, bf16[8,256,256]{2,1,0:T(8,128)(2,1)S(1)} %collective-permute-done.2.other), custom_call_target="tpu_custom_call" | custom-call | tf_op jit(solution)/shard_map/pallas_call | solution.py:211
  51.4 2.2 %collective-permute-start.5 = (bf16[2,128,256]{2,1,0:T(8,128)(2,1)S(1)}, bf16[2,128,256]{2,1,0:T(8,128)(2,1)S(1)}, u32[]{:S(2)}, u32[]{:S(2)}) collective-permute-start(bf16[2,128,256]{2,1,0:T(8,128)(2,1)S(1)} %shard_map.47), channel_id=1, source_target_pairs={{0,192},{1,577},{2,194},{3,579},{4,196},{5,581},{6,198},{7,583},{8... | collective-permute-start | bytes 393224 | tf_op jit(solution)/shard_map/ppermute | solution.py:29
  53.6 1.1 %shard_map.49.early = f32[16,64,256]{2,1,0:T(8,128)S(1)} custom-call(s32[2,2,4,2]{3,2,1,0:T(4,128)S(1)} %copy.17.lists, s32[2,2,4,2]{3,2,1,0:T(4,128)S(1)} %collective-permute-done.1.far, bf16[2048,128]{1,0:T(8,128)(2,1)S(1)} %all_gather.11.held, bf16[8,256,256]{2,1,0:T(8,128)(2,1)S(1)} %bitcast.11, bf16[2,128,256]{2,1,0:T(8,128)(2,1)S(1)} %collective-permute-done.3.back), custom_call_target="tpu_custom_call" | custom-call | tf_op jit(solution)/shard_map/pallas_call | solution.py:220
  54.7 7.1 %collective-permute-done.4.right = bf16[2,128,256]{2,1,0:T(8,128)(2,1)S(1)} collective-permute-done((bf16[2,128,256]{2,1,0:T(8,128)(2,1)S(1)}, bf16[2,128,256]{2,1,0:T(8,128)(2,1)S(1)}, u32[]{:S(2)}, u32[]{:S(2)}) %collective-permute-start.4) | collective-permute-done | bytes 131104 | tf_op jit(solution)/shard_map/ppermute | solution.py:29
  61.8 1.5 %shard_map.51 = (f32[1024,128]{1,0:T(8,128)S(1)}, f32[1024,128]{1,0:T(8,128)S(1)}, f32[16,64,256]{2,1,0:T(8,128)S(1)}) custom-call(s32[2,2,4,2]{3,2,1,0:T(4,128)S(1)} %copy.17.lists, s32[2,2,4,2]{3,2,1,0:T(4,128)S(1)} %collective-permute-done.far3, f32[16,64,256]{2,1,0:T(8,128)S(1)} %shard_map.49.early, ...), custom_call_target="tpu_custom_call", output_to_operand_aliasing={{2}: (2, {})} | custom-call | tf_op jit(solution)/shard_map/pallas_call | solution.py:228
  63.3 3.1 %collective-permute-start.6 = (f32[1024,128]{1,0:T(8,128)S(1)}, f32[1024,128]{1,0:T(8,128)S(1)}, u32[]{:S(2)}, u32[]{:S(2)}) collective-permute-start(f32[1024,128]{1,0:T(8,128)S(1)} %get-tuple-element.12), channel_id=1, source_target_pairs={{0,1},{1,0},{2,3},{3,2},{4,5},{5,4},{6,7},{7,6},{8,9},{9,8},{10,11... | collective-permute-start | bytes 1572872 | tf_op jit(solution)/shard_map/ppermute | solution.py:242
  66.4 1.5 %collective-permute-done.6.got = f32[1024,128]{1,0:T(8,128)S(1)} collective-permute-done((f32[1024,128]{1,0:T(8,128)S(1)}, f32[1024,128]{1,0:T(8,128)S(1)}, u32[]{:S(2)}, u32[]{:S(2)}) %collective-permute-start.6) | collective-permute-done | bytes 524320 | tf_op jit(solution)/shard_map/ppermute | solution.py:242
  68.0 19.8 %all_to_all.10 = bf16[32,32,128]{2,1,0:T(8,128)(2,1)S(1)} all-to-all(bf16[32,32,128]{2,1,0:T(8,128)(2,1)S(1)} %bitcast.13), channel_id=1, replica_groups=mesh['blk'=12,'pos'=32,'core'=2] {'pos'}, dimensions={0} | all-to-all | bytes 524288 | tf_op jit(solution)/shard_map/all_to_all | solution.py:33
  87.8 0.9 shard_map.53
  (9 shorter events, 0.1 us)
Async XLA Ops:
  0.0 39.4 %copy-start = (bf16[1,1,4,2,256,256]{5,4,3,2,1,0:T(8,128)(2,1)S(1)}, bf16[1,1,4,2,256,256]{5,4,3,2,1,0:T(8,128)(2,1)}, u32[]{:S(2)}) copy-start(bf16[1,1,4,2,256,256]{5,4,3,2,1,0:T(8,128)(2,1)} %param.5) | copy-start | bytes 3145732
  0.0 39.4 %collective-permute-start.2 = (bf16[8,256,256]{2,1,0:T(8,128)(2,1)}, bf16[8,256,256]{2,1,0:T(8,128)(2,1)S(1)}, u32[]{:S(2)}, u32[]{:S(2)}) collective-permute-start(bf16[8,256,256]{2,1,0:T(8,128)(2,1)} %bitcast.8), channel_id=1, source_target_pairs={{0,1},{1,0},{2,3},{3,2},{4,5},{5,4},{6,7},{7,6},{8,9},{9,8},{10,11... | collective-permute-start | bytes 3145736 | tf_op jit(solution)/shard_map/ppermute | solution.py:190
  12.6 0.8 copy-start.1
  14.3 21.2 %all-to-all-start = ((bf16[32,32,128]{2,1,0:T(8,128)(2,1)}), bf16[32,32,128]{2,1,0:T(8,128)(2,1)S(1)}, u32[]{:S(2)}, u32[]{:S(2)}) async-start(bf16[32,32,128]{2,1,0:T(8,128)(2,1)} %bitcast.3), calls=%async_computation | async-start | bytes 524288 | tf_op jit(solution)/shard_map/all_to_all | solution.py:33
  20.7 25.3 %collective-permute-start.1 = (s32[2,2,4,2]{3,2,1,0:T(4,128)S(1)}, s32[2,2,4,2]{3,2,1,0:T(4,128)S(1)}, u32[]{:S(2)}, u32[]{:S(2)}) collective-permute-start(s32[2,2,4,2]{3,2,1,0:T(4,128)S(1)} %copy.17.lists), channel_id=1, source_target_pairs={{0,704},{1,641},{2,706},{3,643},{4,708},{5,645},{6,710},{7,647},{8... | collective-permute-start | bytes 392 | tf_op jit(solution)/shard_map/ppermute | solution.py:29
  33.0 17.3 %collective-permute-start = (s32[2,2,4,2]{3,2,1,0:T(4,128)S(1)}, s32[2,2,4,2]{3,2,1,0:T(4,128)S(1)}, u32[]{:S(2)}, u32[]{:S(2)}) collective-permute-start(s32[2,2,4,2]{3,2,1,0:T(4,128)S(1)} %copy.17.lists), channel_id=1, source_target_pairs={{0,576},{1,577},{2,578},{3,579},{4,580},{5,581},{6,582},{7,583},{8... | collective-permute-start | bytes 392 | tf_op jit(solution)/shard_map/ppermute | solution.py:29
  40.3 13.3 %collective-permute-start.3 = (bf16[2,128,256]{2,1,0:T(8,128)(2,1)S(1)}, bf16[2,128,256]{2,1,0:T(8,128)(2,1)S(1)}, u32[]{:S(2)}, u32[]{:S(2)}) collective-permute-start(bf16[2,128,256]{2,1,0:T(8,128)(2,1)S(1)} %shard_map.48), channel_id=1, source_target_pairs={{0,704},{1,641},{2,706},{3,643},{4,708},{5,645},{6,710},{7,647},{8... | collective-permute-start | bytes 393224 | tf_op jit(solution)/shard_map/ppermute | solution.py:29
  46.8 15.0 %collective-permute-start.4 = (bf16[2,128,256]{2,1,0:T(8,128)(2,1)S(1)}, bf16[2,128,256]{2,1,0:T(8,128)(2,1)S(1)}, u32[]{:S(2)}, u32[]{:S(2)}) collective-permute-start(bf16[2,128,256]{2,1,0:T(8,128)(2,1)S(1)} %shard_map.50), channel_id=1, source_target_pairs={{0,64},{1,129},{2,66},{3,131},{4,68},{5,133},{6,70},{7,135},{8,72}... | collective-permute-start | bytes 393224 | tf_op jit(solution)/shard_map/ppermute | solution.py:29
  51.4 10.4 %collective-permute-start.5 = (bf16[2,128,256]{2,1,0:T(8,128)(2,1)S(1)}, bf16[2,128,256]{2,1,0:T(8,128)(2,1)S(1)}, u32[]{:S(2)}, u32[]{:S(2)}) collective-permute-start(bf16[2,128,256]{2,1,0:T(8,128)(2,1)S(1)} %shard_map.47), channel_id=1, source_target_pairs={{0,192},{1,577},{2,194},{3,579},{4,196},{5,581},{6,198},{7,583},{8... | collective-permute-start | bytes 393224 | tf_op jit(solution)/shard_map/ppermute | solution.py:29
  63.3 4.6 %collective-permute-start.6 = (f32[1024,128]{1,0:T(8,128)S(1)}, f32[1024,128]{1,0:T(8,128)S(1)}, u32[]{:S(2)}, u32[]{:S(2)}) collective-permute-start(f32[1024,128]{1,0:T(8,128)S(1)} %get-tuple-element.12), channel_id=1, source_target_pairs={{0,1},{1,0},{2,3},{3,2},{4,5},{5,4},{6,7},{7,6},{8,9},{9,8},{10,11... | collective-permute-start | bytes 1572872 | tf_op jit(solution)/shard_map/ppermute | solution.py:242

commit v9 on v8

--- a/solution.py
+++ b/solution.py
@@ -119,7 +119,8 @@
         for q in range(4):
             part = whole[:, 64 * q : 64 * q + 64]
             start = (row * 2 + q // 2) * CHUNK
-            outs[q % 2][start : start + CHUNK, :] = jnp.concatenate([part[:32], part[32:]], axis=1)
+            out = outs[q % 2]
+            out[start : start + CHUNK, :] = jnp.concatenate([part[:32], part[32:]], axis=1).astype(out.dtype)
 
 
 def late_sums(lists, far3, early, blocks, other, right, third, kept, given, total):
@@ -154,7 +155,8 @@
 
 
 def both_cores(kept, got, out):
-    out[...] = (kept[...] + got[...]).astype(BF16)
+    theirs = got[1 - lax.axis_index("core")]
+    out[...] = (kept[...] + theirs.astype(F32)).astype(BF16)
 
 
 def gathered_sum(arrived, out):
@@ -224,10 +226,10 @@
         out_specs=VM,
         compiler_params=PARAMS,
     )(lists, far, lax.optimization_barrier((held, third_sent))[0], stored, back)
-    half = shape_of((COL // 2 * CHUNK, HALF), F32)
+    half = (COL // 2 * CHUNK, HALF)
     kept, given, _ = pl.pallas_call(
         late_sums,
-        out_shape=(half, half, shape_of((NBB, NV, BS), F32)),
+        out_shape=(shape_of(half, F32), shape_of(half, BF16), shape_of((NBB, NV, BS), F32)),
         in_specs=[SM] * 2 + [VM] * 5,
         out_specs=(VM,) * 3,
         input_output_aliases={2: 2},
@@ -235,11 +237,11 @@
     )(lists, far3, early, stored, other, right, third)
     chips = pl.pallas_call(
         both_cores,
-        out_shape=shape_of((COL // 2 * CHUNK, HALF), BF16),
+        out_shape=shape_of(half, BF16),
         in_specs=[VM, VM],
         out_specs=VM,
         compiler_params=PARAMS,
-    )(kept, lax.ppermute(given, "core", [(0, 1), (1, 0)]))
+    )(kept, lax.all_gather(given, "core"))
     return pl.pallas_call(
         gathered_sum,
         out_shape=shape_of((64, NV), F32),

time: 89.8 us -> 88.1 us (0.981)
  starting transfers between devices: 45.6 us -> 42.5 us
  blocking collectives: 25.5 us -> 28.5 us
  waiting for transfers between devices: 8.67 us -> 7.16 us
    ppermute x1 -> x0, starting transfers between devices: 3.12 us -> none  [per_device(): lax.ppermute(given, 'core', [(0, 1), (1, 0)])]
    all_gather x0 -> x1, blocking collectives: none -> 3.03 us  [per_device(): lax.all_gather(given, 'core')]
    ppermute x1 -> x0, waiting for transfers between devices: 1.51 us -> none  [per_device(): lax.ppermute(given, 'core', [(0, 1), (1, 0)])]
  transfers between devices with their start and end apart: 8 -> 7, of which waited for: 2 -> 1; matrix products, arithmetic and copies ran while one was open for 1% -> 1% of each run, Pallas kernels for 5% -> 6%
where the time goes in v9:
time: 88.1 us; the launch traced here: 87 us
  starting transfers between devices  42.5 us (48%)
  blocking collectives  28.5 us (32%)
  waiting for transfers between devices  7.16 us (8%)
  Pallas kernels  7.11 us (8%)
    ppermute x5, starting transfers between devices, routed(): return lax.ppermute(block, AXES, route)  26.1 us
    all_to_all x1, blocking collectives, exchanged(): lax.all_to_all(flat.reshape(-1, rows, HALF), axes, 0, 0, tiled=True)  19.8 us
    ppermute x1, starting transfers between devices, per_device(): other = lax.ppermute(stored, 'core', [(0, 1), (1, 0)])  12.5 us
    ppermute x5, waiting for transfers between devices, routed(): return lax.ppermute(block, AXES, route)  7.15 us
    all_gather x1, blocking collectives, per_device(): held = lax.all_gather(arriving, 'core', tiled=True)  3.9 us
    all_to_all x1, starting transfers between devices, exchanged(): lax.all_to_all(flat.reshape(-1, rows, HALF), axes, 0, 0, tiled=True)  3.87 us
    all_gather x1, blocking collectives, per_device(): lax.all_gather(given, 'core')  3.03 us
    all_gather x1, blocking collectives, per_device(): lax.all_gather(jnp.stack([row_blocks[0, 0], col_blocks[0, 0]]), 'core')  1.77 us
  transfers between devices with their start and end apart: 7, of which 1 were waited for; matrix products, arithmetic and copies ran while one was open for 1% of the time, Pallas kernels for 6%

profile of v9, /device:TPU:1, one launch (start us, length us, event | category | flops | bytes accessed | tf_op | source)
XLA Modules:
  0.0 87.0 jit_solution(4737506494258419813)
XLA Ops:
  0.0 12.5 %collective-permute-start.2 = (bf16[8,256,256]{2,1,0:T(8,128)(2,1)}, bf16[8,256,256]{2,1,0:T(8,128)(2,1)S(1)}, u32[]{:S(2)}, u32[]{:S(2)}) collective-permute-start(bf16[8,256,256]{2,1,0:T(8,128)(2,1)} %bitcast.9), channel_id=1, source_target_pairs={{0,1},{1,0},{2,3},{3,2},{4,5},{5,4},{6,7},{7,6},{8,9},{9,8},{10,11... | collective-permute-start | bytes 3145736 | tf_op jit(solution)/shard_map/ppermute | solution.py:192
  12.6 0.7 copy-done.1
  13.3 0.9 %shard_map.46 = bf16[1024,128]{1,0:T(8,128)(2,1)} custom-call(f32[64,64]{1,0:T(8,128)S(1)} %copy-done.1), custom_call_target="tpu_custom_call" | custom-call | tf_op jit(solution)/shard_map/pallas_call | solution.py:182
  14.3 3.9 %all-to-all-start = ((bf16[32,32,128]{2,1,0:T(8,128)(2,1)}), bf16[32,32,128]{2,1,0:T(8,128)(2,1)S(1)}, u32[]{:S(2)}, u32[]{:S(2)}) async-start(bf16[32,32,128]{2,1,0:T(8,128)(2,1)} %bitcast.3), calls=%async_computation | async-start | bytes 524288 | tf_op jit(solution)/shard_map/all_to_all | solution.py:33
  18.1 0.7 pad_add_fusion
  18.8 1.8 %all-gather = s32[4,4,2]{1,2,0:T(2,128)S(1)} all-gather(s32[2,4,2]{1,2,0:T(2,128)S(1)} %pad_add_fusion), channel_id=2, replica_groups=mesh['blk'=12,'pos'=32,'core'=2] {'core'}, dimensions={0}, use_global_device_ids=true | all-gather | bytes 192 | tf_op jit(solution)/shard_map/all_gather | solution.py:190
  20.6 0.1 copy.17.lists
  20.7 12.3 %collective-permute-start.1 = (s32[2,2,4,2]{3,2,1,0:T(4,128)S(1)}, s32[2,2,4,2]{3,2,1,0:T(4,128)S(1)}, u32[]{:S(2)}, u32[]{:S(2)}) collective-permute-start(s32[2,2,4,2]{3,2,1,0:T(4,128)S(1)} %copy.17.lists), channel_id=1, source_target_pairs={{0,704},{1,641},{2,706},{3,643},{4,708},{5,645},{6,710},{7,647},{8... | collective-permute-start | bytes 392 | tf_op jit(solution)/shard_map/ppermute | solution.py:29
  33.0 2.5 %collective-permute-start = (s32[2,2,4,2]{3,2,1,0:T(4,128)S(1)}, s32[2,2,4,2]{3,2,1,0:T(4,128)S(1)}, u32[]{:S(2)}, u32[]{:S(2)}) collective-permute-start(s32[2,2,4,2]{3,2,1,0:T(4,128)S(1)} %copy.17.lists), channel_id=1, source_target_pairs={{0,576},{1,577},{2,578},{3,579},{4,580},{5,581},{6,582},{7,583},{8... | collective-permute-start | bytes 392 | tf_op jit(solution)/shard_map/ppermute | solution.py:29
  35.5 0.0 all-to-all-done
  35.5 3.9 %all_gather.17.held = bf16[2048,128]{1,0:T(8,128)(2,1)S(1)} all-gather(bf16[1024,128]{1,0:T(8,128)(2,1)S(1)} %bitcast.17), channel_id=1, replica_groups=mesh['blk'=12,'pos'=32,'core'=2] {'core'}, dimensions={0}, use_global_device_ids=true | all-gather | bytes 786432 | tf_op jit(solution)/shard_map/all_gather | solution.py:193
  39.4 0.0 collective-permute-done.2.other
  39.4 0.9 %shard_map.48 = bf16[2,128,256]{2,1,0:T(8,128)(2,1)S(1)} custom-call(s32[2,2,4,2]{3,2,1,0:T(4,128)S(1)} %copy.17.lists, bf16[2048,128]{1,0:T(8,128)(2,1)S(1)} %all_gather.17.held, bf16[8,256,256]{2,1,0:T(8,128)(2,1)S(1)} %bitcast.10, bf16[8,256,256]{2,1,0:T(8,128)(2,1)S(1)} %collective-permute-done.2.other), custom_call_target="tpu_custom_call" | custom-call | tf_op jit(solution)/shard_map/pallas_call | solution.py:195
  40.3 5.7 %collective-permute-start.3 = (bf16[2,128,256]{2,1,0:T(8,128)(2,1)S(1)}, bf16[2,128,256]{2,1,0:T(8,128)(2,1)S(1)}, u32[]{:S(2)}, u32[]{:S(2)}) collective-permute-start(bf16[2,128,256]{2,1,0:T(8,128)(2,1)S(1)} %shard_map.48), channel_id=1, source_target_pairs={{0,704},{1,641},{2,706},{3,643},{4,708},{5,645},{6,710},{7,647},{8... | collective-permute-start | bytes 393224 | tf_op jit(solution)/shard_map/ppermute | solution.py:29
  46.1 0.8 shard_map.50
  46.8 3.5 %collective-permute-start.4 = (bf16[2,128,256]{2,1,0:T(8,128)(2,1)S(1)}, bf16[2,128,256]{2,1,0:T(8,128)(2,1)S(1)}, u32[]{:S(2)}, u32[]{:S(2)}) collective-permute-start(bf16[2,128,256]{2,1,0:T(8,128)(2,1)S(1)} %shard_map.50), channel_id=1, source_target_pairs={{0,64},{1,129},{2,66},{3,131},{4,68},{5,133},{6,70},{7,135},{8,72}... | collective-permute-start | bytes 393224 | tf_op jit(solution)/shard_map/ppermute | solution.py:29
  50.3 1.1 %shard_map.47 = bf16[2,128,256]{2,1,0:T(8,128)(2,1)S(1)} custom-call(s32[2,2,4,2]{3,2,1,0:T(4,128)S(1)} %copy.17.lists, s32[2,2,4,2]{3,2,1,0:T(4,128)S(1)} %collective-permute-done.far3, bf16[2048,128]{1,0:T(8,128)(2,1)S(1)} %all_gather.17.held, bf16[8,256,256]{2,1,0:T(8,128)(2,1)S(1)} %bitcast.11, bf16[8,256,256]{2,1,0:T(8,128)(2,1)S(1)} %collective-permute-done.2.other), custom_call_target="tpu_custom_call" | custom-call | tf_op jit(solution)/shard_map/pallas_call | solution.py:213
  51.4 2.2 %collective-permute-start.5 = (bf16[2,128,256]{2,1,0:T(8,128)(2,1)S(1)}, bf16[2,128,256]{2,1,0:T(8,128)(2,1)S(1)}, u32[]{:S(2)}, u32[]{:S(2)}) collective-permute-start(bf16[2,128,256]{2,1,0:T(8,128)(2,1)S(1)} %shard_map.47), channel_id=1, source_target_pairs={{0,192},{1,577},{2,194},{3,579},{4,196},{5,581},{6,198},{7,583},{8... | collective-permute-start | bytes 393224 | tf_op jit(solution)/shard_map/ppermute | solution.py:29
  53.6 1.1 %shard_map.49.early = f32[16,64,256]{2,1,0:T(8,128)S(1)} custom-call(s32[2,2,4,2]{3,2,1,0:T(4,128)S(1)} %copy.17.lists, s32[2,2,4,2]{3,2,1,0:T(4,128)S(1)} %collective-permute-done.1.far, bf16[2048,128]{1,0:T(8,128)(2,1)S(1)} %all_gather.17.held, bf16[8,256,256]{2,1,0:T(8,128)(2,1)S(1)} %bitcast.12, bf16[2,128,256]{2,1,0:T(8,128)(2,1)S(1)} %collective-permute-done.3.back), custom_call_target="tpu_custom_call" | custom-call | tf_op jit(solution)/shard_map/pallas_call | solution.py:222
  54.7 7.1 %collective-permute-done.4.right = bf16[2,128,256]{2,1,0:T(8,128)(2,1)S(1)} collective-permute-done((bf16[2,128,256]{2,1,0:T(8,128)(2,1)S(1)}, bf16[2,128,256]{2,1,0:T(8,128)(2,1)S(1)}, u32[]{:S(2)}, u32[]{:S(2)}) %collective-permute-start.4) | collective-permute-done | bytes 131104 | tf_op jit(solution)/shard_map/ppermute | solution.py:29
  61.8 1.4 %shard_map.51 = (f32[1024,128]{1,0:T(8,128)S(1)}, bf16[1024,128]{1,0:T(8,128)(2,1)S(1)}, f32[16,64,256]{2,1,0:T(8,128)S(1)}) custom-call(s32[2,2,4,2]{3,2,1,0:T(4,128)S(1)} %copy.17.lists, s32[2,2,4,2]{3,2,1,0:T(4,128)S(1)} %collective-permute-done.far3, f32[16,64,256]{2,1,0:T(8,128)S(1)} %shard_map.49.early, ...), custom_call_target="tpu_custom_call", output_to_operand_aliasing={{2}: (2, {})} | custom-call | tf_op jit(solution)/shard_map/pallas_call | solution.py:230
  63.2 3.0 %all-gather.1 = bf16[2048,128]{1,0:T(8,128)(2,1)S(1)} all-gather(bf16[1024,128]{1,0:T(8,128)(2,1)S(1)} %get-tuple-element.12), channel_id=3, replica_groups=mesh['blk'=12,'pos'=32,'core'=2] {'core'}, dimensions={0}, use_global_device_ids=true | all-gather | bytes 786432 | tf_op jit(solution)/shard_map/all_gather | solution.py:244
  66.3 19.8 %all_to_all.10 = bf16[32,32,128]{2,1,0:T(8,128)(2,1)S(1)} all-to-all(bf16[32,32,128]{2,1,0:T(8,128)(2,1)S(1)} %bitcast.15), channel_id=1, replica_groups=mesh['blk'=12,'pos'=32,'core'=2] {'pos'}, dimensions={0} | all-to-all | bytes 524288 | tf_op jit(solution)/shard_map/all_to_all | solution.py:33
  86.1 0.9 shard_map.53
  (8 shorter events, 0.1 us)
Async XLA Ops:
  0.0 39.4 %copy-start = (bf16[1,1,4,2,256,256]{5,4,3,2,1,0:T(8,128)(2,1)S(1)}, bf16[1,1,4,2,256,256]{5,4,3,2,1,0:T(8,128)(2,1)}, u32[]{:S(2)}) copy-start(bf16[1,1,4,2,256,256]{5,4,3,2,1,0:T(8,128)(2,1)} %param.5) | copy-start | bytes 3145732
  0.0 39.4 %collective-permute-start.2 = (bf16[8,256,256]{2,1,0:T(8,128)(2,1)}, bf16[8,256,256]{2,1,0:T(8,128)(2,1)S(1)}, u32[]{:S(2)}, u32[]{:S(2)}) collective-permute-start(bf16[8,256,256]{2,1,0:T(8,128)(2,1)} %bitcast.9), channel_id=1, source_target_pairs={{0,1},{1,0},{2,3},{3,2},{4,5},{5,4},{6,7},{7,6},{8,9},{9,8},{10,11... | collective-permute-start | bytes 3145736 | tf_op jit(solution)/shard_map/ppermute | solution.py:192
  12.6 0.8 copy-start.1
  14.3 21.2 %all-to-all-start = ((bf16[32,32,128]{2,1,0:T(8,128)(2,1)}), bf16[32,32,128]{2,1,0:T(8,128)(2,1)S(1)}, u32[]{:S(2)}, u32[]{:S(2)}) async-start(bf16[32,32,128]{2,1,0:T(8,128)(2,1)} %bitcast.3), calls=%async_computation | async-start | bytes 524288 | tf_op jit(solution)/shard_map/all_to_all | solution.py:33
  20.7 25.3 %collective-permute-start.1 = (s32[2,2,4,2]{3,2,1,0:T(4,128)S(1)}, s32[2,2,4,2]{3,2,1,0:T(4,128)S(1)}, u32[]{:S(2)}, u32[]{:S(2)}) collective-permute-start(s32[2,2,4,2]{3,2,1,0:T(4,128)S(1)} %copy.17.lists), channel_id=1, source_target_pairs={{0,704},{1,641},{2,706},{3,643},{4,708},{5,645},{6,710},{7,647},{8... | collective-permute-start | bytes 392 | tf_op jit(solution)/shard_map/ppermute | solution.py:29
  33.0 17.3 %collective-permute-start = (s32[2,2,4,2]{3,2,1,0:T(4,128)S(1)}, s32[2,2,4,2]{3,2,1,0:T(4,128)S(1)}, u32[]{:S(2)}, u32[]{:S(2)}) collective-permute-start(s32[2,2,4,2]{3,2,1,0:T(4,128)S(1)} %copy.17.lists), channel_id=1, source_target_pairs={{0,576},{1,577},{2,578},{3,579},{4,580},{5,581},{6,582},{7,583},{8... | collective-permute-start | bytes 392 | tf_op jit(solution)/shard_map/ppermute | solution.py:29
  40.3 13.3 %collective-permute-start.3 = (bf16[2,128,256]{2,1,0:T(8,128)(2,1)S(1)}, bf16[2,128,256]{2,1,0:T(8,128)(2,1)S(1)}, u32[]{:S(2)}, u32[]{:S(2)}) collective-permute-start(bf16[2,128,256]{2,1,0:T(8,128)(2,1)S(1)} %shard_map.48), channel_id=1, source_target_pairs={{0,704},{1,641},{2,706},{3,643},{4,708},{5,645},{6,710},{7,647},{8... | collective-permute-start | bytes 393224 | tf_op jit(solution)/shard_map/ppermute | solution.py:29
  46.8 15.0 %collective-permute-start.4 = (bf16[2,128,256]{2,1,0:T(8,128)(2,1)S(1)}, bf16[2,128,256]{2,1,0:T(8,128)(2,1)S(1)}, u32[]{:S(2)}, u32[]{:S(2)}) collective-permute-start(bf16[2,128,256]{2,1,0:T(8,128)(2,1)S(1)} %shard_map.50), channel_id=1, source_target_pairs={{0,64},{1,129},{2,66},{3,131},{4,68},{5,133},{6,70},{7,135},{8,72}... | collective-permute-start | bytes 393224 | tf_op jit(solution)/shard_map/ppermute | solution.py:29
  51.4 10.4 %collective-permute-start.5 = (bf16[2,128,256]{2,1,0:T(8,128)(2,1)S(1)}, bf16[2,128,256]{2,1,0:T(8,128)(2,1)S(1)}, u32[]{:S(2)}, u32[]{:S(2)}) collective-permute-start(bf16[2,128,256]{2,1,0:T(8,128)(2,1)S(1)} %shard_map.47), channel_id=1, source_target_pairs={{0,192},{1,577},{2,194},{3,579},{4,196},{5,581},{6,198},{7,583},{8... | collective-permute-start | bytes 393224 | tf_op jit(solution)/shard_map/ppermute | solution.py:29

commit v10 on v9

--- a/solution.py
+++ b/solution.py
@@ -72,7 +72,7 @@
     for k in range(SLOTS):
         part = slice(NV * k, NV * (k + 1))
         for core, owner in enumerate((me, 1 - me)):
-            left = dense_block(held, lists[owner, 0, 1 + me, k])
+            left = dense_block(held, lists[owner, 0, 0, 1 + me, k])
             partials[core, part, :] = times(left, shared_block(blocks, other, 1 + me, core, k)).astype(BF16)
 
 
@@ -80,23 +80,23 @@
     me = lax.axis_index("core")
     for k in range(SLOTS):
         for core, owner in enumerate((me, 1 - me)):
-            picked[core, NV * k : NV * (k + 1), :] = dense_block(held, far[owner, 1, 1 + me, k])
-
-
-def third_blocks(lists, far3, held, blocks, other, third):
+            picked[core, NV * k : NV * (k + 1), :] = dense_block(held, far[owner, 0, 1, 1 + me, k])
+
+
+def third_blocks(lists, held, blocks, other, third):
     me = lax.axis_index("core")
 
     @pl.when(me == 0)
     def _():
         for k in range(SLOTS):
             for core in range(2):
-                third[core, NV * k : NV * (k + 1), :] = dense_block(held, far3[core, 1, 3, k])
+                third[core, NV * k : NV * (k + 1), :] = dense_block(held, lists[core, 1, 1, 3, k])
 
     @pl.when(me == 1)
     def _():
         for k in range(SLOTS):
             for core in range(2):
-                left = dense_block(held, lists[1 - core, 0, 3, k])
+                left = dense_block(held, lists[1 - core, 0, 0, 3, k])
                 product = times(left, shared_block(blocks, other, 3, core, k))
                 third[1 - core, NV * k : NV * (k + 1), :] = product.astype(BF16)
 
@@ -106,11 +106,11 @@
     total[...] = jnp.zeros_like(total)
     for k in range(SLOTS):
         part = slice(NV * k, NV * (k + 1))
-        row, col = lists[me, 0, 0, k], lists[me, 1, 0, k]
+        row, col = lists[me, 0, 0, 0, k], lists[me, 0, 1, 0, k]
         total[row] += times_transposed(dense_block(held, col), blocks[k])
         total[col] += times(dense_block(held, row), blocks[k])
         for core, owner in enumerate((me, 1 - me)):
-            total[far[owner, 1, 1 + me, k]] += back[core, part, :].astype(F32)
+            total[far[owner, 0, 1, 1 + me, k]] += back[core, part, :].astype(F32)
 
 
 def packed_rows(total, *outs):
@@ -123,13 +123,13 @@
             out[start : start + CHUNK, :] = jnp.concatenate([part[:32], part[32:]], axis=1).astype(out.dtype)
 
 
-def late_sums(lists, far3, early, blocks, other, right, third, kept, given, total):
+def late_sums(lists, early, blocks, other, right, third, kept, given, total):
     me = lax.axis_index("core")
     for k in range(SLOTS):
         part = slice(NV * k, NV * (k + 1))
         for core, owner in enumerate((me, 1 - me)):
             block = shared_block(blocks, other, 1 + me, core, k)
-            total[lists[owner, 0, 1 + me, k]] += times_transposed(right[core, part, :], block)
+            total[lists[owner, 0, 0, 1 + me, k]] += times_transposed(right[core, part, :], block)
 
     @pl.when(me == 0)
     def _():
@@ -137,13 +137,13 @@
             for core in range(2):
                 came = third[core, NV * k : NV * (k + 1), :]
                 block = shared_block(blocks, other, 3, core, k)
-                total[lists[core, 0, 3, k]] += times_transposed(came, block)
+                total[lists[core, 0, 0, 3, k]] += times_transposed(came, block)
 
     @pl.when(me == 1)
     def _():
         for k in range(SLOTS):
             for core in range(2):
-                total[far3[core, 1, 3, k]] += third[core, NV * k : NV * (k + 1), :].astype(F32)
+                total[lists[core, 1, 1, 3, k]] += third[core, NV * k : NV * (k + 1), :].astype(F32)
 
     @pl.when(me == 0)
     def _():
@@ -179,6 +179,8 @@
 
 def per_device(vectors, blocks, row_blocks, col_blocks):
     stored = blocks.reshape(STEPS * SLOTS, BS, BS)
+    listed = jnp.stack([row_blocks[0, 0], col_blocks[0, 0]])
+    three_on = routed(listed, -3, -3)
     mine = pl.pallas_call(
         prepared,
         out_shape=shape_of((COL // 2 * CHUNK, HALF), BF16),
@@ -186,8 +188,8 @@
         out_specs=VM,
         compiler_params=PARAMS,
     )(vectors)
-    arriving = exchanged(mine, CHUNK, "pos")
-    lists = lax.all_gather(jnp.stack([row_blocks[0, 0], col_blocks[0, 0]]), "core")
+    arriving = exchanged(lax.optimization_barrier((mine, three_on))[0], CHUNK, "pos")
+    lists = lax.all_gather(jnp.stack([listed, three_on]), "core")
     far = routed(lists, -1, -2)
     other = lax.ppermute(stored, "core", [(0, 1), (1, 0)])
     held = lax.all_gather(arriving, "core", tiled=True)
@@ -201,7 +203,6 @@
     )(lists, held, stored, other)
     back = routed(partials, -1, -2)
     later_far, _ = lax.optimization_barrier((far, partials))
-    far3 = routed(lists, -3, -3)
     picked = pl.pallas_call(
         asked_blocks,
         out_shape=two,
@@ -213,10 +214,10 @@
     third = pl.pallas_call(
         third_blocks,
         out_shape=two,
-        in_specs=[SM, SM] + [VM] * 3,
-        out_specs=VM,
-        compiler_params=PARAMS,
-    )(lists, far3, held, stored, other)
+        in_specs=[SM] + [VM] * 3,
+        out_specs=VM,
+        compiler_params=PARAMS,
+    )(lists, held, stored, other)
     third_sent = third
     third = routed(third, 3, -3)
     early = pl.pallas_call(
@@ -230,11 +231,11 @@
     kept, given, _ = pl.pallas_call(
         late_sums,
         out_shape=(shape_of(half, F32), shape_of(half, BF16), shape_of((NBB, NV, BS), F32)),
-        in_specs=[SM] * 2 + [VM] * 5,
+        in_specs=[SM] + [VM] * 5,
         out_specs=(VM,) * 3,
-        input_output_aliases={2: 2},
-        compiler_params=PARAMS,
-    )(lists, far3, early, stored, other, right, third)
+        input_output_aliases={1: 2},
+        compiler_params=PARAMS,
+    )(lists, early, stored, other, right, third)
     chips = pl.pallas_call(
         both_cores,
         out_shape=shape_of(half, BF16),

time: 88.1 us -> 91.6 us (1.040)
  starting transfers between devices: 42.5 us -> 46.1 us
  blocking collectives: 28.5 us -> 26.2 us
  waiting for transfers between devices: 7.16 us -> 8.82 us
    ppermute x5, starting transfers between devices: 26.1 us -> 28.1 us  [routed(): return lax.ppermute(block, AXES, route)]
    ppermute x5, waiting for transfers between devices: 7.15 us -> 8.82 us  [routed(): return lax.ppermute(block, AXES, route)]
    all_to_all x1, blocking collectives: 19.8 us -> 18.3 us  [exchanged(): lax.all_to_all(flat.reshape(-1, rows, HALF), axes, 0, 0, tiled=True)]
    all_to_all x1, starting transfers between devices: 3.87 us -> 5.39 us  [exchanged(): lax.all_to_all(flat.reshape(-1, rows, HALF), axes, 0, 0, tiled=True)]
  transfers between devices with their start and end apart: 7 -> 7, of which waited for: 1 -> 2; matrix products, arithmetic and copies ran while one was open for 1% -> 1% of each run, Pallas kernels for 6% -> 6%
where the time goes in v10:
time: 91.6 us; the launch traced here: 90.5 us
  starting transfers between devices  46.1 us (50%)
  blocking collectives  26.2 us (29%)
  waiting for transfers between devices  8.82 us (10%)
  Pallas kernels  7.66 us (8%)
    ppermute x5, starting transfers between devices, routed(): return lax.ppermute(block, AXES, route)  28.1 us
    all_to_all x1, blocking collectives, exchanged(): lax.all_to_all(flat.reshape(-1, rows, HALF), axes, 0, 0, tiled=True)  18.3 us
    ppermute x1, starting transfers between devices, per_device(): other = lax.ppermute(stored, 'core', [(0, 1), (1, 0)])  12.5 us
    ppermute x5, waiting for transfers between devices, routed(): return lax.ppermute(block, AXES, route)  8.82 us
    all_to_all x1, starting transfers between devices, exchanged(): lax.all_to_all(flat.reshape(-1, rows, HALF), axes, 0, 0, tiled=True)  5.39 us
    all_gather x1, blocking collectives, per_device(): held = lax.all_gather(arriving, 'core', tiled=True)  3.63 us
    all_gather x1, blocking collectives, per_device(): lax.all_gather(given, 'core')  2.27 us
    all_gather x1, blocking collectives, per_device(): lists = lax.all_gather(jnp.stack([listed, three_on]), 'core')  2.07 us
  transfers between devices with their start and end apart: 7, of which 2 were waited for; matrix products, arithmetic and copies ran while one was open for 1% of the time, Pallas kernels for 6%

profile of v10, /device:TPU:1, one launch (start us, length us, event | category | flops | bytes accessed | tf_op | source)
XLA Modules:
  0.0 90.5 jit_solution(16303032099178658190)
XLA Ops:
  0.0 12.5 %collective-permute-start.2 = (bf16[8,256,256]{2,1,0:T(8,128)(2,1)}, bf16[8,256,256]{2,1,0:T(8,128)(2,1)S(1)}, u32[]{:S(2)}, u32[]{:S(2)}) collective-permute-start(bf16[8,256,256]{2,1,0:T(8,128)(2,1)} %bitcast.12), channel_id=1, source_target_pairs={{0,1},{1,0},{2,3},{3,2},{4,5},{5,4},{6,7},{7,6},{8,9},{9,8},{10,11... | collective-permute-start | bytes 3145736 | tf_op jit(solution)/shard_map/ppermute | solution.py:194
  12.6 0.7 fusion
  13.3 1.9 %collective-permute-start = (s32[2,4,2]{1,2,0:T(2,128)S(1)}, s32[2,4,2]{1,2,0:T(2,128)S(1)}, u32[]{:S(2)}, u32[]{:S(2)}) collective-permute-start(s32[2,4,2]{1,2,0:T(2,128)S(1)} %get-tuple-element.16), channel_id=1, source_target_pairs={{0,576},{1,577},{2,578},{3,579},{4,580},{5,581},{6,582},{7,583},{8... | collective-permute-start | bytes 200 | tf_op jit(solution)/shard_map/ppermute | solution.py:29
  15.2 0.0 copy-start.1
  15.2 0.7 copy-done.1
  15.9 0.9 %shard_map.46 = bf16[1024,128]{1,0:T(8,128)(2,1)} custom-call(f32[64,64]{1,0:T(8,128)S(1)} %copy-done.1), custom_call_target="tpu_custom_call" | custom-call | tf_op jit(solution)/shard_map/pallas_call | solution.py:184
  16.9 0.7 collective-permute-done
  17.6 5.4 %all-to-all-start = ((bf16[32,32,128]{2,1,0:T(8,128)(2,1)}), bf16[32,32,128]{2,1,0:T(8,128)(2,1)S(1)}, u32[]{:S(2)}, u32[]{:S(2)}) async-start(bf16[32,32,128]{2,1,0:T(8,128)(2,1)} %bitcast.5), calls=%async_computation | async-start | bytes 524288 | tf_op jit(solution)/shard_map/all_to_all | solution.py:33
  23.0 2.1 %all-gather = s32[4,2,4,2]{2,3,1,0:T(2,128)S(1)} all-gather(s32[2,2,4,2]{2,3,1,0:T(2,128)S(1)} %pad_add_fusion), channel_id=2, replica_groups=mesh['blk'=12,'pos'=32,'core'=2] {'core'}, dimensions={0}, use_global_device_ids=true | all-gather | bytes 384 | tf_op jit(solution)/shard_map/all_gather | solution.py:192
  25.1 0.1 copy.15.lists
  25.2 12.8 %collective-permute-start.1 = (s32[2,2,2,4,2]{4,3,2,1,0:T(4,128)S(1)}, s32[2,2,2,4,2]{4,3,2,1,0:T(4,128)S(1)}, u32[]{:S(2)}, u32[]{:S(2)}) collective-permute-start(s32[2,2,2,4,2]{4,3,2,1,0:T(4,128)S(1)} %copy.15.lists), channel_id=1, source_target_pairs={{0,704},{1,641},{2,706},{3,643},{4,708},{5,645},{6,710},{7,647},{8... | collective-permute-start | bytes 776 | tf_op jit(solution)/shard_map/ppermute | solution.py:29
  38.0 3.6 %all_gather.17.held = bf16[2048,128]{1,0:T(8,128)(2,1)S(1)} all-gather(bf16[1024,128]{1,0:T(8,128)(2,1)S(1)} %bitcast.20), channel_id=1, replica_groups=mesh['blk'=12,'pos'=32,'core'=2] {'core'}, dimensions={0}, use_global_device_ids=true | all-gather | bytes 786432 | tf_op jit(solution)/shard_map/all_gather | solution.py:195
  41.7 1.1 %shard_map.48 = bf16[2,128,256]{2,1,0:T(8,128)(2,1)S(1)} custom-call(s32[2,2,2,4,2]{4,3,2,1,0:T(4,128)S(1)} %copy.15.lists, bf16[2048,128]{1,0:T(8,128)(2,1)S(1)} %all_gather.17.held, bf16[8,256,256]{2,1,0:T(8,128)(2,1)S(1)} %bitcast.13, bf16[8,256,256]{2,1,0:T(8,128)(2,1)S(1)} %collective-permute-done.2.other), custom_call_target="tpu_custom_call" | custom-call | tf_op jit(solution)/shard_map/pallas_call | solution.py:197
  42.7 8.0 %collective-permute-start.3 = (bf16[2,128,256]{2,1,0:T(8,128)(2,1)S(1)}, bf16[2,128,256]{2,1,0:T(8,128)(2,1)S(1)}, u32[]{:S(2)}, u32[]{:S(2)}) collective-permute-start(bf16[2,128,256]{2,1,0:T(8,128)(2,1)S(1)} %shard_map.48), channel_id=1, source_target_pairs={{0,704},{1,641},{2,706},{3,643},{4,708},{5,645},{6,710},{7,647},{8... | collective-permute-start | bytes 393224 | tf_op jit(solution)/shard_map/ppermute | solution.py:29
  50.8 0.9 %shard_map.50 = bf16[2,128,256]{2,1,0:T(8,128)(2,1)S(1)} custom-call(s32[2,2,2,4,2]{4,3,2,1,0:T(4,128)S(1)} %collective-permute-done.1.far, bf16[2048,128]{1,0:T(8,128)(2,1)S(1)} %all_gather.17.held), custom_call_target="tpu_custom_call" | custom-call | tf_op jit(solution)/shard_map/pallas_call | solution.py:206
  51.7 1.9 %collective-permute-start.4 = (bf16[2,128,256]{2,1,0:T(8,128)(2,1)S(1)}, bf16[2,128,256]{2,1,0:T(8,128)(2,1)S(1)}, u32[]{:S(2)}, u32[]{:S(2)}) collective-permute-start(bf16[2,128,256]{2,1,0:T(8,128)(2,1)S(1)} %shard_map.50), channel_id=1, source_target_pairs={{0,64},{1,129},{2,66},{3,131},{4,68},{5,133},{6,70},{7,135},{8,72}... | collective-permute-start | bytes 393224 | tf_op jit(solution)/shard_map/ppermute | solution.py:29
  53.6 1.1 %shard_map.47 = bf16[2,128,256]{2,1,0:T(8,128)(2,1)S(1)} custom-call(s32[2,2,2,4,2]{4,3,2,1,0:T(4,128)S(1)} %copy.15.lists, bf16[2048,128]{1,0:T(8,128)(2,1)S(1)} %all_gather.17.held, bf16[8,256,256]{2,1,0:T(8,128)(2,1)S(1)} %bitcast.14, bf16[8,256,256]{2,1,0:T(8,128)(2,1)S(1)} %collective-permute-done.2.other), custom_call_target="tpu_custom_call" | custom-call | tf_op jit(solution)/shard_map/pallas_call | solution.py:214
  54.7 3.4 %collective-permute-start.5 = (bf16[2,128,256]{2,1,0:T(8,128)(2,1)S(1)}, bf16[2,128,256]{2,1,0:T(8,128)(2,1)S(1)}, u32[]{:S(2)}, u32[]{:S(2)}) collective-permute-start(bf16[2,128,256]{2,1,0:T(8,128)(2,1)S(1)} %shard_map.47), channel_id=1, source_target_pairs={{0,192},{1,577},{2,194},{3,579},{4,196},{5,581},{6,198},{7,583},{8... | collective-permute-start | bytes 393224 | tf_op jit(solution)/shard_map/ppermute | solution.py:29
  58.2 1.4 %shard_map.49.early = f32[16,64,256]{2,1,0:T(8,128)S(1)} custom-call(s32[2,2,2,4,2]{4,3,2,1,0:T(4,128)S(1)} %copy.15.lists, s32[2,2,2,4,2]{4,3,2,1,0:T(4,128)S(1)} %collective-permute-done.1.far, bf16[2048,128]{1,0:T(8,128)(2,1)S(1)} %all_gather.17.held, bf16[8,256,256]{2,1,0:T(8,128)(2,1)S(1)} %bitcast.15, bf16[2,128,256]{2,1,0:T(8,128)(2,1)S(1)} %collective-permute-done.3.back), custom_call_target="tpu_custom_call" | custom-call | tf_op jit(solution)/shard_map/pallas_call | solution.py:223
  59.5 8.1 %collective-permute-done.4.right = bf16[2,128,256]{2,1,0:T(8,128)(2,1)S(1)} collective-permute-done((bf16[2,128,256]{2,1,0:T(8,128)(2,1)S(1)}, bf16[2,128,256]{2,1,0:T(8,128)(2,1)S(1)}, u32[]{:S(2)}, u32[]{:S(2)}) %collective-permute-start.4) | collective-permute-done | bytes 131104 | tf_op jit(solution)/shard_map/ppermute | solution.py:29
  67.7 1.4 %shard_map.51 = (f32[1024,128]{1,0:T(8,128)S(1)}, bf16[1024,128]{1,0:T(8,128)(2,1)S(1)}, f32[16,64,256]{2,1,0:T(8,128)S(1)}) custom-call(s32[2,2,2,4,2]{4,3,2,1,0:T(4,128)S(1)} %copy.15.lists, f32[16,64,256]{2,1,0:T(8,128)S(1)} %shard_map.49.early, bf16[8,256,256]{2,1,0:T(8,128)(2,1)S(1)} %bitcast.16, ...), custom_call_target="tpu_custom_call", output_to_operand_aliasing={{2}: (1, {})} | custom-call | tf_op jit(solution)/shard_map/pallas_call | solution.py:231
  69.1 2.3 %all-gather.1 = bf16[2048,128]{1,0:T(8,128)(2,1)S(1)} all-gather(bf16[1024,128]{1,0:T(8,128)(2,1)S(1)} %get-tuple-element.14), channel_id=3, replica_groups=mesh['blk'=12,'pos'=32,'core'=2] {'core'}, dimensions={0}, use_global_device_ids=true | all-gather | bytes 786432 | tf_op jit(solution)/shard_map/all_gather | solution.py:245
  71.4 18.3 %all_to_all.10 = bf16[32,32,128]{2,1,0:T(8,128)(2,1)S(1)} all-to-all(bf16[32,32,128]{2,1,0:T(8,128)(2,1)S(1)} %bitcast.18), channel_id=1, replica_groups=mesh['blk'=12,'pos'=32,'core'=2] {'pos'}, dimensions={0} | all-to-all | bytes 524288 | tf_op jit(solution)/shard_map/all_to_all | solution.py:33
  89.6 0.9 shard_map.53
  (9 shorter events, 0.1 us)
Async XLA Ops:
  0.0 41.7 %copy-start = (bf16[1,1,4,2,256,256]{5,4,3,2,1,0:T(8,128)(2,1)S(1)}, bf16[1,1,4,2,256,256]{5,4,3,2,1,0:T(8,128)(2,1)}, u32[]{:S(2)}) copy-start(bf16[1,1,4,2,256,256]{5,4,3,2,1,0:T(8,128)(2,1)} %param.5) | copy-start | bytes 3145732
  0.0 41.7 %collective-permute-start.2 = (bf16[8,256,256]{2,1,0:T(8,128)(2,1)}, bf16[8,256,256]{2,1,0:T(8,128)(2,1)S(1)}, u32[]{:S(2)}, u32[]{:S(2)}) collective-permute-start(bf16[8,256,256]{2,1,0:T(8,128)(2,1)} %bitcast.12), channel_id=1, source_target_pairs={{0,1},{1,0},{2,3},{3,2},{4,5},{5,4},{6,7},{7,6},{8,9},{9,8},{10,11... | collective-permute-start | bytes 3145736 | tf_op jit(solution)/shard_map/ppermute | solution.py:194
  13.3 4.3 %collective-permute-start = (s32[2,4,2]{1,2,0:T(2,128)S(1)}, s32[2,4,2]{1,2,0:T(2,128)S(1)}, u32[]{:S(2)}, u32[]{:S(2)}) collective-permute-start(s32[2,4,2]{1,2,0:T(2,128)S(1)} %get-tuple-element.16), channel_id=1, source_target_pairs={{0,576},{1,577},{2,578},{3,579},{4,580},{5,581},{6,582},{7,583},{8... | collective-permute-start | bytes 200 | tf_op jit(solution)/shard_map/ppermute | solution.py:29
  15.2 0.8 copy-start.1
  17.6 20.5 %all-to-all-start = ((bf16[32,32,128]{2,1,0:T(8,128)(2,1)}), bf16[32,32,128]{2,1,0:T(8,128)(2,1)S(1)}, u32[]{:S(2)}, u32[]{:S(2)}) async-start(bf16[32,32,128]{2,1,0:T(8,128)(2,1)} %bitcast.5), calls=%async_computation | async-start | bytes 524288 | tf_op jit(solution)/shard_map/all_to_all | solution.py:33
  25.2 25.6 %collective-permute-start.1 = (s32[2,2,2,4,2]{4,3,2,1,0:T(4,128)S(1)}, s32[2,2,2,4,2]{4,3,2,1,0:T(4,128)S(1)}, u32[]{:S(2)}, u32[]{:S(2)}) collective-permute-start(s32[2,2,2,4,2]{4,3,2,1,0:T(4,128)S(1)} %copy.15.lists), channel_id=1, source_target_pairs={{0,704},{1,641},{2,706},{3,643},{4,708},{5,645},{6,710},{7,647},{8... | collective-permute-start | bytes 776 | tf_op jit(solution)/shard_map/ppermute | solution.py:29
  42.7 15.4 %collective-permute-start.3 = (bf16[2,128,256]{2,1,0:T(8,128)(2,1)S(1)}, bf16[2,128,256]{2,1,0:T(8,128)(2,1)S(1)}, u32[]{:S(2)}, u32[]{:S(2)}) collective-permute-start(bf16[2,128,256]{2,1,0:T(8,128)(2,1)S(1)} %shard_map.48), channel_id=1, source_target_pairs={{0,704},{1,641},{2,706},{3,643},{4,708},{5,645},{6,710},{7,647},{8... | collective-permute-start | bytes 393224 | tf_op jit(solution)/shard_map/ppermute | solution.py:29
  51.7 15.9 %collective-permute-start.4 = (bf16[2,128,256]{2,1,0:T(8,128)(2,1)S(1)}, bf16[2,128,256]{2,1,0:T(8,128)(2,1)S(1)}, u32[]{:S(2)}, u32[]{:S(2)}) collective-permute-start(bf16[2,128,256]{2,1,0:T(8,128)(2,1)S(1)} %shard_map.50), channel_id=1, source_target_pairs={{0,64},{1,129},{2,66},{3,131},{4,68},{5,133},{6,70},{7,135},{8,72}... | collective-permute-start | bytes 393224 | tf_op jit(solution)/shard_map/ppermute | solution.py:29
  54.7 12.9 %collective-permute-start.5 = (bf16[2,128,256]{2,1,0:T(8,128)(2,1)S(1)}, bf16[2,128,256]{2,1,0:T(8,128)(2,1)S(1)}, u32[]{:S(2)}, u32[]{:S(2)}) collective-permute-start(bf16[2,128,256]{2,1,0:T(8,128)(2,1)S(1)} %shard_map.47), channel_id=1, source_target_pairs={{0,192},{1,577},{2,194},{3,579},{4,196},{5,581},{6,198},{7,583},{8... | collective-permute-start | bytes 393224 | tf_op jit(solution)/shard_map/ppermute | solution.py:29

commit v11 on v9

--- a/solution.py
+++ b/solution.py
@@ -114,13 +114,18 @@
 
 
 def packed_rows(total, *outs):
+    first = lax.broadcasted_iota(jnp.int32, (CHUNK, HALF), 1) < 64
     for row in range(NBB):
-        whole = total[row]
-        for q in range(4):
-            part = whole[:, 64 * q : 64 * q + 64]
-            start = (row * 2 + q // 2) * CHUNK
-            out = outs[q % 2]
-            out[start : start + CHUNK, :] = jnp.concatenate([part[:32], part[32:]], axis=1).astype(out.dtype)
+        for half in range(2):
+            whole = total[row, :, half * HALF : (half + 1) * HALF]
+            top, bottom = whole[:CHUNK], whole[CHUNK:]
+            pieces = (
+                jnp.where(first, top, pltpu.roll(bottom, 64, 1)),
+                jnp.where(first, pltpu.roll(top, 64, 1), bottom),
+            )
+            start = (row * 2 + half) * CHUNK
+            for out, piece in zip(outs, pieces):
+                out[start : start + CHUNK, :] = piece.astype(out.dtype)
 
 
 def late_sums(lists, far3, early, blocks, other, right, third, kept, given, total):

time: 88.1 us -> 88.1 us (level)
  no operation moved by 1% of the time
where the time goes in v11:
time: 88.1 us; the launch traced here: 87 us
  starting transfers between devices  42.5 us (48%)
  blocking collectives  28.5 us (32%)
  waiting for transfers between devices  7.16 us (8%)
  Pallas kernels  7.11 us (8%)
    ppermute x5, starting transfers between devices, routed(): return lax.ppermute(block, AXES, route)  26.1 us
    all_to_all x1, blocking collectives, exchanged(): lax.all_to_all(flat.reshape(-1, rows, HALF), axes, 0, 0, tiled=True)  19.8 us
    ppermute x1, starting transfers between devices, per_device(): other = lax.ppermute(stored, 'core', [(0, 1), (1, 0)])  12.5 us
    ppermute x5, waiting for transfers between devices, routed(): return lax.ppermute(block, AXES, route)  7.15 us
    all_gather x1, blocking collectives, per_device(): held = lax.all_gather(arriving, 'core', tiled=True)  3.9 us
    all_to_all x1, starting transfers between devices, exchanged(): lax.all_to_all(flat.reshape(-1, rows, HALF), axes, 0, 0, tiled=True)  3.87 us
    all_gather x1, blocking collectives, per_device(): lax.all_gather(given, 'core')  3.03 us
    all_gather x1, blocking collectives, per_device(): lax.all_gather(jnp.stack([row_blocks[0, 0], col_blocks[0, 0]]), 'core')  1.77 us
  transfers between devices with their start and end apart: 7, of which 1 were waited for; matrix products, arithmetic and copies ran while one was open for 1% of the time, Pallas kernels for 6%

profile of v11, /device:TPU:1, one launch (start us, length us, event | category | flops | bytes accessed | tf_op | source)
XLA Modules:
  0.0 87.0 jit_solution(8914100290149082908)
XLA Ops:
  0.0 12.5 %collective-permute-start.2 = (bf16[8,256,256]{2,1,0:T(8,128)(2,1)}, bf16[8,256,256]{2,1,0:T(8,128)(2,1)S(1)}, u32[]{:S(2)}, u32[]{:S(2)}) collective-permute-start(bf16[8,256,256]{2,1,0:T(8,128)(2,1)} %bitcast.9), channel_id=1, source_target_pairs={{0,1},{1,0},{2,3},{3,2},{4,5},{5,4},{6,7},{7,6},{8,9},{9,8},{10,11... | collective-permute-start | bytes 3145736 | tf_op jit(solution)/shard_map/ppermute | solution.py:197
  12.6 0.7 copy-done.1
  13.3 0.9 %shard_map.46 = bf16[1024,128]{1,0:T(8,128)(2,1)} custom-call(f32[64,64]{1,0:T(8,128)S(1)} %copy-done.1), custom_call_target="tpu_custom_call" | custom-call | tf_op jit(solution)/shard_map/pallas_call | solution.py:187
  14.3 3.9 %all-to-all-start = ((bf16[32,32,128]{2,1,0:T(8,128)(2,1)}), bf16[32,32,128]{2,1,0:T(8,128)(2,1)S(1)}, u32[]{:S(2)}, u32[]{:S(2)}) async-start(bf16[32,32,128]{2,1,0:T(8,128)(2,1)} %bitcast.3), calls=%async_computation | async-start | bytes 524288 | tf_op jit(solution)/shard_map/all_to_all | solution.py:33
  18.1 0.7 pad_add_fusion
  18.8 1.8 %all-gather = s32[4,4,2]{1,2,0:T(2,128)S(1)} all-gather(s32[2,4,2]{1,2,0:T(2,128)S(1)} %pad_add_fusion), channel_id=2, replica_groups=mesh['blk'=12,'pos'=32,'core'=2] {'core'}, dimensions={0}, use_global_device_ids=true | all-gather | bytes 192 | tf_op jit(solution)/shard_map/all_gather | solution.py:195
  20.6 0.1 copy.17.lists
  20.7 12.3 %collective-permute-start.1 = (s32[2,2,4,2]{3,2,1,0:T(4,128)S(1)}, s32[2,2,4,2]{3,2,1,0:T(4,128)S(1)}, u32[]{:S(2)}, u32[]{:S(2)}) collective-permute-start(s32[2,2,4,2]{3,2,1,0:T(4,128)S(1)} %copy.17.lists), channel_id=1, source_target_pairs={{0,704},{1,641},{2,706},{3,643},{4,708},{5,645},{6,710},{7,647},{8... | collective-permute-start | bytes 392 | tf_op jit(solution)/shard_map/ppermute | solution.py:29
  33.0 2.5 %collective-permute-start = (s32[2,2,4,2]{3,2,1,0:T(4,128)S(1)}, s32[2,2,4,2]{3,2,1,0:T(4,128)S(1)}, u32[]{:S(2)}, u32[]{:S(2)}) collective-permute-start(s32[2,2,4,2]{3,2,1,0:T(4,128)S(1)} %copy.17.lists), channel_id=1, source_target_pairs={{0,576},{1,577},{2,578},{3,579},{4,580},{5,581},{6,582},{7,583},{8... | collective-permute-start | bytes 392 | tf_op jit(solution)/shard_map/ppermute | solution.py:29
  35.5 0.0 all-to-all-done
  35.5 3.9 %all_gather.17.held = bf16[2048,128]{1,0:T(8,128)(2,1)S(1)} all-gather(bf16[1024,128]{1,0:T(8,128)(2,1)S(1)} %bitcast.17), channel_id=1, replica_groups=mesh['blk'=12,'pos'=32,'core'=2] {'core'}, dimensions={0}, use_global_device_ids=true | all-gather | bytes 786432 | tf_op jit(solution)/shard_map/all_gather | solution.py:198
  39.4 0.0 collective-permute-done.2.other
  39.4 0.9 %shard_map.48 = bf16[2,128,256]{2,1,0:T(8,128)(2,1)S(1)} custom-call(s32[2,2,4,2]{3,2,1,0:T(4,128)S(1)} %copy.17.lists, bf16[2048,128]{1,0:T(8,128)(2,1)S(1)} %all_gather.17.held, bf16[8,256,256]{2,1,0:T(8,128)(2,1)S(1)} %bitcast.10, bf16[8,256,256]{2,1,0:T(8,128)(2,1)S(1)} %collective-permute-done.2.other), custom_call_target="tpu_custom_call" | custom-call | tf_op jit(solution)/shard_map/pallas_call | solution.py:200
  40.3 5.7 %collective-permute-start.3 = (bf16[2,128,256]{2,1,0:T(8,128)(2,1)S(1)}, bf16[2,128,256]{2,1,0:T(8,128)(2,1)S(1)}, u32[]{:S(2)}, u32[]{:S(2)}) collective-permute-start(bf16[2,128,256]{2,1,0:T(8,128)(2,1)S(1)} %shard_map.48), channel_id=1, source_target_pairs={{0,704},{1,641},{2,706},{3,643},{4,708},{5,645},{6,710},{7,647},{8... | collective-permute-start | bytes 393224 | tf_op jit(solution)/shard_map/ppermute | solution.py:29
  46.1 0.8 shard_map.50
  46.8 3.5 %collective-permute-start.4 = (bf16[2,128,256]{2,1,0:T(8,128)(2,1)S(1)}, bf16[2,128,256]{2,1,0:T(8,128)(2,1)S(1)}, u32[]{:S(2)}, u32[]{:S(2)}) collective-permute-start(bf16[2,128,256]{2,1,0:T(8,128)(2,1)S(1)} %shard_map.50), channel_id=1, source_target_pairs={{0,64},{1,129},{2,66},{3,131},{4,68},{5,133},{6,70},{7,135},{8,72}... | collective-permute-start | bytes 393224 | tf_op jit(solution)/shard_map/ppermute | solution.py:29
  50.3 1.1 %shard_map.47 = bf16[2,128,256]{2,1,0:T(8,128)(2,1)S(1)} custom-call(s32[2,2,4,2]{3,2,1,0:T(4,128)S(1)} %copy.17.lists, s32[2,2,4,2]{3,2,1,0:T(4,128)S(1)} %collective-permute-done.far3, bf16[2048,128]{1,0:T(8,128)(2,1)S(1)} %all_gather.17.held, bf16[8,256,256]{2,1,0:T(8,128)(2,1)S(1)} %bitcast.11, bf16[8,256,256]{2,1,0:T(8,128)(2,1)S(1)} %collective-permute-done.2.other), custom_call_target="tpu_custom_call" | custom-call | tf_op jit(solution)/shard_map/pallas_call | solution.py:218
  51.4 2.2 %collective-permute-start.5 = (bf16[2,128,256]{2,1,0:T(8,128)(2,1)S(1)}, bf16[2,128,256]{2,1,0:T(8,128)(2,1)S(1)}, u32[]{:S(2)}, u32[]{:S(2)}) collective-permute-start(bf16[2,128,256]{2,1,0:T(8,128)(2,1)S(1)} %shard_map.47), channel_id=1, source_target_pairs={{0,192},{1,577},{2,194},{3,579},{4,196},{5,581},{6,198},{7,583},{8... | collective-permute-start | bytes 393224 | tf_op jit(solution)/shard_map/ppermute | solution.py:29
  53.6 1.1 %shard_map.49.early = f32[16,64,256]{2,1,0:T(8,128)S(1)} custom-call(s32[2,2,4,2]{3,2,1,0:T(4,128)S(1)} %copy.17.lists, s32[2,2,4,2]{3,2,1,0:T(4,128)S(1)} %collective-permute-done.1.far, bf16[2048,128]{1,0:T(8,128)(2,1)S(1)} %all_gather.17.held, bf16[8,256,256]{2,1,0:T(8,128)(2,1)S(1)} %bitcast.12, bf16[2,128,256]{2,1,0:T(8,128)(2,1)S(1)} %collective-permute-done.3.back), custom_call_target="tpu_custom_call" | custom-call | tf_op jit(solution)/shard_map/pallas_call | solution.py:227
  54.7 7.1 %collective-permute-done.4.right = bf16[2,128,256]{2,1,0:T(8,128)(2,1)S(1)} collective-permute-done((bf16[2,128,256]{2,1,0:T(8,128)(2,1)S(1)}, bf16[2,128,256]{2,1,0:T(8,128)(2,1)S(1)}, u32[]{:S(2)}, u32[]{:S(2)}) %collective-permute-start.4) | collective-permute-done | bytes 131104 | tf_op jit(solution)/shard_map/ppermute | solution.py:29
  61.8 1.4 %shard_map.51 = (f32[1024,128]{1,0:T(8,128)S(1)}, bf16[1024,128]{1,0:T(8,128)(2,1)S(1)}, f32[16,64,256]{2,1,0:T(8,128)S(1)}) custom-call(s32[2,2,4,2]{3,2,1,0:T(4,128)S(1)} %copy.17.lists, s32[2,2,4,2]{3,2,1,0:T(4,128)S(1)} %collective-permute-done.far3, f32[16,64,256]{2,1,0:T(8,128)S(1)} %shard_map.49.early, ...), custom_call_target="tpu_custom_call", output_to_operand_aliasing={{2}: (2, {})} | custom-call | tf_op jit(solution)/shard_map/pallas_call | solution.py:235
  63.2 3.0 %all-gather.1 = bf16[2048,128]{1,0:T(8,128)(2,1)S(1)} all-gather(bf16[1024,128]{1,0:T(8,128)(2,1)S(1)} %get-tuple-element.12), channel_id=3, replica_groups=mesh['blk'=12,'pos'=32,'core'=2] {'core'}, dimensions={0}, use_global_device_ids=true | all-gather | bytes 786432 | tf_op jit(solution)/shard_map/all_gather | solution.py:249
  66.3 19.8 %all_to_all.10 = bf16[32,32,128]{2,1,0:T(8,128)(2,1)S(1)} all-to-all(bf16[32,32,128]{2,1,0:T(8,128)(2,1)S(1)} %bitcast.15), channel_id=1, replica_groups=mesh['blk'=12,'pos'=32,'core'=2] {'pos'}, dimensions={0} | all-to-all | bytes 524288 | tf_op jit(solution)/shard_map/all_to_all | solution.py:33
  86.1 0.9 shard_map.53
  (8 shorter events, 0.1 us)
Async XLA Ops:
  0.0 39.4 %copy-start = (bf16[1,1,4,2,256,256]{5,4,3,2,1,0:T(8,128)(2,1)S(1)}, bf16[1,1,4,2,256,256]{5,4,3,2,1,0:T(8,128)(2,1)}, u32[]{:S(2)}) copy-start(bf16[1,1,4,2,256,256]{5,4,3,2,1,0:T(8,128)(2,1)} %param.5) | copy-start | bytes 3145732
  0.0 39.4 %collective-permute-start.2 = (bf16[8,256,256]{2,1,0:T(8,128)(2,1)}, bf16[8,256,256]{2,1,0:T(8,128)(2,1)S(1)}, u32[]{:S(2)}, u32[]{:S(2)}) collective-permute-start(bf16[8,256,256]{2,1,0:T(8,128)(2,1)} %bitcast.9), channel_id=1, source_target_pairs={{0,1},{1,0},{2,3},{3,2},{4,5},{5,4},{6,7},{7,6},{8,9},{9,8},{10,11... | collective-permute-start | bytes 3145736 | tf_op jit(solution)/shard_map/ppermute | solution.py:197
  12.6 0.8 copy-start.1
  14.3 21.2 %all-to-all-start = ((bf16[32,32,128]{2,1,0:T(8,128)(2,1)}), bf16[32,32,128]{2,1,0:T(8,128)(2,1)S(1)}, u32[]{:S(2)}, u32[]{:S(2)}) async-start(bf16[32,32,128]{2,1,0:T(8,128)(2,1)} %bitcast.3), calls=%async_computation | async-start | bytes 524288 | tf_op jit(solution)/shard_map/all_to_all | solution.py:33
  20.7 25.3 %collective-permute-start.1 = (s32[2,2,4,2]{3,2,1,0:T(4,128)S(1)}, s32[2,2,4,2]{3,2,1,0:T(4,128)S(1)}, u32[]{:S(2)}, u32[]{:S(2)}) collective-permute-start(s32[2,2,4,2]{3,2,1,0:T(4,128)S(1)} %copy.17.lists), channel_id=1, source_target_pairs={{0,704},{1,641},{2,706},{3,643},{4,708},{5,645},{6,710},{7,647},{8... | collective-permute-start | bytes 392 | tf_op jit(solution)/shard_map/ppermute | solution.py:29
  33.0 17.3 %collective-permute-start = (s32[2,2,4,2]{3,2,1,0:T(4,128)S(1)}, s32[2,2,4,2]{3,2,1,0:T(4,128)S(1)}, u32[]{:S(2)}, u32[]{:S(2)}) collective-permute-start(s32[2,2,4,2]{3,2,1,0:T(4,128)S(1)} %copy.17.lists), channel_id=1, source_target_pairs={{0,576},{1,577},{2,578},{3,579},{4,580},{5,581},{6,582},{7,583},{8... | collective-permute-start | bytes 392 | tf_op jit(solution)/shard_map/ppermute | solution.py:29
  40.3 13.3 %collective-permute-start.3 = (bf16[2,128,256]{2,1,0:T(8,128)(2,1)S(1)}, bf16[2,128,256]{2,1,0:T(8,128)(2,1)S(1)}, u32[]{:S(2)}, u32[]{:S(2)}) collective-permute-start(bf16[2,128,256]{2,1,0:T(8,128)(2,1)S(1)} %shard_map.48), channel_id=1, source_target_pairs={{0,704},{1,641},{2,706},{3,643},{4,708},{5,645},{6,710},{7,647},{8... | collective-permute-start | bytes 393224 | tf_op jit(solution)/shard_map/ppermute | solution.py:29
  46.8 15.0 %collective-permute-start.4 = (bf16[2,128,256]{2,1,0:T(8,128)(2,1)S(1)}, bf16[2,128,256]{2,1,0:T(8,128)(2,1)S(1)}, u32[]{:S(2)}, u32[]{:S(2)}) collective-permute-start(bf16[2,128,256]{2,1,0:T(8,128)(2,1)S(1)} %shard_map.50), channel_id=1, source_target_pairs={{0,64},{1,129},{2,66},{3,131},{4,68},{5,133},{6,70},{7,135},{8,72}... | collective-permute-start | bytes 393224 | tf_op jit(solution)/shard_map/ppermute | solution.py:29
  51.4 10.4 %collective-permute-start.5 = (bf16[2,128,256]{2,1,0:T(8,128)(2,1)S(1)}, bf16[2,128,256]{2,1,0:T(8,128)(2,1)S(1)}, u32[]{:S(2)}, u32[]{:S(2)}) collective-permute-start(bf16[2,128,256]{2,1,0:T(8,128)(2,1)S(1)} %shard_map.47), channel_id=1, source_target_pairs={{0,192},{1,577},{2,194},{3,579},{4,196},{5,581},{6,198},{7,583},{8... | collective-permute-start | bytes 393224 | tf_op jit(solution)/shard_map/ppermute | solution.py:29

commit v12 on v9

--- a/solution.py
+++ b/solution.py
@@ -201,7 +201,8 @@
     )(lists, held, stored, other)
     back = routed(partials, -1, -2)
     later_far, _ = lax.optimization_barrier((far, partials))
-    far3 = routed(lists, -3, -3)
+    later_lists, _ = lax.optimization_barrier((lists, partials))
+    far3 = routed(later_lists, -3, -3)
     picked = pl.pallas_call(
         asked_blocks,
         out_shape=two,
@@ -217,7 +218,6 @@
         out_specs=VM,
         compiler_params=PARAMS,
     )(lists, far3, held, stored, other)
-    third_sent = third
     third = routed(third, 3, -3)
     early = pl.pallas_call(
         early_sums,
@@ -225,7 +225,7 @@
         in_specs=[SM] * 2 + [VM] * 3,
         out_specs=VM,
         compiler_params=PARAMS,
-    )(lists, far, lax.optimization_barrier((held, third_sent))[0], stored, back)
+    )(lists, far, held, stored, back)
     half = (COL // 2 * CHUNK, HALF)
     kept, given, _ = pl.pallas_call(
         late_sums,

time: 88.1 us -> 89.2 us (1.012)
  starting transfers between devices: 42.5 us -> 45 us
  blocking collectives: 28.5 us -> 26.4 us
    ppermute x5, starting transfers between devices: 26.1 us -> 28.5 us  [routed(): return lax.ppermute(block, AXES, route)]
    all_to_all x1, blocking collectives: 19.8 us -> 18.6 us  [exchanged(): lax.all_to_all(flat.reshape(-1, rows, HALF), axes, 0, 0, tiled=True)]
  transfers between devices with their start and end apart: 7 -> 7, of which waited for: 1 -> 1; matrix products, arithmetic and copies ran while one was open for 1% -> 1% of each run, Pallas kernels for 6% -> 5%
where the time goes in v12:
time: 89.2 us; the launch traced here: 88.1 us
  starting transfers between devices  45 us (50%)
  blocking collectives  26.4 us (30%)
  waiting for transfers between devices  7.79 us (9%)
  Pallas kernels  7.11 us (8%)
  local copies, waits for them, and re-layouts  0.98 us (1%)
    ppermute x5, starting transfers between devices, routed(): return lax.ppermute(block, AXES, route)  28.5 us
    all_to_all x1, blocking collectives, exchanged(): lax.all_to_all(flat.reshape(-1, rows, HALF), axes, 0, 0, tiled=True)  18.6 us
    ppermute x1, starting transfers between devices, per_device(): other = lax.ppermute(stored, 'core', [(0, 1), (1, 0)])  12.5 us
    ppermute x5, waiting for transfers between devices, routed(): return lax.ppermute(block, AXES, route)  7.79 us
    all_to_all x1, starting transfers between devices, exchanged(): lax.all_to_all(flat.reshape(-1, rows, HALF), axes, 0, 0, tiled=True)  3.87 us
    all_gather x1, blocking collectives, per_device(): held = lax.all_gather(arriving, 'core', tiled=True)  3.62 us
    all_gather x1, blocking collectives, per_device(): lax.all_gather(given, 'core')  2.5 us
  transfers between devices with their start and end apart: 7, of which 1 were waited for; matrix products, arithmetic and copies ran while one was open for 1% of the time, Pallas kernels for 5%

profile of v12, /device:TPU:1, one launch (start us, length us, event | category | flops | bytes accessed | tf_op | source)
XLA Modules:
  0.0 88.1 jit_solution(8952073728867625287)
XLA Ops:
  0.0 12.5 %collective-permute-start = (bf16[8,256,256]{2,1,0:T(8,128)(2,1)}, bf16[8,256,256]{2,1,0:T(8,128)(2,1)S(1)}, u32[]{:S(2)}, u32[]{:S(2)}) collective-permute-start(bf16[8,256,256]{2,1,0:T(8,128)(2,1)} %bitcast.9), channel_id=1, source_target_pairs={{0,1},{1,0},{2,3},{3,2},{4,5},{5,4},{6,7},{7,6},{8,9},{9,8},{10,11... | collective-permute-start | bytes 3145736 | tf_op jit(solution)/shard_map/ppermute | solution.py:192
  12.6 0.7 copy-done.1
  13.3 0.9 %shard_map.46 = bf16[1024,128]{1,0:T(8,128)(2,1)} custom-call(f32[64,64]{1,0:T(8,128)S(1)} %copy-done.1), custom_call_target="tpu_custom_call" | custom-call | tf_op jit(solution)/shard_map/pallas_call | solution.py:182
  14.3 3.9 %all-to-all-start = ((bf16[32,32,128]{2,1,0:T(8,128)(2,1)}), bf16[32,32,128]{2,1,0:T(8,128)(2,1)S(1)}, u32[]{:S(2)}, u32[]{:S(2)}) async-start(bf16[32,32,128]{2,1,0:T(8,128)(2,1)} %bitcast.3), calls=%async_computation | async-start | bytes 524288 | tf_op jit(solution)/shard_map/all_to_all | solution.py:33
  18.1 0.7 pad_add_fusion
  18.8 1.8 %all-gather = s32[4,4,2]{1,2,0:T(2,128)S(1)} all-gather(s32[2,4,2]{1,2,0:T(2,128)S(1)} %pad_add_fusion), channel_id=2, replica_groups=mesh['blk'=12,'pos'=32,'core'=2] {'core'}, dimensions={0}, use_global_device_ids=true | all-gather | bytes 192 | tf_op jit(solution)/shard_map/all_gather | solution.py:190
  20.6 0.1 copy.17.lists
  20.7 12.3 %collective-permute-start.2 = (s32[2,2,4,2]{3,2,1,0:T(4,128)S(1)}, s32[2,2,4,2]{3,2,1,0:T(4,128)S(1)}, u32[]{:S(2)}, u32[]{:S(2)}) collective-permute-start(s32[2,2,4,2]{3,2,1,0:T(4,128)S(1)} %copy.17.lists), channel_id=1, source_target_pairs={{0,704},{1,641},{2,706},{3,643},{4,708},{5,645},{6,710},{7,647},{8... | collective-permute-start | bytes 392 | tf_op jit(solution)/shard_map/ppermute | solution.py:29
  33.0 3.6 %all_gather.17.held = bf16[2048,128]{1,0:T(8,128)(2,1)S(1)} all-gather(bf16[1024,128]{1,0:T(8,128)(2,1)S(1)} %bitcast.17), channel_id=1, replica_groups=mesh['blk'=12,'pos'=32,'core'=2] {'core'}, dimensions={0}, use_global_device_ids=true | all-gather | bytes 786432 | tf_op jit(solution)/shard_map/all_gather | solution.py:193
  36.6 0.0 collective-permute-done.other
  36.6 0.9 %shard_map.47 = bf16[2,128,256]{2,1,0:T(8,128)(2,1)S(1)} custom-call(s32[2,2,4,2]{3,2,1,0:T(4,128)S(1)} %copy.17.lists, bf16[2048,128]{1,0:T(8,128)(2,1)S(1)} %all_gather.17.held, bf16[8,256,256]{2,1,0:T(8,128)(2,1)S(1)} %bitcast.10, bf16[8,256,256]{2,1,0:T(8,128)(2,1)S(1)} %collective-permute-done.other), custom_call_target="tpu_custom_call" | custom-call | tf_op jit(solution)/shard_map/pallas_call | solution.py:195
  37.6 8.5 %collective-permute-start.3 = (bf16[2,128,256]{2,1,0:T(8,128)(2,1)S(1)}, bf16[2,128,256]{2,1,0:T(8,128)(2,1)S(1)}, u32[]{:S(2)}, u32[]{:S(2)}) collective-permute-start(bf16[2,128,256]{2,1,0:T(8,128)(2,1)S(1)} %shard_map.47), channel_id=1, source_target_pairs={{0,704},{1,641},{2,706},{3,643},{4,708},{5,645},{6,710},{7,647},{8... | collective-permute-start | bytes 393224 | tf_op jit(solution)/shard_map/ppermute | solution.py:29
  46.1 0.1 copy.13
  46.2 2.4 %collective-permute-start.1 = (s32[2,2,4,2]{3,2,1,0:T(4,128)S(1)}, s32[2,2,4,2]{3,2,1,0:T(4,128)S(1)}, u32[]{:S(2)}, u32[]{:S(2)}) collective-permute-start(s32[2,2,4,2]{3,2,1,0:T(4,128)S(1)} %copy.13), channel_id=1, source_target_pairs={{0,576},{1,577},{2,578},{3,579},{4,580},{5,581},{6,582},{7,583},{8... | collective-permute-start | bytes 392 | tf_op jit(solution)/shard_map/ppermute | solution.py:29
  48.6 0.8 shard_map.49
  49.4 2.9 %collective-permute-start.4 = (bf16[2,128,256]{2,1,0:T(8,128)(2,1)S(1)}, bf16[2,128,256]{2,1,0:T(8,128)(2,1)S(1)}, u32[]{:S(2)}, u32[]{:S(2)}) collective-permute-start(bf16[2,128,256]{2,1,0:T(8,128)(2,1)S(1)} %shard_map.49), channel_id=1, source_target_pairs={{0,64},{1,129},{2,66},{3,131},{4,68},{5,133},{6,70},{7,135},{8,72}... | collective-permute-start | bytes 393224 | tf_op jit(solution)/shard_map/ppermute | solution.py:29
  52.3 1.1 %shard_map.50 = bf16[2,128,256]{2,1,0:T(8,128)(2,1)S(1)} custom-call(s32[2,2,4,2]{3,2,1,0:T(4,128)S(1)} %copy.17.lists, s32[2,2,4,2]{3,2,1,0:T(4,128)S(1)} %collective-permute-done.1.far3, bf16[2048,128]{1,0:T(8,128)(2,1)S(1)} %all_gather.17.held, bf16[8,256,256]{2,1,0:T(8,128)(2,1)S(1)} %bitcast.11, bf16[8,256,256]{2,1,0:T(8,128)(2,1)S(1)} %collective-permute-done.other), custom_call_target="tpu_custom_call" | custom-call | tf_op jit(solution)/shard_map/pallas_call | solution.py:214
  53.4 2.5 %collective-permute-start.5 = (bf16[2,128,256]{2,1,0:T(8,128)(2,1)S(1)}, bf16[2,128,256]{2,1,0:T(8,128)(2,1)S(1)}, u32[]{:S(2)}, u32[]{:S(2)}) collective-permute-start(bf16[2,128,256]{2,1,0:T(8,128)(2,1)S(1)} %shard_map.50), channel_id=1, source_target_pairs={{0,192},{1,577},{2,194},{3,579},{4,196},{5,581},{6,198},{7,583},{8... | collective-permute-start | bytes 393224 | tf_op jit(solution)/shard_map/ppermute | solution.py:29
  55.9 1.1 %shard_map.48.early = f32[16,64,256]{2,1,0:T(8,128)S(1)} custom-call(s32[2,2,4,2]{3,2,1,0:T(4,128)S(1)} %copy.17.lists, s32[2,2,4,2]{3,2,1,0:T(4,128)S(1)} %collective-permute-done.2.far, bf16[2048,128]{1,0:T(8,128)(2,1)S(1)} %all_gather.17.held, bf16[8,256,256]{2,1,0:T(8,128)(2,1)S(1)} %bitcast.12, bf16[2,128,256]{2,1,0:T(8,128)(2,1)S(1)} %collective-permute-done.3.back), custom_call_target="tpu_custom_call" | custom-call | tf_op jit(solution)/shard_map/pallas_call | solution.py:222
  57.0 7.8 %collective-permute-done.4.right = bf16[2,128,256]{2,1,0:T(8,128)(2,1)S(1)} collective-permute-done((bf16[2,128,256]{2,1,0:T(8,128)(2,1)S(1)}, bf16[2,128,256]{2,1,0:T(8,128)(2,1)S(1)}, u32[]{:S(2)}, u32[]{:S(2)}) %collective-permute-start.4) | collective-permute-done | bytes 131104 | tf_op jit(solution)/shard_map/ppermute | solution.py:29
  64.8 1.4 %shard_map.51 = (f32[1024,128]{1,0:T(8,128)S(1)}, bf16[1024,128]{1,0:T(8,128)(2,1)S(1)}, f32[16,64,256]{2,1,0:T(8,128)S(1)}) custom-call(s32[2,2,4,2]{3,2,1,0:T(4,128)S(1)} %copy.17.lists, s32[2,2,4,2]{3,2,1,0:T(4,128)S(1)} %collective-permute-done.1.far3, f32[16,64,256]{2,1,0:T(8,128)S(1)} %shard_map.48.early, ...), custom_call_target="tpu_custom_call", output_to_operand_aliasing={{2}: (2, {})} | custom-call | tf_op jit(solution)/shard_map/pallas_call | solution.py:230
  66.1 2.5 %all-gather.1 = bf16[2048,128]{1,0:T(8,128)(2,1)S(1)} all-gather(bf16[1024,128]{1,0:T(8,128)(2,1)S(1)} %get-tuple-element.12), channel_id=3, replica_groups=mesh['blk'=12,'pos'=32,'core'=2] {'core'}, dimensions={0}, use_global_device_ids=true | all-gather | bytes 786432 | tf_op jit(solution)/shard_map/all_gather | solution.py:244
  68.7 18.6 %all_to_all.10 = bf16[32,32,128]{2,1,0:T(8,128)(2,1)S(1)} all-to-all(bf16[32,32,128]{2,1,0:T(8,128)(2,1)S(1)} %bitcast.15), channel_id=1, replica_groups=mesh['blk'=12,'pos'=32,'core'=2] {'pos'}, dimensions={0} | all-to-all | bytes 524288 | tf_op jit(solution)/shard_map/all_to_all | solution.py:33
  87.3 0.9 shard_map.53
  (9 shorter events, 0.1 us)
Async XLA Ops:
  0.0 36.6 %copy-start = (bf16[1,1,4,2,256,256]{5,4,3,2,1,0:T(8,128)(2,1)S(1)}, bf16[1,1,4,2,256,256]{5,4,3,2,1,0:T(8,128)(2,1)}, u32[]{:S(2)}) copy-start(bf16[1,1,4,2,256,256]{5,4,3,2,1,0:T(8,128)(2,1)} %param.5) | copy-start | bytes 3145732
  0.0 36.6 %collective-permute-start = (bf16[8,256,256]{2,1,0:T(8,128)(2,1)}, bf16[8,256,256]{2,1,0:T(8,128)(2,1)S(1)}, u32[]{:S(2)}, u32[]{:S(2)}) collective-permute-start(bf16[8,256,256]{2,1,0:T(8,128)(2,1)} %bitcast.9), channel_id=1, source_target_pairs={{0,1},{1,0},{2,3},{3,2},{4,5},{5,4},{6,7},{7,6},{8,9},{9,8},{10,11... | collective-permute-start | bytes 3145736 | tf_op jit(solution)/shard_map/ppermute | solution.py:192
  12.6 0.8 copy-start.1
  14.3 18.8 %all-to-all-start = ((bf16[32,32,128]{2,1,0:T(8,128)(2,1)}), bf16[32,32,128]{2,1,0:T(8,128)(2,1)S(1)}, u32[]{:S(2)}, u32[]{:S(2)}) async-start(bf16[32,32,128]{2,1,0:T(8,128)(2,1)} %bitcast.3), calls=%async_computation | async-start | bytes 524288 | tf_op jit(solution)/shard_map/all_to_all | solution.py:33
  20.7 25.3 %collective-permute-start.2 = (s32[2,2,4,2]{3,2,1,0:T(4,128)S(1)}, s32[2,2,4,2]{3,2,1,0:T(4,128)S(1)}, u32[]{:S(2)}, u32[]{:S(2)}) collective-permute-start(s32[2,2,4,2]{3,2,1,0:T(4,128)S(1)} %copy.17.lists), channel_id=1, source_target_pairs={{0,704},{1,641},{2,706},{3,643},{4,708},{5,645},{6,710},{7,647},{8... | collective-permute-start | bytes 392 | tf_op jit(solution)/shard_map/ppermute | solution.py:29
  37.6 18.3 %collective-permute-start.3 = (bf16[2,128,256]{2,1,0:T(8,128)(2,1)S(1)}, bf16[2,128,256]{2,1,0:T(8,128)(2,1)S(1)}, u32[]{:S(2)}, u32[]{:S(2)}) collective-permute-start(bf16[2,128,256]{2,1,0:T(8,128)(2,1)S(1)} %shard_map.47), channel_id=1, source_target_pairs={{0,704},{1,641},{2,706},{3,643},{4,708},{5,645},{6,710},{7,647},{8... | collective-permute-start | bytes 393224 | tf_op jit(solution)/shard_map/ppermute | solution.py:29
  46.2 6.1 %collective-permute-start.1 = (s32[2,2,4,2]{3,2,1,0:T(4,128)S(1)}, s32[2,2,4,2]{3,2,1,0:T(4,128)S(1)}, u32[]{:S(2)}, u32[]{:S(2)}) collective-permute-start(s32[2,2,4,2]{3,2,1,0:T(4,128)S(1)} %copy.13), channel_id=1, source_target_pairs={{0,576},{1,577},{2,578},{3,579},{4,580},{5,581},{6,582},{7,583},{8... | collective-permute-start | bytes 392 | tf_op jit(solution)/shard_map/ppermute | solution.py:29
  49.4 15.3 %collective-permute-start.4 = (bf16[2,128,256]{2,1,0:T(8,128)(2,1)S(1)}, bf16[2,128,256]{2,1,0:T(8,128)(2,1)S(1)}, u32[]{:S(2)}, u32[]{:S(2)}) collective-permute-start(bf16[2,128,256]{2,1,0:T(8,128)(2,1)S(1)} %shard_map.49), channel_id=1, source_target_pairs={{0,64},{1,129},{2,66},{3,131},{4,68},{5,133},{6,70},{7,135},{8,72}... | collective-permute-start | bytes 393224 | tf_op jit(solution)/shard_map/ppermute | solution.py:29
  53.4 11.4 %collective-permute-start.5 = (bf16[2,128,256]{2,1,0:T(8,128)(2,1)S(1)}, bf16[2,128,256]{2,1,0:T(8,128)(2,1)S(1)}, u32[]{:S(2)}, u32[]{:S(2)}) collective-permute-start(bf16[2,128,256]{2,1,0:T(8,128)(2,1)S(1)} %shard_map.50), channel_id=1, source_target_pairs={{0,192},{1,577},{2,194},{3,579},{4,196},{5,581},{6,198},{7,583},{8... | collective-permute-start | bytes 393224 | tf_op jit(solution)/shard_map/ppermute | solution.py:29

commit v13 on v9

--- a/solution.py
+++ b/solution.py
@@ -55,8 +55,9 @@
     return lax.dot_general(left, block, (((1,), (1,)), ((), ())), preferred_element_type=F32)
 
 
-def prepared(vectors, out):
-    rows = vectors[...]
+def prepared(vectors, out, held_rows):
+    pltpu.sync_copy(vectors, held_rows)
+    rows = held_rows[...]
     turned = jnp.transpose(jnp.concatenate([rows, rows], axis=1))
     packed = jnp.concatenate([turned[:32], turned[32:64]], axis=1).astype(BF16)
     for i in range(COL // 2):
@@ -182,8 +183,9 @@
     mine = pl.pallas_call(
         prepared,
         out_shape=shape_of((COL // 2 * CHUNK, HALF), BF16),
-        in_specs=[VM],
-        out_specs=VM,
+        in_specs=[pl.BlockSpec(memory_space=pl.ANY)],
+        out_specs=VM,
+        scratch_shapes=[pltpu.VMEM((64, NV), F32)],
         compiler_params=PARAMS,
     )(vectors)
     arriving = exchanged(mine, CHUNK, "pos")

time: 88.1 us -> 88.1 us (level)
  no operation moved by 1% of the time
where the time goes in v13:
time: 88.1 us; the launch traced here: 87 us
  starting transfers between devices  42.5 us (48%)
  blocking collectives  28.5 us (32%)
  waiting for transfers between devices  7.16 us (8%)
  Pallas kernels  7.13 us (8%)
    ppermute x5, starting transfers between devices, routed(): return lax.ppermute(block, AXES, route)  26.1 us
    all_to_all x1, blocking collectives, exchanged(): lax.all_to_all(flat.reshape(-1, rows, HALF), axes, 0, 0, tiled=True)  19.8 us
    ppermute x1, starting transfers between devices, per_device(): other = lax.ppermute(stored, 'core', [(0, 1), (1, 0)])  12.5 us
    ppermute x5, waiting for transfers between devices, routed(): return lax.ppermute(block, AXES, route)  7.15 us
    all_gather x1, blocking collectives, per_device(): held = lax.all_gather(arriving, 'core', tiled=True)  3.9 us
    all_to_all x1, starting transfers between devices, exchanged(): lax.all_to_all(flat.reshape(-1, rows, HALF), axes, 0, 0, tiled=True)  3.87 us
    all_gather x1, blocking collectives, per_device(): lax.all_gather(given, 'core')  3.02 us
    all_gather x1, blocking collectives, per_device(): lax.all_gather(jnp.stack([row_blocks[0, 0], col_blocks[0, 0]]), 'core')  1.77 us
  transfers between devices with their start and end apart: 7, of which 1 were waited for; matrix products, arithmetic and copies ran while one was open for 1% of the time, Pallas kernels for 6%

profile of v13, /device:TPU:1, one launch (start us, length us, event | category | flops | bytes accessed | tf_op | source)
XLA Modules:
  0.0 87.0 jit_solution(16992807177672911256)
XLA Ops:
  0.0 12.5 %collective-permute-start.2 = (bf16[8,256,256]{2,1,0:T(8,128)(2,1)}, bf16[8,256,256]{2,1,0:T(8,128)(2,1)S(1)}, u32[]{:S(2)}, u32[]{:S(2)}) collective-permute-start(bf16[8,256,256]{2,1,0:T(8,128)(2,1)} %bitcast.9), channel_id=1, source_target_pairs={{0,1},{1,0},{2,3},{3,2},{4,5},{5,4},{6,7},{7,6},{8,9},{9,8},{10,11... | collective-permute-start | bytes 3145736 | tf_op jit(solution)/shard_map/ppermute | solution.py:194
  12.6 0.7 copy-done.1
  13.3 1.0 %shard_map.46 = bf16[1024,128]{1,0:T(8,128)(2,1)} custom-call(f32[64,64]{1,0:T(8,128)S(1)} %copy-done.1), custom_call_target="tpu_custom_call" | custom-call | tf_op jit(solution)/shard_map/pallas_call | solution.py:183
  14.3 3.9 %all-to-all-start = ((bf16[32,32,128]{2,1,0:T(8,128)(2,1)}), bf16[32,32,128]{2,1,0:T(8,128)(2,1)S(1)}, u32[]{:S(2)}, u32[]{:S(2)}) async-start(bf16[32,32,128]{2,1,0:T(8,128)(2,1)} %bitcast.3), calls=%async_computation | async-start | bytes 524288 | tf_op jit(solution)/shard_map/all_to_all | solution.py:33
  18.1 0.7 pad_add_fusion
  18.9 1.8 %all-gather = s32[4,4,2]{1,2,0:T(2,128)S(1)} all-gather(s32[2,4,2]{1,2,0:T(2,128)S(1)} %pad_add_fusion), channel_id=2, replica_groups=mesh['blk'=12,'pos'=32,'core'=2] {'core'}, dimensions={0}, use_global_device_ids=true | all-gather | bytes 192 | tf_op jit(solution)/shard_map/all_gather | solution.py:192
  20.6 0.1 copy.17.lists
  20.7 12.3 %collective-permute-start.1 = (s32[2,2,4,2]{3,2,1,0:T(4,128)S(1)}, s32[2,2,4,2]{3,2,1,0:T(4,128)S(1)}, u32[]{:S(2)}, u32[]{:S(2)}) collective-permute-start(s32[2,2,4,2]{3,2,1,0:T(4,128)S(1)} %copy.17.lists), channel_id=1, source_target_pairs={{0,704},{1,641},{2,706},{3,643},{4,708},{5,645},{6,710},{7,647},{8... | collective-permute-start | bytes 392 | tf_op jit(solution)/shard_map/ppermute | solution.py:29
  33.0 2.5 %collective-permute-start = (s32[2,2,4,2]{3,2,1,0:T(4,128)S(1)}, s32[2,2,4,2]{3,2,1,0:T(4,128)S(1)}, u32[]{:S(2)}, u32[]{:S(2)}) collective-permute-start(s32[2,2,4,2]{3,2,1,0:T(4,128)S(1)} %copy.17.lists), channel_id=1, source_target_pairs={{0,576},{1,577},{2,578},{3,579},{4,580},{5,581},{6,582},{7,583},{8... | collective-permute-start | bytes 392 | tf_op jit(solution)/shard_map/ppermute | solution.py:29
  35.5 0.0 all-to-all-done
  35.5 3.9 %all_gather.17.held = bf16[2048,128]{1,0:T(8,128)(2,1)S(1)} all-gather(bf16[1024,128]{1,0:T(8,128)(2,1)S(1)} %bitcast.17), channel_id=1, replica_groups=mesh['blk'=12,'pos'=32,'core'=2] {'core'}, dimensions={0}, use_global_device_ids=true | all-gather | bytes 786432 | tf_op jit(solution)/shard_map/all_gather | solution.py:195
  39.4 0.0 collective-permute-done.2.other
  39.4 0.9 %shard_map.48 = bf16[2,128,256]{2,1,0:T(8,128)(2,1)S(1)} custom-call(s32[2,2,4,2]{3,2,1,0:T(4,128)S(1)} %copy.17.lists, bf16[2048,128]{1,0:T(8,128)(2,1)S(1)} %all_gather.17.held, bf16[8,256,256]{2,1,0:T(8,128)(2,1)S(1)} %bitcast.10, bf16[8,256,256]{2,1,0:T(8,128)(2,1)S(1)} %collective-permute-done.2.other), custom_call_target="tpu_custom_call" | custom-call | tf_op jit(solution)/shard_map/pallas_call | solution.py:197
  40.3 5.7 %collective-permute-start.3 = (bf16[2,128,256]{2,1,0:T(8,128)(2,1)S(1)}, bf16[2,128,256]{2,1,0:T(8,128)(2,1)S(1)}, u32[]{:S(2)}, u32[]{:S(2)}) collective-permute-start(bf16[2,128,256]{2,1,0:T(8,128)(2,1)S(1)} %shard_map.48), channel_id=1, source_target_pairs={{0,704},{1,641},{2,706},{3,643},{4,708},{5,645},{6,710},{7,647},{8... | collective-permute-start | bytes 393224 | tf_op jit(solution)/shard_map/ppermute | solution.py:29
  46.1 0.8 shard_map.50
  46.9 3.5 %collective-permute-start.4 = (bf16[2,128,256]{2,1,0:T(8,128)(2,1)S(1)}, bf16[2,128,256]{2,1,0:T(8,128)(2,1)S(1)}, u32[]{:S(2)}, u32[]{:S(2)}) collective-permute-start(bf16[2,128,256]{2,1,0:T(8,128)(2,1)S(1)} %shard_map.50), channel_id=1, source_target_pairs={{0,64},{1,129},{2,66},{3,131},{4,68},{5,133},{6,70},{7,135},{8,72}... | collective-permute-start | bytes 393224 | tf_op jit(solution)/shard_map/ppermute | solution.py:29
  50.3 1.1 %shard_map.47 = bf16[2,128,256]{2,1,0:T(8,128)(2,1)S(1)} custom-call(s32[2,2,4,2]{3,2,1,0:T(4,128)S(1)} %copy.17.lists, s32[2,2,4,2]{3,2,1,0:T(4,128)S(1)} %collective-permute-done.far3, bf16[2048,128]{1,0:T(8,128)(2,1)S(1)} %all_gather.17.held, bf16[8,256,256]{2,1,0:T(8,128)(2,1)S(1)} %bitcast.11, bf16[8,256,256]{2,1,0:T(8,128)(2,1)S(1)} %collective-permute-done.2.other), custom_call_target="tpu_custom_call" | custom-call | tf_op jit(solution)/shard_map/pallas_call | solution.py:215
  51.4 2.2 %collective-permute-start.5 = (bf16[2,128,256]{2,1,0:T(8,128)(2,1)S(1)}, bf16[2,128,256]{2,1,0:T(8,128)(2,1)S(1)}, u32[]{:S(2)}, u32[]{:S(2)}) collective-permute-start(bf16[2,128,256]{2,1,0:T(8,128)(2,1)S(1)} %shard_map.47), channel_id=1, source_target_pairs={{0,192},{1,577},{2,194},{3,579},{4,196},{5,581},{6,198},{7,583},{8... | collective-permute-start | bytes 393224 | tf_op jit(solution)/shard_map/ppermute | solution.py:29
  53.6 1.1 %shard_map.49.early = f32[16,64,256]{2,1,0:T(8,128)S(1)} custom-call(s32[2,2,4,2]{3,2,1,0:T(4,128)S(1)} %copy.17.lists, s32[2,2,4,2]{3,2,1,0:T(4,128)S(1)} %collective-permute-done.1.far, bf16[2048,128]{1,0:T(8,128)(2,1)S(1)} %all_gather.17.held, bf16[8,256,256]{2,1,0:T(8,128)(2,1)S(1)} %bitcast.12, bf16[2,128,256]{2,1,0:T(8,128)(2,1)S(1)} %collective-permute-done.3.back), custom_call_target="tpu_custom_call" | custom-call | tf_op jit(solution)/shard_map/pallas_call | solution.py:224
  54.7 7.1 %collective-permute-done.4.right = bf16[2,128,256]{2,1,0:T(8,128)(2,1)S(1)} collective-permute-done((bf16[2,128,256]{2,1,0:T(8,128)(2,1)S(1)}, bf16[2,128,256]{2,1,0:T(8,128)(2,1)S(1)}, u32[]{:S(2)}, u32[]{:S(2)}) %collective-permute-start.4) | collective-permute-done | bytes 131104 | tf_op jit(solution)/shard_map/ppermute | solution.py:29
  61.8 1.4 %shard_map.51 = (f32[1024,128]{1,0:T(8,128)S(1)}, bf16[1024,128]{1,0:T(8,128)(2,1)S(1)}, f32[16,64,256]{2,1,0:T(8,128)S(1)}) custom-call(s32[2,2,4,2]{3,2,1,0:T(4,128)S(1)} %copy.17.lists, s32[2,2,4,2]{3,2,1,0:T(4,128)S(1)} %collective-permute-done.far3, f32[16,64,256]{2,1,0:T(8,128)S(1)} %shard_map.49.early, ...), custom_call_target="tpu_custom_call", output_to_operand_aliasing={{2}: (2, {})} | custom-call | tf_op jit(solution)/shard_map/pallas_call | solution.py:232
  63.3 3.0 %all-gather.1 = bf16[2048,128]{1,0:T(8,128)(2,1)S(1)} all-gather(bf16[1024,128]{1,0:T(8,128)(2,1)S(1)} %get-tuple-element.12), channel_id=3, replica_groups=mesh['blk'=12,'pos'=32,'core'=2] {'core'}, dimensions={0}, use_global_device_ids=true | all-gather | bytes 786432 | tf_op jit(solution)/shard_map/all_gather | solution.py:246
  66.3 19.8 %all_to_all.10 = bf16[32,32,128]{2,1,0:T(8,128)(2,1)S(1)} all-to-all(bf16[32,32,128]{2,1,0:T(8,128)(2,1)S(1)} %bitcast.15), channel_id=1, replica_groups=mesh['blk'=12,'pos'=32,'core'=2] {'pos'}, dimensions={0} | all-to-all | bytes 524288 | tf_op jit(solution)/shard_map/all_to_all | solution.py:33
  86.1 0.9 shard_map.53
  (8 shorter events, 0.1 us)
Async XLA Ops:
  0.0 39.4 %copy-start = (bf16[1,1,4,2,256,256]{5,4,3,2,1,0:T(8,128)(2,1)S(1)}, bf16[1,1,4,2,256,256]{5,4,3,2,1,0:T(8,128)(2,1)}, u32[]{:S(2)}) copy-start(bf16[1,1,4,2,256,256]{5,4,3,2,1,0:T(8,128)(2,1)} %param.5) | copy-start | bytes 3145732
  0.0 39.4 %collective-permute-start.2 = (bf16[8,256,256]{2,1,0:T(8,128)(2,1)}, bf16[8,256,256]{2,1,0:T(8,128)(2,1)S(1)}, u32[]{:S(2)}, u32[]{:S(2)}) collective-permute-start(bf16[8,256,256]{2,1,0:T(8,128)(2,1)} %bitcast.9), channel_id=1, source_target_pairs={{0,1},{1,0},{2,3},{3,2},{4,5},{5,4},{6,7},{7,6},{8,9},{9,8},{10,11... | collective-permute-start | bytes 3145736 | tf_op jit(solution)/shard_map/ppermute | solution.py:194
  12.6 0.8 copy-start.1
  14.3 21.2 %all-to-all-start = ((bf16[32,32,128]{2,1,0:T(8,128)(2,1)}), bf16[32,32,128]{2,1,0:T(8,128)(2,1)S(1)}, u32[]{:S(2)}, u32[]{:S(2)}) async-start(bf16[32,32,128]{2,1,0:T(8,128)(2,1)} %bitcast.3), calls=%async_computation | async-start | bytes 524288 | tf_op jit(solution)/shard_map/all_to_all | solution.py:33
  20.7 25.3 %collective-permute-start.1 = (s32[2,2,4,2]{3,2,1,0:T(4,128)S(1)}, s32[2,2,4,2]{3,2,1,0:T(4,128)S(1)}, u32[]{:S(2)}, u32[]{:S(2)}) collective-permute-start(s32[2,2,4,2]{3,2,1,0:T(4,128)S(1)} %copy.17.lists), channel_id=1, source_target_pairs={{0,704},{1,641},{2,706},{3,643},{4,708},{5,645},{6,710},{7,647},{8... | collective-permute-start | bytes 392 | tf_op jit(solution)/shard_map/ppermute | solution.py:29
  33.0 17.3 %collective-permute-start = (s32[2,2,4,2]{3,2,1,0:T(4,128)S(1)}, s32[2,2,4,2]{3,2,1,0:T(4,128)S(1)}, u32[]{:S(2)}, u32[]{:S(2)}) collective-permute-start(s32[2,2,4,2]{3,2,1,0:T(4,128)S(1)} %copy.17.lists), channel_id=1, source_target_pairs={{0,576},{1,577},{2,578},{3,579},{4,580},{5,581},{6,582},{7,583},{8... | collective-permute-start | bytes 392 | tf_op jit(solution)/shard_map/ppermute | solution.py:29
  40.3 13.3 %collective-permute-start.3 = (bf16[2,128,256]{2,1,0:T(8,128)(2,1)S(1)}, bf16[2,128,256]{2,1,0:T(8,128)(2,1)S(1)}, u32[]{:S(2)}, u32[]{:S(2)}) collective-permute-start(bf16[2,128,256]{2,1,0:T(8,128)(2,1)S(1)} %shard_map.48), channel_id=1, source_target_pairs={{0,704},{1,641},{2,706},{3,643},{4,708},{5,645},{6,710},{7,647},{8... | collective-permute-start | bytes 393224 | tf_op jit(solution)/shard_map/ppermute | solution.py:29
  46.9 15.0 %collective-permute-start.4 = (bf16[2,128,256]{2,1,0:T(8,128)(2,1)S(1)}, bf16[2,128,256]{2,1,0:T(8,128)(2,1)S(1)}, u32[]{:S(2)}, u32[]{:S(2)}) collective-permute-start(bf16[2,128,256]{2,1,0:T(8,128)(2,1)S(1)} %shard_map.50), channel_id=1, source_target_pairs={{0,64},{1,129},{2,66},{3,131},{4,68},{5,133},{6,70},{7,135},{8,72}... | collective-permute-start | bytes 393224 | tf_op jit(solution)/shard_map/ppermute | solution.py:29
  51.4 10.4 %collective-permute-start.5 = (bf16[2,128,256]{2,1,0:T(8,128)(2,1)S(1)}, bf16[2,128,256]{2,1,0:T(8,128)(2,1)S(1)}, u32[]{:S(2)}, u32[]{:S(2)}) collective-permute-start(bf16[2,128,256]{2,1,0:T(8,128)(2,1)S(1)} %shard_map.47), channel_id=1, source_target_pairs={{0,192},{1,577},{2,194},{3,579},{4,196},{5,581},{6,198},{7,583},{8... | collective-permute-start | bytes 393224 | tf_op jit(solution)/shard_map/ppermute | solution.py:29

commit v14 on v9

--- a/solution.py
+++ b/solution.py
@@ -37,8 +37,7 @@
 def dense_block(held, index):
     tops, bottoms = [], []
     for quarter in range(4):
-        place = (quarter % 2) * (COL // 2) + index * 2 + quarter // 2
-        start = pl.multiple_of(place * CHUNK, CHUNK)
+        start = pl.multiple_of((index * 4 + quarter) * CHUNK, CHUNK)
         piece = held[pl.ds(start, CHUNK), :]
         tops.append(piece[:, :64])
         bottoms.append(piece[:, 64:])
@@ -59,7 +58,7 @@
     rows = vectors[...]
     turned = jnp.transpose(jnp.concatenate([rows, rows], axis=1))
     packed = jnp.concatenate([turned[:32], turned[32:64]], axis=1).astype(BF16)
-    for i in range(COL // 2):
+    for i in range(COL):
         out[i * CHUNK : (i + 1) * CHUNK, :] = packed
 
 
@@ -181,16 +180,15 @@
     stored = blocks.reshape(STEPS * SLOTS, BS, BS)
     mine = pl.pallas_call(
         prepared,
-        out_shape=shape_of((COL // 2 * CHUNK, HALF), BF16),
+        out_shape=shape_of((COL * CHUNK, HALF), BF16),
         in_specs=[VM],
         out_specs=VM,
         compiler_params=PARAMS,
     )(vectors)
-    arriving = exchanged(mine, CHUNK, "pos")
+    held = exchanged(mine, CHUNK, ("pos", "core"))
     lists = lax.all_gather(jnp.stack([row_blocks[0, 0], col_blocks[0, 0]]), "core")
     far = routed(lists, -1, -2)
     other = lax.ppermute(stored, "core", [(0, 1), (1, 0)])
-    held = lax.all_gather(arriving, "core", tiled=True)
     two = shape_of((2, SLOTS * NV, BS), BF16)
     partials = pl.pallas_call(
         transposed_products,

time: 88.1 us -> 88.5 us (level)
  starting transfers between devices: 42.5 us -> 47.2 us
  blocking collectives: 28.5 us -> 23.9 us
    all_to_all x1, starting transfers between devices: 3.87 us -> 14.7 us  [exchanged(): lax.all_to_all(flat.reshape(-1, rows, HALF), axes, 0, 0, tiled=True)]
    ppermute x1, starting transfers between devices: 12.5 us -> 2.47 us  [per_device(): other = lax.ppermute(stored, 'core', [(0, 1), (1, 0)])]
    ppermute x5, starting transfers between devices: 26.1 us -> 30 us  [routed(): return lax.ppermute(block, AXES, route)]
    all_gather x1 -> x0, blocking collectives: 3.9 us -> none  [per_device(): held = lax.all_gather(arriving, 'core', tiled=True)]
    all_to_all x1, blocking collectives: 19.8 us -> 16.3 us  [exchanged(): lax.all_to_all(flat.reshape(-1, rows, HALF), axes, 0, 0, tiled=True)]
    all_gather x1, blocking collectives: 3.03 us -> 5.89 us  [per_device(): lax.all_gather(given, 'core')]
  transfers between devices with their start and end apart: 7 -> 7, of which waited for: 1 -> 1; matrix products, arithmetic and copies ran while one was open for 1% -> 0% of each run, Pallas kernels for 6% -> 4%
where the time goes in v14:
time: 88.5 us; the launch traced here: 87.5 us
  starting transfers between devices  47.2 us (53%)
  blocking collectives  23.9 us (27%)
  waiting for transfers between devices  7.31 us (8%)
  Pallas kernels  7.23 us (8%)
  local copies, waits for them, and re-layouts  1.63 us (2%)
    ppermute x5, starting transfers between devices, routed(): return lax.ppermute(block, AXES, route)  30 us
    all_to_all x1, blocking collectives, exchanged(): lax.all_to_all(flat.reshape(-1, rows, HALF), axes, 0, 0, tiled=True)  16.3 us
    all_to_all x1, starting transfers between devices, exchanged(): lax.all_to_all(flat.reshape(-1, rows, HALF), axes, 0, 0, tiled=True)  14.7 us
    ppermute x5, waiting for transfers between devices, routed(): return lax.ppermute(block, AXES, route)  7.31 us
    all_gather x1, blocking collectives, per_device(): lax.all_gather(given, 'core')  5.89 us
    ppermute x1, starting transfers between devices, per_device(): other = lax.ppermute(stored, 'core', [(0, 1), (1, 0)])  2.47 us
  transfers between devices with their start and end apart: 7, of which 1 were waited for; matrix products, arithmetic and copies ran while one was open for 0% of the time, Pallas kernels for 4%

profile of v14, /device:TPU:1, one launch (start us, length us, event | category | flops | bytes accessed | tf_op | source)
XLA Modules:
  0.0 87.5 jit_solution(626973311579585183)
XLA Ops:
  0.0 0.8 copy-done.1
  0.8 1.1 %shard_map.46 = bf16[2048,128]{1,0:T(8,128)(2,1)} custom-call(f32[64,64]{1,0:T(8,128)S(1)} %copy-done.1), custom_call_target="tpu_custom_call" | custom-call | tf_op jit(solution)/shard_map/pallas_call | solution.py:181
  1.9 14.7 %all-to-all-start = ((bf16[64,32,128]{2,1,0:T(8,128)(2,1)}), bf16[64,32,128]{2,1,0:T(8,128)(2,1)S(1)}, u32[]{:S(2)}, u32[]{:S(2)}) async-start(bf16[64,32,128]{2,1,0:T(8,128)(2,1)} %bitcast.3), calls=%async_computation | async-start | bytes 1048576 | tf_op jit(solution)/shard_map/all_to_all | solution.py:33
  16.6 2.5 %collective-permute-start.2 = (bf16[8,256,256]{2,1,0:T(8,128)(2,1)S(1)}, bf16[8,256,256]{2,1,0:T(8,128)(2,1)S(1)}, u32[]{:S(2)}, u32[]{:S(2)}) collective-permute-start(bf16[8,256,256]{2,1,0:T(8,128)(2,1)S(1)} %bitcast.9), channel_id=1, source_target_pairs={{0,1},{1,0},{2,3},{3,2},{4,5},{5,4},{6,7},{7,6},{8,9},{9,8},{10,11... | collective-permute-start | bytes 3145736 | tf_op jit(solution)/shard_map/ppermute | solution.py:191
  19.1 0.0 copy-start.2
  19.1 0.7 copy-done.2
  19.8 1.8 %all-gather = s32[4,4,2]{1,2,0:T(2,128)S(1)} all-gather(s32[2,4,2]{1,2,0:T(2,128)S(1)} %pad_add_fusion), channel_id=2, replica_groups=mesh['blk'=12,'pos'=32,'core'=2] {'core'}, dimensions={0}, use_global_device_ids=true | all-gather | bytes 192 | tf_op jit(solution)/shard_map/all_gather | solution.py:189
  21.6 0.1 copy.17.lists
  21.7 12.4 %collective-permute-start.1 = (s32[2,2,4,2]{3,2,1,0:T(4,128)S(1)}, s32[2,2,4,2]{3,2,1,0:T(4,128)S(1)}, u32[]{:S(2)}, u32[]{:S(2)}) collective-permute-start(s32[2,2,4,2]{3,2,1,0:T(4,128)S(1)} %copy.17.lists), channel_id=1, source_target_pairs={{0,704},{1,641},{2,706},{3,643},{4,708},{5,645},{6,710},{7,647},{8... | collective-permute-start | bytes 392 | tf_op jit(solution)/shard_map/ppermute | solution.py:29
  34.1 2.5 %collective-permute-start = (s32[2,2,4,2]{3,2,1,0:T(4,128)S(1)}, s32[2,2,4,2]{3,2,1,0:T(4,128)S(1)}, u32[]{:S(2)}, u32[]{:S(2)}) collective-permute-start(s32[2,2,4,2]{3,2,1,0:T(4,128)S(1)} %copy.17.lists), channel_id=1, source_target_pairs={{0,576},{1,577},{2,578},{3,579},{4,580},{5,581},{6,582},{7,583},{8... | collective-permute-start | bytes 392 | tf_op jit(solution)/shard_map/ppermute | solution.py:29
  36.6 0.0 all-to-all-done
  36.6 0.9 %shard_map.48 = bf16[2,128,256]{2,1,0:T(8,128)(2,1)S(1)} custom-call(s32[2,2,4,2]{3,2,1,0:T(4,128)S(1)} %copy.17.lists, bf16[2048,128]{1,0:T(8,128)(2,1)S(1)} %bitcast.14, bf16[8,256,256]{2,1,0:T(8,128)(2,1)S(1)} %bitcast.10, bf16[8,256,256]{2,1,0:T(8,128)(2,1)S(1)} %collective-permute-done.2.other), custom_call_target="tpu_custom_call" | custom-call | tf_op jit(solution)/shard_map/pallas_call | solution.py:193
  37.5 9.8 %collective-permute-start.3 = (bf16[2,128,256]{2,1,0:T(8,128)(2,1)S(1)}, bf16[2,128,256]{2,1,0:T(8,128)(2,1)S(1)}, u32[]{:S(2)}, u32[]{:S(2)}) collective-permute-start(bf16[2,128,256]{2,1,0:T(8,128)(2,1)S(1)} %shard_map.48), channel_id=1, source_target_pairs={{0,704},{1,641},{2,706},{3,643},{4,708},{5,645},{6,710},{7,647},{8... | collective-permute-start | bytes 393224 | tf_op jit(solution)/shard_map/ppermute | solution.py:29
  47.3 0.0 collective-permute-done.1.far
  47.4 0.8 shard_map.50
  48.1 1.9 %collective-permute-start.4 = (bf16[2,128,256]{2,1,0:T(8,128)(2,1)S(1)}, bf16[2,128,256]{2,1,0:T(8,128)(2,1)S(1)}, u32[]{:S(2)}, u32[]{:S(2)}) collective-permute-start(bf16[2,128,256]{2,1,0:T(8,128)(2,1)S(1)} %shard_map.50), channel_id=1, source_target_pairs={{0,64},{1,129},{2,66},{3,131},{4,68},{5,133},{6,70},{7,135},{8,72}... | collective-permute-start | bytes 393224 | tf_op jit(solution)/shard_map/ppermute | solution.py:29
  50.1 1.1 %shard_map.47 = bf16[2,128,256]{2,1,0:T(8,128)(2,1)S(1)} custom-call(s32[2,2,4,2]{3,2,1,0:T(4,128)S(1)} %copy.17.lists, s32[2,2,4,2]{3,2,1,0:T(4,128)S(1)} %collective-permute-done.far3, bf16[2048,128]{1,0:T(8,128)(2,1)S(1)} %bitcast.16, bf16[8,256,256]{2,1,0:T(8,128)(2,1)S(1)} %bitcast.11, bf16[8,256,256]{2,1,0:T(8,128)(2,1)S(1)} %collective-permute-done.2.other), custom_call_target="tpu_custom_call" | custom-call | tf_op jit(solution)/shard_map/pallas_call | solution.py:211
  51.1 3.4 %collective-permute-start.5 = (bf16[2,128,256]{2,1,0:T(8,128)(2,1)S(1)}, bf16[2,128,256]{2,1,0:T(8,128)(2,1)S(1)}, u32[]{:S(2)}, u32[]{:S(2)}) collective-permute-start(bf16[2,128,256]{2,1,0:T(8,128)(2,1)S(1)} %shard_map.47), channel_id=1, source_target_pairs={{0,192},{1,577},{2,194},{3,579},{4,196},{5,581},{6,198},{7,583},{8... | collective-permute-start | bytes 393224 | tf_op jit(solution)/shard_map/ppermute | solution.py:29
  54.6 1.1 %shard_map.49.early = f32[16,64,256]{2,1,0:T(8,128)S(1)} custom-call(s32[2,2,4,2]{3,2,1,0:T(4,128)S(1)} %copy.17.lists, s32[2,2,4,2]{3,2,1,0:T(4,128)S(1)} %collective-permute-done.1.far, bf16[2048,128]{1,0:T(8,128)(2,1)S(1)} %bitcast.17, bf16[8,256,256]{2,1,0:T(8,128)(2,1)S(1)} %bitcast.12, bf16[2,128,256]{2,1,0:T(8,128)(2,1)S(1)} %collective-permute-done.3.back), custom_call_target="tpu_custom_call" | custom-call | tf_op jit(solution)/shard_map/pallas_call | solution.py:220
  55.7 7.3 %collective-permute-done.4.right = bf16[2,128,256]{2,1,0:T(8,128)(2,1)S(1)} collective-permute-done((bf16[2,128,256]{2,1,0:T(8,128)(2,1)S(1)}, bf16[2,128,256]{2,1,0:T(8,128)(2,1)S(1)}, u32[]{:S(2)}, u32[]{:S(2)}) %collective-permute-start.4) | collective-permute-done | bytes 131104 | tf_op jit(solution)/shard_map/ppermute | solution.py:29
  63.0 1.4 %shard_map.51 = (f32[1024,128]{1,0:T(8,128)S(1)}, bf16[1024,128]{1,0:T(8,128)(2,1)S(1)}, f32[16,64,256]{2,1,0:T(8,128)S(1)}) custom-call(s32[2,2,4,2]{3,2,1,0:T(4,128)S(1)} %copy.17.lists, s32[2,2,4,2]{3,2,1,0:T(4,128)S(1)} %collective-permute-done.far3, f32[16,64,256]{2,1,0:T(8,128)S(1)} %shard_map.49.early, ...), custom_call_target="tpu_custom_call", output_to_operand_aliasing={{2}: (2, {})} | custom-call | tf_op jit(solution)/shard_map/pallas_call | solution.py:228
  64.4 5.9 %all-gather.1 = bf16[2048,128]{1,0:T(8,128)(2,1)S(1)} all-gather(bf16[1024,128]{1,0:T(8,128)(2,1)S(1)} %get-tuple-element.12), channel_id=3, replica_groups=mesh['blk'=12,'pos'=32,'core'=2] {'core'}, dimensions={0}, use_global_device_ids=true | all-gather | bytes 786432 | tf_op jit(solution)/shard_map/all_gather | solution.py:242
  70.3 16.3 %all_to_all.10 = bf16[32,32,128]{2,1,0:T(8,128)(2,1)S(1)} all-to-all(bf16[32,32,128]{2,1,0:T(8,128)(2,1)S(1)} %bitcast.19), channel_id=1, replica_groups=mesh['blk'=12,'pos'=32,'core'=2] {'pos'}, dimensions={0} | all-to-all | bytes 524288 | tf_op jit(solution)/shard_map/all_to_all | solution.py:33
  86.6 0.9 shard_map.53
  (11 shorter events, 0.1 us)
Async XLA Ops:
  0.0 16.6 %copy-start = (bf16[1,1,4,2,256,256]{5,4,3,2,1,0:T(8,128)(2,1)S(1)}, bf16[1,1,4,2,256,256]{5,4,3,2,1,0:T(8,128)(2,1)}, u32[]{:S(2)}) copy-start(bf16[1,1,4,2,256,256]{5,4,3,2,1,0:T(8,128)(2,1)} %param.5) | copy-start | bytes 3145732
  0.0 0.8 copy-start.1
  1.9 17.2 %copy-start.3 = (s32[1,1,4,2]{2,3,1,0:T(2,128)S(1)}, s32[1,1,4,2]{2,3,1,0:T(2,128)}, u32[]{:S(2)}) copy-start(s32[1,1,4,2]{2,3,1,0:T(2,128)} %param.6) | copy-start | bytes 100
  1.9 34.7 %all-to-all-start = ((bf16[64,32,128]{2,1,0:T(8,128)(2,1)}), bf16[64,32,128]{2,1,0:T(8,128)(2,1)S(1)}, u32[]{:S(2)}, u32[]{:S(2)}) async-start(bf16[64,32,128]{2,1,0:T(8,128)(2,1)} %bitcast.3), calls=%async_computation | async-start | bytes 1048576 | tf_op jit(solution)/shard_map/all_to_all | solution.py:33
  16.6 19.9 %collective-permute-start.2 = (bf16[8,256,256]{2,1,0:T(8,128)(2,1)S(1)}, bf16[8,256,256]{2,1,0:T(8,128)(2,1)S(1)}, u32[]{:S(2)}, u32[]{:S(2)}) collective-permute-start(bf16[8,256,256]{2,1,0:T(8,128)(2,1)S(1)} %bitcast.9), channel_id=1, source_target_pairs={{0,1},{1,0},{2,3},{3,2},{4,5},{5,4},{6,7},{7,6},{8,9},{9,8},{10,11... | collective-permute-start | bytes 3145736 | tf_op jit(solution)/shard_map/ppermute | solution.py:191
  19.1 0.7 copy-start.2
  21.7 25.7 %collective-permute-start.1 = (s32[2,2,4,2]{3,2,1,0:T(4,128)S(1)}, s32[2,2,4,2]{3,2,1,0:T(4,128)S(1)}, u32[]{:S(2)}, u32[]{:S(2)}) collective-permute-start(s32[2,2,4,2]{3,2,1,0:T(4,128)S(1)} %copy.17.lists), channel_id=1, source_target_pairs={{0,704},{1,641},{2,706},{3,643},{4,708},{5,645},{6,710},{7,647},{8... | collective-permute-start | bytes 392 | tf_op jit(solution)/shard_map/ppermute | solution.py:29
  34.1 16.0 %collective-permute-start = (s32[2,2,4,2]{3,2,1,0:T(4,128)S(1)}, s32[2,2,4,2]{3,2,1,0:T(4,128)S(1)}, u32[]{:S(2)}, u32[]{:S(2)}) collective-permute-start(s32[2,2,4,2]{3,2,1,0:T(4,128)S(1)} %copy.17.lists), channel_id=1, source_target_pairs={{0,576},{1,577},{2,578},{3,579},{4,580},{5,581},{6,582},{7,583},{8... | collective-permute-start | bytes 392 | tf_op jit(solution)/shard_map/ppermute | solution.py:29
  37.5 17.0 %collective-permute-start.3 = (bf16[2,128,256]{2,1,0:T(8,128)(2,1)S(1)}, bf16[2,128,256]{2,1,0:T(8,128)(2,1)S(1)}, u32[]{:S(2)}, u32[]{:S(2)}) collective-permute-start(bf16[2,128,256]{2,1,0:T(8,128)(2,1)S(1)} %shard_map.48), channel_id=1, source_target_pairs={{0,704},{1,641},{2,706},{3,643},{4,708},{5,645},{6,710},{7,647},{8... | collective-permute-start | bytes 393224 | tf_op jit(solution)/shard_map/ppermute | solution.py:29
  48.1 14.9 %collective-permute-start.4 = (bf16[2,128,256]{2,1,0:T(8,128)(2,1)S(1)}, bf16[2,128,256]{2,1,0:T(8,128)(2,1)S(1)}, u32[]{:S(2)}, u32[]{:S(2)}) collective-permute-start(bf16[2,128,256]{2,1,0:T(8,128)(2,1)S(1)} %shard_map.50), channel_id=1, source_target_pairs={{0,64},{1,129},{2,66},{3,131},{4,68},{5,133},{6,70},{7,135},{8,72}... | collective-permute-start | bytes 393224 | tf_op jit(solution)/shard_map/ppermute | solution.py:29
  51.1 11.9 %collective-permute-start.5 = (bf16[2,128,256]{2,1,0:T(8,128)(2,1)S(1)}, bf16[2,128,256]{2,1,0:T(8,128)(2,1)S(1)}, u32[]{:S(2)}, u32[]{:S(2)}) collective-permute-start(bf16[2,128,256]{2,1,0:T(8,128)(2,1)S(1)} %shard_map.47), channel_id=1, source_target_pairs={{0,192},{1,577},{2,194},{3,579},{4,196},{5,581},{6,198},{7,583},{8... | collective-permute-start | bytes 393224 | tf_op jit(solution)/shard_map/ppermute | solution.py:29

commit v15 on v9

--- a/solution.py
+++ b/solution.py
@@ -64,7 +64,7 @@
 
 
 def shared_block(blocks, other, step, core, k):
-    return (other if core else blocks)[step * SLOTS + k]
+    return other[(step - 1) * SLOTS + k] if core else blocks[step * SLOTS + k]
 
 
 def transposed_products(lists, held, blocks, other, partials):
@@ -189,7 +189,8 @@
     arriving = exchanged(mine, CHUNK, "pos")
     lists = lax.all_gather(jnp.stack([row_blocks[0, 0], col_blocks[0, 0]]), "core")
     far = routed(lists, -1, -2)
-    other = lax.ppermute(stored, "core", [(0, 1), (1, 0)])
+    later, _ = lax.optimization_barrier((stored[SLOTS:], lists))
+    other = lax.ppermute(later, "core", [(0, 1), (1, 0)])
     held = lax.all_gather(arriving, "core", tiled=True)
     two = shape_of((2, SLOTS * NV, BS), BF16)
     partials = pl.pallas_call(

time: 88.1 us -> 89.8 us (1.019)
  local copies, waits for them, and re-layouts: 0.86 us -> 2.81 us
  blocking collectives: 28.5 us -> 30.2 us
  waiting for transfers between devices: 7.16 us -> 6.22 us
    ppermute x1, starting transfers between devices: 12.5 us -> 2.21 us  [per_device(): other = lax.ppermute(later, 'core', [(0, 1), (1, 0)])]
    all_to_all x1, starting transfers between devices: 3.87 us -> 13.6 us  [exchanged(): lax.all_to_all(flat.reshape(-1, rows, HALF), axes, 0, 0, tiled=True)]
    all_to_all x1, blocking collectives: 19.8 us -> 21.2 us  [exchanged(): lax.all_to_all(flat.reshape(-1, rows, HALF), axes, 0, 0, tiled=True)]
    slice x0 -> x1, local copies, waits for them, and re-layouts: none -> 1.27 us  [per_device(): later, _ = lax.optimization_barrier((stored[SLOTS:], lists))]
    ppermute x5, waiting for transfers between devices: 7.15 us -> 6.22 us  [routed(): return lax.ppermute(block, AXES, route)]
  transfers between devices with their start and end apart: 7 -> 7, of which waited for: 1 -> 1; matrix products, arithmetic and copies ran while one was open for 1% -> 2% of each run, Pallas kernels for 6% -> 4%
where the time goes in v15:
time: 89.8 us; the launch traced here: 88.7 us
  starting transfers between devices  42.1 us (47%)
  blocking collectives  30.2 us (34%)
  Pallas kernels  7.11 us (8%)
  waiting for transfers between devices  6.22 us (7%)
  local copies, waits for them, and re-layouts  2.81 us (3%)
    ppermute x5, starting transfers between devices, routed(): return lax.ppermute(block, AXES, route)  26.3 us
    all_to_all x1, blocking collectives, exchanged(): lax.all_to_all(flat.reshape(-1, rows, HALF), axes, 0, 0, tiled=True)  21.2 us
    all_to_all x1, starting transfers between devices, exchanged(): lax.all_to_all(flat.reshape(-1, rows, HALF), axes, 0, 0, tiled=True)  13.6 us
    ppermute x5, waiting for transfers between devices, routed(): return lax.ppermute(block, AXES, route)  6.22 us
    all_gather x1, blocking collectives, per_device(): held = lax.all_gather(arriving, 'core', tiled=True)  3.81 us
    all_gather x1, blocking collectives, per_device(): lax.all_gather(given, 'core')  2.76 us
    all_gather x1, blocking collectives, per_device(): lax.all_gather(jnp.stack([row_blocks[0, 0], col_blocks[0, 0]]), 'core')  2.42 us
    ppermute x1, starting transfers between devices, per_device(): other = lax.ppermute(later, 'core', [(0, 1), (1, 0)])  2.21 us
  transfers between devices with their start and end apart: 7, of which 1 were waited for; matrix products, arithmetic and copies ran while one was open for 2% of the time, Pallas kernels for 4%

profile of v15, /device:TPU:1, one launch (start us, length us, event | category | flops | bytes accessed | tf_op | source)
XLA Modules:
  0.0 88.7 jit_solution(2607616244490608108)
XLA Ops:
  0.0 0.8 copy-done.1
  0.8 0.9 %shard_map.46 = bf16[1024,128]{1,0:T(8,128)(2,1)} custom-call(f32[64,64]{1,0:T(8,128)S(1)} %copy-done.1), custom_call_target="tpu_custom_call" | custom-call | tf_op jit(solution)/shard_map/pallas_call | solution.py:182
  1.7 13.6 %all-to-all-start = ((bf16[32,32,128]{2,1,0:T(8,128)(2,1)}), bf16[32,32,128]{2,1,0:T(8,128)(2,1)S(1)}, u32[]{:S(2)}, u32[]{:S(2)}) async-start(bf16[32,32,128]{2,1,0:T(8,128)(2,1)} %bitcast.3), calls=%async_computation | async-start | bytes 524288 | tf_op jit(solution)/shard_map/all_to_all | solution.py:33
  15.3 0.0 copy-start.2
  15.3 0.7 copy-done.2
  16.0 2.4 %all-gather = s32[4,4,2]{1,2,0:T(2,128)S(1)} all-gather(s32[2,4,2]{1,2,0:T(2,128)S(1)} %pad_add_fusion), channel_id=2, replica_groups=mesh['blk'=12,'pos'=32,'core'=2] {'core'}, dimensions={0}, use_global_device_ids=true | all-gather | bytes 192 | tf_op jit(solution)/shard_map/all_gather | solution.py:190
  18.4 1.3 %slice.6 = bf16[1,1,3,2,256,256]{5,4,3,2,1,0:T(8,128)(2,1)S(1)} slice(bf16[1,1,4,2,256,256]{5,4,3,2,1,0:T(8,128)(2,1)} %param.5), slice={[0:1], [0:1], [1:4], [0:2], [0:256], [0:256]} | slice | bytes 1572864 | tf_op jit(solution)/shard_map/slice | solution.py:192
  19.7 2.2 %collective-permute-start.2 = (bf16[6,256,256]{2,1,0:T(8,128)(2,1)S(1)}, bf16[6,256,256]{2,1,0:T(8,128)(2,1)S(1)}, u32[]{:S(2)}, u32[]{:S(2)}) collective-permute-start(bf16[6,256,256]{2,1,0:T(8,128)(2,1)S(1)} %bitcast.18), channel_id=1, source_target_pairs={{0,1},{1,0},{2,3},{3,2},{4,5},{5,4},{6,7},{7,6},{8,9},{9,8},{10,11... | collective-permute-start | bytes 2359304 | tf_op jit(solution)/shard_map/ppermute | solution.py:193
  21.9 0.1 copy.17.lists
  22.0 12.5 %collective-permute-start.1 = (s32[2,2,4,2]{3,2,1,0:T(4,128)S(1)}, s32[2,2,4,2]{3,2,1,0:T(4,128)S(1)}, u32[]{:S(2)}, u32[]{:S(2)}) collective-permute-start(s32[2,2,4,2]{3,2,1,0:T(4,128)S(1)} %copy.17.lists), channel_id=1, source_target_pairs={{0,704},{1,641},{2,706},{3,643},{4,708},{5,645},{6,710},{7,647},{8... | collective-permute-start | bytes 392 | tf_op jit(solution)/shard_map/ppermute | solution.py:29
  34.6 2.5 %collective-permute-start = (s32[2,2,4,2]{3,2,1,0:T(4,128)S(1)}, s32[2,2,4,2]{3,2,1,0:T(4,128)S(1)}, u32[]{:S(2)}, u32[]{:S(2)}) collective-permute-start(s32[2,2,4,2]{3,2,1,0:T(4,128)S(1)} %copy.17.lists), channel_id=1, source_target_pairs={{0,576},{1,577},{2,578},{3,579},{4,580},{5,581},{6,582},{7,583},{8... | collective-permute-start | bytes 392 | tf_op jit(solution)/shard_map/ppermute | solution.py:29
  37.0 3.8 %all_gather.17.held = bf16[2048,128]{1,0:T(8,128)(2,1)S(1)} all-gather(bf16[1024,128]{1,0:T(8,128)(2,1)S(1)} %bitcast.17), channel_id=1, replica_groups=mesh['blk'=12,'pos'=32,'core'=2] {'core'}, dimensions={0}, use_global_device_ids=true | all-gather | bytes 786432 | tf_op jit(solution)/shard_map/all_gather | solution.py:194
  40.8 0.9 %shard_map.48 = bf16[2,128,256]{2,1,0:T(8,128)(2,1)S(1)} custom-call(s32[2,2,4,2]{3,2,1,0:T(4,128)S(1)} %copy.17.lists, bf16[2048,128]{1,0:T(8,128)(2,1)S(1)} %all_gather.17.held, bf16[8,256,256]{2,1,0:T(8,128)(2,1)S(1)} %bitcast.10, bf16[6,256,256]{2,1,0:T(8,128)(2,1)S(1)} %collective-permute-done.2.other), custom_call_target="tpu_custom_call" | custom-call | tf_op jit(solution)/shard_map/pallas_call | solution.py:196
  41.8 4.2 %collective-permute-start.3 = (bf16[2,128,256]{2,1,0:T(8,128)(2,1)S(1)}, bf16[2,128,256]{2,1,0:T(8,128)(2,1)S(1)}, u32[]{:S(2)}, u32[]{:S(2)}) collective-permute-start(bf16[2,128,256]{2,1,0:T(8,128)(2,1)S(1)} %shard_map.48), channel_id=1, source_target_pairs={{0,704},{1,641},{2,706},{3,643},{4,708},{5,645},{6,710},{7,647},{8... | collective-permute-start | bytes 393224 | tf_op jit(solution)/shard_map/ppermute | solution.py:29
  46.0 0.8 shard_map.50
  46.8 5.0 %collective-permute-start.4 = (bf16[2,128,256]{2,1,0:T(8,128)(2,1)S(1)}, bf16[2,128,256]{2,1,0:T(8,128)(2,1)S(1)}, u32[]{:S(2)}, u32[]{:S(2)}) collective-permute-start(bf16[2,128,256]{2,1,0:T(8,128)(2,1)S(1)} %shard_map.50), channel_id=1, source_target_pairs={{0,64},{1,129},{2,66},{3,131},{4,68},{5,133},{6,70},{7,135},{8,72}... | collective-permute-start | bytes 393224 | tf_op jit(solution)/shard_map/ppermute | solution.py:29
  51.8 1.1 %shard_map.47 = bf16[2,128,256]{2,1,0:T(8,128)(2,1)S(1)} custom-call(s32[2,2,4,2]{3,2,1,0:T(4,128)S(1)} %copy.17.lists, s32[2,2,4,2]{3,2,1,0:T(4,128)S(1)} %collective-permute-done.far3, bf16[2048,128]{1,0:T(8,128)(2,1)S(1)} %all_gather.17.held, bf16[8,256,256]{2,1,0:T(8,128)(2,1)S(1)} %bitcast.11, bf16[6,256,256]{2,1,0:T(8,128)(2,1)S(1)} %collective-permute-done.2.other), custom_call_target="tpu_custom_call" | custom-call | tf_op jit(solution)/shard_map/pallas_call | solution.py:214
  52.9 2.2 %collective-permute-start.5 = (bf16[2,128,256]{2,1,0:T(8,128)(2,1)S(1)}, bf16[2,128,256]{2,1,0:T(8,128)(2,1)S(1)}, u32[]{:S(2)}, u32[]{:S(2)}) collective-permute-start(bf16[2,128,256]{2,1,0:T(8,128)(2,1)S(1)} %shard_map.47), channel_id=1, source_target_pairs={{0,192},{1,577},{2,194},{3,579},{4,196},{5,581},{6,198},{7,583},{8... | collective-permute-start | bytes 393224 | tf_op jit(solution)/shard_map/ppermute | solution.py:29
  55.0 1.1 %shard_map.49.early = f32[16,64,256]{2,1,0:T(8,128)S(1)} custom-call(s32[2,2,4,2]{3,2,1,0:T(4,128)S(1)} %copy.17.lists, s32[2,2,4,2]{3,2,1,0:T(4,128)S(1)} %collective-permute-done.1.far, bf16[2048,128]{1,0:T(8,128)(2,1)S(1)} %all_gather.17.held, bf16[8,256,256]{2,1,0:T(8,128)(2,1)S(1)} %bitcast.12, bf16[2,128,256]{2,1,0:T(8,128)(2,1)S(1)} %collective-permute-done.3.back), custom_call_target="tpu_custom_call" | custom-call | tf_op jit(solution)/shard_map/pallas_call | solution.py:223
  56.2 6.2 %collective-permute-done.4.right = bf16[2,128,256]{2,1,0:T(8,128)(2,1)S(1)} collective-permute-done((bf16[2,128,256]{2,1,0:T(8,128)(2,1)S(1)}, bf16[2,128,256]{2,1,0:T(8,128)(2,1)S(1)}, u32[]{:S(2)}, u32[]{:S(2)}) %collective-permute-start.4) | collective-permute-done | bytes 131104 | tf_op jit(solution)/shard_map/ppermute | solution.py:29
  62.4 1.4 %shard_map.51 = (f32[1024,128]{1,0:T(8,128)S(1)}, bf16[1024,128]{1,0:T(8,128)(2,1)S(1)}, f32[16,64,256]{2,1,0:T(8,128)S(1)}) custom-call(s32[2,2,4,2]{3,2,1,0:T(4,128)S(1)} %copy.17.lists, s32[2,2,4,2]{3,2,1,0:T(4,128)S(1)} %collective-permute-done.far3, f32[16,64,256]{2,1,0:T(8,128)S(1)} %shard_map.49.early, ...), custom_call_target="tpu_custom_call", output_to_operand_aliasing={{2}: (2, {})} | custom-call | tf_op jit(solution)/shard_map/pallas_call | solution.py:231
  63.8 2.8 %all-gather.1 = bf16[2048,128]{1,0:T(8,128)(2,1)S(1)} all-gather(bf16[1024,128]{1,0:T(8,128)(2,1)S(1)} %get-tuple-element.14), channel_id=3, replica_groups=mesh['blk'=12,'pos'=32,'core'=2] {'core'}, dimensions={0}, use_global_device_ids=true | all-gather | bytes 786432 | tf_op jit(solution)/shard_map/all_gather | solution.py:245
  66.6 21.2 %all_to_all.10 = bf16[32,32,128]{2,1,0:T(8,128)(2,1)S(1)} all-to-all(bf16[32,32,128]{2,1,0:T(8,128)(2,1)S(1)} %bitcast.15), channel_id=1, replica_groups=mesh['blk'=12,'pos'=32,'core'=2] {'pos'}, dimensions={0} | all-to-all | bytes 524288 | tf_op jit(solution)/shard_map/all_to_all | solution.py:33
  87.8 0.9 shard_map.53
  (13 shorter events, 0.1 us)
Async XLA Ops:
  0.0 0.8 copy-start.1
  1.7 13.6 %copy-start.3 = (s32[1,1,4,2]{2,3,1,0:T(2,128)S(1)}, s32[1,1,4,2]{2,3,1,0:T(2,128)}, u32[]{:S(2)}) copy-start(s32[1,1,4,2]{2,3,1,0:T(2,128)} %param.6) | copy-start | bytes 100
  1.7 35.3 %all-to-all-start = ((bf16[32,32,128]{2,1,0:T(8,128)(2,1)}), bf16[32,32,128]{2,1,0:T(8,128)(2,1)S(1)}, u32[]{:S(2)}, u32[]{:S(2)}) async-start(bf16[32,32,128]{2,1,0:T(8,128)(2,1)} %bitcast.3), calls=%async_computation | async-start | bytes 524288 | tf_op jit(solution)/shard_map/all_to_all | solution.py:33
  15.3 0.7 copy-start.2
  18.4 22.4 %copy-start = (bf16[1,1,4,2,256,256]{5,4,3,2,1,0:T(8,128)(2,1)S(1)}, bf16[1,1,4,2,256,256]{5,4,3,2,1,0:T(8,128)(2,1)}, u32[]{:S(2)}) copy-start(bf16[1,1,4,2,256,256]{5,4,3,2,1,0:T(8,128)(2,1)} %param.5) | copy-start | bytes 3145732
  19.7 21.2 %collective-permute-start.2 = (bf16[6,256,256]{2,1,0:T(8,128)(2,1)S(1)}, bf16[6,256,256]{2,1,0:T(8,128)(2,1)S(1)}, u32[]{:S(2)}, u32[]{:S(2)}) collective-permute-start(bf16[6,256,256]{2,1,0:T(8,128)(2,1)S(1)} %bitcast.18), channel_id=1, source_target_pairs={{0,1},{1,0},{2,3},{3,2},{4,5},{5,4},{6,7},{7,6},{8,9},{9,8},{10,11... | collective-permute-start | bytes 2359304 | tf_op jit(solution)/shard_map/ppermute | solution.py:193
  22.0 23.9 %collective-permute-start.1 = (s32[2,2,4,2]{3,2,1,0:T(4,128)S(1)}, s32[2,2,4,2]{3,2,1,0:T(4,128)S(1)}, u32[]{:S(2)}, u32[]{:S(2)}) collective-permute-start(s32[2,2,4,2]{3,2,1,0:T(4,128)S(1)} %copy.17.lists), channel_id=1, source_target_pairs={{0,704},{1,641},{2,706},{3,643},{4,708},{5,645},{6,710},{7,647},{8... | collective-permute-start | bytes 392 | tf_op jit(solution)/shard_map/ppermute | solution.py:29
  34.6 17.2 %collective-permute-start = (s32[2,2,4,2]{3,2,1,0:T(4,128)S(1)}, s32[2,2,4,2]{3,2,1,0:T(4,128)S(1)}, u32[]{:S(2)}, u32[]{:S(2)}) collective-permute-start(s32[2,2,4,2]{3,2,1,0:T(4,128)S(1)} %copy.17.lists), channel_id=1, source_target_pairs={{0,576},{1,577},{2,578},{3,579},{4,580},{5,581},{6,582},{7,583},{8... | collective-permute-start | bytes 392 | tf_op jit(solution)/shard_map/ppermute | solution.py:29
  41.8 13.3 %collective-permute-start.3 = (bf16[2,128,256]{2,1,0:T(8,128)(2,1)S(1)}, bf16[2,128,256]{2,1,0:T(8,128)(2,1)S(1)}, u32[]{:S(2)}, u32[]{:S(2)}) collective-permute-start(bf16[2,128,256]{2,1,0:T(8,128)(2,1)S(1)} %shard_map.48), channel_id=1, source_target_pairs={{0,704},{1,641},{2,706},{3,643},{4,708},{5,645},{6,710},{7,647},{8... | collective-permute-start | bytes 393224 | tf_op jit(solution)/shard_map/ppermute | solution.py:29
  46.8 15.6 %collective-permute-start.4 = (bf16[2,128,256]{2,1,0:T(8,128)(2,1)S(1)}, bf16[2,128,256]{2,1,0:T(8,128)(2,1)S(1)}, u32[]{:S(2)}, u32[]{:S(2)}) collective-permute-start(bf16[2,128,256]{2,1,0:T(8,128)(2,1)S(1)} %shard_map.50), channel_id=1, source_target_pairs={{0,64},{1,129},{2,66},{3,131},{4,68},{5,133},{6,70},{7,135},{8,72}... | collective-permute-start | bytes 393224 | tf_op jit(solution)/shard_map/ppermute | solution.py:29
  52.9 9.5 %collective-permute-start.5 = (bf16[2,128,256]{2,1,0:T(8,128)(2,1)S(1)}, bf16[2,128,256]{2,1,0:T(8,128)(2,1)S(1)}, u32[]{:S(2)}, u32[]{:S(2)}) collective-permute-start(bf16[2,128,256]{2,1,0:T(8,128)(2,1)S(1)} %shard_map.47), channel_id=1, source_target_pairs={{0,192},{1,577},{2,194},{3,579},{4,196},{5,581},{6,198},{7,583},{8... | collective-permute-start | bytes 393224 | tf_op jit(solution)/shard_map/ppermute | solution.py:29

commit v16 on v9

--- a/solution.py
+++ b/solution.py
@@ -179,6 +179,7 @@
 
 def per_device(vectors, blocks, row_blocks, col_blocks):
     stored = blocks.reshape(STEPS * SLOTS, BS, BS)
+    listed = jnp.stack([row_blocks[0, 0], col_blocks[0, 0]])
     mine = pl.pallas_call(
         prepared,
         out_shape=shape_of((COL // 2 * CHUNK, HALF), BF16),
@@ -186,10 +187,11 @@
         out_specs=VM,
         compiler_params=PARAMS,
     )(vectors)
-    arriving = exchanged(mine, CHUNK, "pos")
-    lists = lax.all_gather(jnp.stack([row_blocks[0, 0], col_blocks[0, 0]]), "core")
+    arriving = exchanged(lax.optimization_barrier((mine, listed))[0], CHUNK, "pos")
+    lists = lax.all_gather(listed, "core")
     far = routed(lists, -1, -2)
-    other = lax.ppermute(stored, "core", [(0, 1), (1, 0)])
+    whole, _ = lax.optimization_barrier((stored, listed))
+    other = lax.ppermute(whole, "core", [(0, 1), (1, 0)])
     held = lax.all_gather(arriving, "core", tiled=True)
     two = shape_of((2, SLOTS * NV, BS), BF16)
     partials = pl.pallas_call(

time: 88.1 us -> 88 us (level)
  blocking collectives: 28.5 us -> 27.3 us
    all_to_all x1, blocking collectives: 19.8 us -> 18.5 us  [exchanged(): lax.all_to_all(flat.reshape(-1, rows, HALF), axes, 0, 0, tiled=True)]
  transfers between devices with their start and end apart: 7 -> 7, of which waited for: 1 -> 1; matrix products, arithmetic and copies ran while one was open for 1% -> 0% of each run, Pallas kernels for 6% -> 6%
where the time goes in v16:
time: 88 us; the launch traced here: 86.9 us
  starting transfers between devices  42.8 us (49%)
  blocking collectives  27.3 us (31%)
  waiting for transfers between devices  7.97 us (9%)
  Pallas kernels  7.11 us (8%)
    ppermute x5, starting transfers between devices, routed(): return lax.ppermute(block, AXES, route)  26.5 us
    all_to_all x1, blocking collectives, exchanged(): lax.all_to_all(flat.reshape(-1, rows, HALF), axes, 0, 0, tiled=True)  18.5 us
    ppermute x1, starting transfers between devices, per_device(): other = lax.ppermute(whole, 'core', [(0, 1), (1, 0)])  12.4 us
    ppermute x5, waiting for transfers between devices, routed(): return lax.ppermute(block, AXES, route)  7.96 us
    all_gather x1, blocking collectives, per_device(): held = lax.all_gather(arriving, 'core', tiled=True)  3.9 us
    all_to_all x1, starting transfers between devices, exchanged(): lax.all_to_all(flat.reshape(-1, rows, HALF), axes, 0, 0, tiled=True)  3.87 us
    all_gather x1, blocking collectives, per_device(): lax.all_gather(given, 'core')  3.13 us
    all_gather x1, blocking collectives, per_device(): lists = lax.all_gather(listed, 'core')  1.78 us
  transfers between devices with their start and end apart: 7, of which 1 were waited for; matrix products, arithmetic and copies ran while one was open for 0% of the time, Pallas kernels for 6%

profile of v16, /device:TPU:1, one launch (start us, length us, event | category | flops | bytes accessed | tf_op | source)
XLA Modules:
  0.0 86.9 jit_solution(1414338121965584032)
XLA Ops:
  0.0 0.8 pad_add_fusion
  0.8 12.4 %collective-permute-start.2 = (bf16[8,256,256]{2,1,0:T(8,128)(2,1)}, bf16[8,256,256]{2,1,0:T(8,128)(2,1)S(1)}, u32[]{:S(2)}, u32[]{:S(2)}) collective-permute-start(bf16[8,256,256]{2,1,0:T(8,128)(2,1)} %bitcast.9), channel_id=1, source_target_pairs={{0,1},{1,0},{2,3},{3,2},{4,5},{5,4},{6,7},{7,6},{8,9},{9,8},{10,11... | collective-permute-start | bytes 3145736 | tf_op jit(solution)/shard_map/ppermute | solution.py:194
  13.2 0.0 copy-start.1
  13.2 0.7 copy-done.1
  14.0 0.9 %shard_map.46 = bf16[1024,128]{1,0:T(8,128)(2,1)} custom-call(f32[64,64]{1,0:T(8,128)S(1)} %copy-done.1), custom_call_target="tpu_custom_call" | custom-call | tf_op jit(solution)/shard_map/pallas_call | solution.py:183
  14.9 3.9 %all-to-all-start = ((bf16[32,32,128]{2,1,0:T(8,128)(2,1)}), bf16[32,32,128]{2,1,0:T(8,128)(2,1)S(1)}, u32[]{:S(2)}, u32[]{:S(2)}) async-start(bf16[32,32,128]{2,1,0:T(8,128)(2,1)} %bitcast.3), calls=%async_computation | async-start | bytes 524288 | tf_op jit(solution)/shard_map/all_to_all | solution.py:33
  18.8 1.8 %all-gather = s32[4,4,2]{1,2,0:T(2,128)S(1)} all-gather(s32[2,4,2]{1,2,0:T(2,128)S(1)} %pad_add_fusion), channel_id=2, replica_groups=mesh['blk'=12,'pos'=32,'core'=2] {'core'}, dimensions={0}, use_global_device_ids=true | all-gather | bytes 192 | tf_op jit(solution)/shard_map/all_gather | solution.py:191
  20.6 0.1 copy.17.lists
  20.7 12.3 %collective-permute-start.1 = (s32[2,2,4,2]{3,2,1,0:T(4,128)S(1)}, s32[2,2,4,2]{3,2,1,0:T(4,128)S(1)}, u32[]{:S(2)}, u32[]{:S(2)}) collective-permute-start(s32[2,2,4,2]{3,2,1,0:T(4,128)S(1)} %copy.17.lists), channel_id=1, source_target_pairs={{0,704},{1,641},{2,706},{3,643},{4,708},{5,645},{6,710},{7,647},{8... | collective-permute-start | bytes 392 | tf_op jit(solution)/shard_map/ppermute | solution.py:29
  33.0 2.5 %collective-permute-start = (s32[2,2,4,2]{3,2,1,0:T(4,128)S(1)}, s32[2,2,4,2]{3,2,1,0:T(4,128)S(1)}, u32[]{:S(2)}, u32[]{:S(2)}) collective-permute-start(s32[2,2,4,2]{3,2,1,0:T(4,128)S(1)} %copy.17.lists), channel_id=1, source_target_pairs={{0,576},{1,577},{2,578},{3,579},{4,580},{5,581},{6,582},{7,583},{8... | collective-permute-start | bytes 392 | tf_op jit(solution)/shard_map/ppermute | solution.py:29
  35.5 3.9 %all_gather.17.held = bf16[2048,128]{1,0:T(8,128)(2,1)S(1)} all-gather(bf16[1024,128]{1,0:T(8,128)(2,1)S(1)} %bitcast.17), channel_id=1, replica_groups=mesh['blk'=12,'pos'=32,'core'=2] {'core'}, dimensions={0}, use_global_device_ids=true | all-gather | bytes 786432 | tf_op jit(solution)/shard_map/all_gather | solution.py:195
  39.4 0.0 collective-permute-done.2.other
  39.4 0.9 %shard_map.48 = bf16[2,128,256]{2,1,0:T(8,128)(2,1)S(1)} custom-call(s32[2,2,4,2]{3,2,1,0:T(4,128)S(1)} %copy.17.lists, bf16[2048,128]{1,0:T(8,128)(2,1)S(1)} %all_gather.17.held, bf16[8,256,256]{2,1,0:T(8,128)(2,1)S(1)} %bitcast.10, bf16[8,256,256]{2,1,0:T(8,128)(2,1)S(1)} %collective-permute-done.2.other), custom_call_target="tpu_custom_call" | custom-call | tf_op jit(solution)/shard_map/pallas_call | solution.py:197
  40.3 6.4 %collective-permute-start.3 = (bf16[2,128,256]{2,1,0:T(8,128)(2,1)S(1)}, bf16[2,128,256]{2,1,0:T(8,128)(2,1)S(1)}, u32[]{:S(2)}, u32[]{:S(2)}) collective-permute-start(bf16[2,128,256]{2,1,0:T(8,128)(2,1)S(1)} %shard_map.48), channel_id=1, source_target_pairs={{0,704},{1,641},{2,706},{3,643},{4,708},{5,645},{6,710},{7,647},{8... | collective-permute-start | bytes 393224 | tf_op jit(solution)/shard_map/ppermute | solution.py:29
  46.7 0.8 shard_map.50
  47.5 2.8 %collective-permute-start.4 = (bf16[2,128,256]{2,1,0:T(8,128)(2,1)S(1)}, bf16[2,128,256]{2,1,0:T(8,128)(2,1)S(1)}, u32[]{:S(2)}, u32[]{:S(2)}) collective-permute-start(bf16[2,128,256]{2,1,0:T(8,128)(2,1)S(1)} %shard_map.50), channel_id=1, source_target_pairs={{0,64},{1,129},{2,66},{3,131},{4,68},{5,133},{6,70},{7,135},{8,72}... | collective-permute-start | bytes 393224 | tf_op jit(solution)/shard_map/ppermute | solution.py:29
  50.3 1.1 %shard_map.47 = bf16[2,128,256]{2,1,0:T(8,128)(2,1)S(1)} custom-call(s32[2,2,4,2]{3,2,1,0:T(4,128)S(1)} %copy.17.lists, s32[2,2,4,2]{3,2,1,0:T(4,128)S(1)} %collective-permute-done.far3, bf16[2048,128]{1,0:T(8,128)(2,1)S(1)} %all_gather.17.held, bf16[8,256,256]{2,1,0:T(8,128)(2,1)S(1)} %bitcast.11, bf16[8,256,256]{2,1,0:T(8,128)(2,1)S(1)} %collective-permute-done.2.other), custom_call_target="tpu_custom_call" | custom-call | tf_op jit(solution)/shard_map/pallas_call | solution.py:215
  51.4 2.6 %collective-permute-start.5 = (bf16[2,128,256]{2,1,0:T(8,128)(2,1)S(1)}, bf16[2,128,256]{2,1,0:T(8,128)(2,1)S(1)}, u32[]{:S(2)}, u32[]{:S(2)}) collective-permute-start(bf16[2,128,256]{2,1,0:T(8,128)(2,1)S(1)} %shard_map.47), channel_id=1, source_target_pairs={{0,192},{1,577},{2,194},{3,579},{4,196},{5,581},{6,198},{7,583},{8... | collective-permute-start | bytes 393224 | tf_op jit(solution)/shard_map/ppermute | solution.py:29
  54.0 1.1 %shard_map.49.early = f32[16,64,256]{2,1,0:T(8,128)S(1)} custom-call(s32[2,2,4,2]{3,2,1,0:T(4,128)S(1)} %copy.17.lists, s32[2,2,4,2]{3,2,1,0:T(4,128)S(1)} %collective-permute-done.1.far, bf16[2048,128]{1,0:T(8,128)(2,1)S(1)} %all_gather.17.held, bf16[8,256,256]{2,1,0:T(8,128)(2,1)S(1)} %bitcast.12, bf16[2,128,256]{2,1,0:T(8,128)(2,1)S(1)} %collective-permute-done.3.back), custom_call_target="tpu_custom_call" | custom-call | tf_op jit(solution)/shard_map/pallas_call | solution.py:224
  55.1 8.0 %collective-permute-done.4.right = bf16[2,128,256]{2,1,0:T(8,128)(2,1)S(1)} collective-permute-done((bf16[2,128,256]{2,1,0:T(8,128)(2,1)S(1)}, bf16[2,128,256]{2,1,0:T(8,128)(2,1)S(1)}, u32[]{:S(2)}, u32[]{:S(2)}) %collective-permute-start.4) | collective-permute-done | bytes 131104 | tf_op jit(solution)/shard_map/ppermute | solution.py:29
  63.0 1.4 %shard_map.51 = (f32[1024,128]{1,0:T(8,128)S(1)}, bf16[1024,128]{1,0:T(8,128)(2,1)S(1)}, f32[16,64,256]{2,1,0:T(8,128)S(1)}) custom-call(s32[2,2,4,2]{3,2,1,0:T(4,128)S(1)} %copy.17.lists, s32[2,2,4,2]{3,2,1,0:T(4,128)S(1)} %collective-permute-done.far3, f32[16,64,256]{2,1,0:T(8,128)S(1)} %shard_map.49.early, ...), custom_call_target="tpu_custom_call", output_to_operand_aliasing={{2}: (2, {})} | custom-call | tf_op jit(solution)/shard_map/pallas_call | solution.py:232
  64.4 3.1 %all-gather.1 = bf16[2048,128]{1,0:T(8,128)(2,1)S(1)} all-gather(bf16[1024,128]{1,0:T(8,128)(2,1)S(1)} %get-tuple-element.16), channel_id=3, replica_groups=mesh['blk'=12,'pos'=32,'core'=2] {'core'}, dimensions={0}, use_global_device_ids=true | all-gather | bytes 786432 | tf_op jit(solution)/shard_map/all_gather | solution.py:246
  67.6 18.5 %all_to_all.10 = bf16[32,32,128]{2,1,0:T(8,128)(2,1)S(1)} all-to-all(bf16[32,32,128]{2,1,0:T(8,128)(2,1)S(1)} %bitcast.15), channel_id=1, replica_groups=mesh['blk'=12,'pos'=32,'core'=2] {'pos'}, dimensions={0} | all-to-all | bytes 524288 | tf_op jit(solution)/shard_map/all_to_all | solution.py:33
  86.1 0.9 shard_map.53
  (8 shorter events, 0.1 us)
Async XLA Ops:
  0.0 39.4 %copy-start = (bf16[1,1,4,2,256,256]{5,4,3,2,1,0:T(8,128)(2,1)S(1)}, bf16[1,1,4,2,256,256]{5,4,3,2,1,0:T(8,128)(2,1)}, u32[]{:S(2)}) copy-start(bf16[1,1,4,2,256,256]{5,4,3,2,1,0:T(8,128)(2,1)} %param.5) | copy-start | bytes 3145732
  0.8 38.6 %collective-permute-start.2 = (bf16[8,256,256]{2,1,0:T(8,128)(2,1)}, bf16[8,256,256]{2,1,0:T(8,128)(2,1)S(1)}, u32[]{:S(2)}, u32[]{:S(2)}) collective-permute-start(bf16[8,256,256]{2,1,0:T(8,128)(2,1)} %bitcast.9), channel_id=1, source_target_pairs={{0,1},{1,0},{2,3},{3,2},{4,5},{5,4},{6,7},{7,6},{8,9},{9,8},{10,11... | collective-permute-start | bytes 3145736 | tf_op jit(solution)/shard_map/ppermute | solution.py:194
  13.2 0.8 copy-start.1
  14.9 20.5 %all-to-all-start = ((bf16[32,32,128]{2,1,0:T(8,128)(2,1)}), bf16[32,32,128]{2,1,0:T(8,128)(2,1)S(1)}, u32[]{:S(2)}, u32[]{:S(2)}) async-start(bf16[32,32,128]{2,1,0:T(8,128)(2,1)} %bitcast.3), calls=%async_computation | async-start | bytes 524288 | tf_op jit(solution)/shard_map/all_to_all | solution.py:33
  20.7 26.0 %collective-permute-start.1 = (s32[2,2,4,2]{3,2,1,0:T(4,128)S(1)}, s32[2,2,4,2]{3,2,1,0:T(4,128)S(1)}, u32[]{:S(2)}, u32[]{:S(2)}) collective-permute-start(s32[2,2,4,2]{3,2,1,0:T(4,128)S(1)} %copy.17.lists), channel_id=1, source_target_pairs={{0,704},{1,641},{2,706},{3,643},{4,708},{5,645},{6,710},{7,647},{8... | collective-permute-start | bytes 392 | tf_op jit(solution)/shard_map/ppermute | solution.py:29
  33.0 17.3 %collective-permute-start = (s32[2,2,4,2]{3,2,1,0:T(4,128)S(1)}, s32[2,2,4,2]{3,2,1,0:T(4,128)S(1)}, u32[]{:S(2)}, u32[]{:S(2)}) collective-permute-start(s32[2,2,4,2]{3,2,1,0:T(4,128)S(1)} %copy.17.lists), channel_id=1, source_target_pairs={{0,576},{1,577},{2,578},{3,579},{4,580},{5,581},{6,582},{7,583},{8... | collective-permute-start | bytes 392 | tf_op jit(solution)/shard_map/ppermute | solution.py:29
  40.3 13.7 %collective-permute-start.3 = (bf16[2,128,256]{2,1,0:T(8,128)(2,1)S(1)}, bf16[2,128,256]{2,1,0:T(8,128)(2,1)S(1)}, u32[]{:S(2)}, u32[]{:S(2)}) collective-permute-start(bf16[2,128,256]{2,1,0:T(8,128)(2,1)S(1)} %shard_map.48), channel_id=1, source_target_pairs={{0,704},{1,641},{2,706},{3,643},{4,708},{5,645},{6,710},{7,647},{8... | collective-permute-start | bytes 393224 | tf_op jit(solution)/shard_map/ppermute | solution.py:29
  47.5 15.5 %collective-permute-start.4 = (bf16[2,128,256]{2,1,0:T(8,128)(2,1)S(1)}, bf16[2,128,256]{2,1,0:T(8,128)(2,1)S(1)}, u32[]{:S(2)}, u32[]{:S(2)}) collective-permute-start(bf16[2,128,256]{2,1,0:T(8,128)(2,1)S(1)} %shard_map.50), channel_id=1, source_target_pairs={{0,64},{1,129},{2,66},{3,131},{4,68},{5,133},{6,70},{7,135},{8,72}... | collective-permute-start | bytes 393224 | tf_op jit(solution)/shard_map/ppermute | solution.py:29
  51.4 11.7 %collective-permute-start.5 = (bf16[2,128,256]{2,1,0:T(8,128)(2,1)S(1)}, bf16[2,128,256]{2,1,0:T(8,128)(2,1)S(1)}, u32[]{:S(2)}, u32[]{:S(2)}) collective-permute-start(bf16[2,128,256]{2,1,0:T(8,128)(2,1)S(1)} %shard_map.47), channel_id=1, source_target_pairs={{0,192},{1,577},{2,194},{3,579},{4,196},{5,581},{6,198},{7,583},{8... | collective-permute-start | bytes 393224 | tf_op jit(solution)/shard_map/ppermute | solution.py:29
